TPU v7x, 1024 devices: a whole 4x4x32 slice. The times are simulated.
1024 devices in a mesh: dp: 64 (over z, core), mp: 16 (over x, y).
Axes of the slice: x: 4, y: 4, z: 32, core: 2. Of those that a mesh axis runs over, the one named last changes fastest.
Arguments:
- cotangent: bfloat16 [16384, 6144], P('dp', 'mp'), may hold values from -384 to 384
- out_weight: bfloat16 [6144, 6144], P('mp', 'dp'), may hold values from -0.078125 to 0.078125
- queries: bfloat16 [16384, 6144], P('dp', 'mp'), may hold values from -2 to 2
- keys: bfloat16 [16384, 6144], P('dp', 'mp'), may hold values from -2 to 2
- values: bfloat16 [16384, 6144], P('dp', 'mp'), may hold values from -6 to 6
- image_loss: float32 [64], P('dp'), may hold values from 0.3 to 4.5
- group_ids: int32 [64], P('dp'), may hold values from 0 to 31
- group_weights: float32 [32], replicated, may hold values from 0.2 to 1
Outputs:
- query_grad: bfloat16 [16384, 6144], P('dp', 'mp')
- key_grad: bfloat16 [16384, 6144], P('dp', 'mp')
- value_grad: bfloat16 [16384, 6144], P('dp', 'mp')
- new_weights: float32 [32], replicated
All inputs are finite; a program needn't handle non-finite values.
Results may differ from a plain program's by a relative error of at most 0.0058.
Values may be sent and summed in bfloat16 or wider, within the bound.
No kernel may reach another device: no remote copies, remote signals or barrier semaphores. Data moves between devices by JAX's collectives and lax.ppermute only.
A program may use at most 32 MiB of HBM per device.

v0:
```python
import jax
import jax.numpy as jnp
from jax import lax
from jax.sharding import PartitionSpec as P

HD = 128
PATCHES = 256


robust_rate = 0.5


def per_device(cotangent, out_weight, queries, keys, values, image_loss, group_ids, group_weights):
    group_count = group_weights.shape[0]
    labels = jnp.arange(group_count, dtype=jnp.int32)
    member = (group_ids[:, None] == labels[None, :]).astype(jnp.float32)
    counts, totals = lax.psum(
        (jnp.sum(member, axis=0), jnp.sum(member * image_loss[:, None], axis=0)), "dp"
    )
    floored = jnp.maximum(counts, 1.0)
    raised = group_weights * jnp.exp(robust_rate * (totals / floored))
    new_weights = raised / jnp.sum(raised)
    image_scale = jnp.sum(member * (new_weights / floored)[None, :], axis=1)
    full_rows = lax.all_gather(cotangent, "mp", axis=1, tiled=True)
    product = lax.dot_general(
        full_rows,
        lax.all_gather(out_weight, "dp", axis=1, tiled=True),
        (((1,), (1,)), ((), ())),
        preferred_element_type=jnp.float32,
    )
    row_count = cotangent.shape[0]
    row_scale = jnp.repeat(image_scale, PATCHES, total_repeat_length=row_count)
    head_grad = (product * row_scale[:, None]).astype(jnp.bfloat16)
    images_here = row_count // PATCHES
    heads_here = queries.shape[1] // HD
    shape4 = (images_here, PATCHES, heads_here, HD)
    query_block = queries.reshape(shape4)
    key_block = keys.reshape(shape4)
    value_block = values.reshape(shape4)
    grad_block = head_grad.reshape(shape4)
    factor = 1.0 / jnp.sqrt(jnp.float32(HD))
    scores = (
        jnp.einsum("iphd,iqhd->ihpq", query_block, key_block, preferred_element_type=jnp.float32)
        * factor
    )
    raised_scores = jnp.exp(scores)
    probs = raised_scores / jnp.sum(raised_scores, axis=-1, keepdims=True)
    probs_low = probs.astype(jnp.bfloat16)
    value_grad = jnp.einsum(
        "ihpq,iphd->iqhd", probs_low, grad_block, preferred_element_type=jnp.float32
    ).astype(jnp.bfloat16)
    prob_grad = jnp.einsum(
        "iphd,iqhd->ihpq", grad_block, value_block, preferred_element_type=jnp.float32
    )
    centre = jnp.sum(probs * prob_grad, axis=-1, keepdims=True)
    score_low = (probs * (prob_grad - centre)).astype(jnp.bfloat16)
    query_grad = (
        jnp.einsum("ihpq,iqhd->iphd", score_low, key_block, preferred_element_type=jnp.float32)
        * factor
    ).astype(jnp.bfloat16)
    key_grad = (
        jnp.einsum("ihpq,iphd->iqhd", score_low, query_block, preferred_element_type=jnp.float32)
        * factor
    ).astype(jnp.bfloat16)
    return (
        query_grad.reshape(queries.shape),
        key_grad.reshape(keys.shape),
        value_grad.reshape(values.shape),
        new_weights,
    )


def solution(mesh):
    placed = (
        P("dp", "mp"),
        P("mp", "dp"),
        P("dp", "mp"),
        P("dp", "mp"),
        P("dp", "mp"),
        P("dp"),
        P("dp"),
        P(),
    )
    return jax.shard_map(
        per_device,
        mesh=mesh,
        in_specs=placed,
        out_specs=(P("dp", "mp"), P("dp", "mp"), P("dp", "mp"), P()),
        check_vma=False,
    )
```

profile of v0, /device:TPU:1, one launch (start us, length us, event | category | flops | bytes accessed | tf_op | source)
XLA Modules:
  0.0 269.1 jit_solution(11255952015332692244)
XLA Ops:
  7.2 0.0 all-gather.3.cloned.1.call-start
  7.2 0.7 all-gather.3.cloned.1.call-update
  7.9 0.0 all-gather.5.cloned.1.call-start
  7.9 0.7 all-gather.5.cloned.1.call-update
  9.9 1.1 copy.25
  11.0 1.1 copy.26
  12.1 1.1 copy.30
  13.2 106.3 %all-reduce = (f32[32]{0:T(128)S(1)}, f32[32]{0:T(128)S(1)}) all-reduce(f32[32]{0:T(128)S(1)} %fusion.8, f32[32]{0:T(128)S(1)} %fusion.7), channel_id=1, replica_groups=mesh['dp'=64,'mp'=16] {'dp'}, use_global_device_ids=true, to_apply=%region_1.0 | all-reduce | flops 64 | bytes 512 | tf_op jit(solution)/shard_map/psum | solution.py:17
  119.5 1.3 fusion.11
  120.7 1.8 broadcast_divide_fusion
  122.5 0.3 fusion
  122.8 0.0 all-gather.3.cloned.1.call-done
  122.8 129.4 %all-gather.5.cloned.1.call-done = bf16[384,6144]{0,1:T(8,128)(2,1)} async-done(((bf16[384,96]{0,1:T(8,128)(2,1)}), bf16[384,6144]{0,1:T(8,128)(2,1)}) %all-gather.5.cloned.1.call-update) | async-done | bytes 4718608 | tf_op jit(solution)/shard_map/all_gather | solution.py:27
  252.2 5.7 %fusion.1 = bf16[256,384]{1,0:T(8,128)(2,1)S(1)} fusion(bf16[256,6144]{1,0:T(8,128)(2,1)} %all-gather.3.cloned.1.call-done, bf16[384,6144]{0,1:T(8,128)(2,1)} %all-gather.5.cloned.1.call-done, f32[]{:T(128)} %get-tuple-element.41), kind=kOutput, calls=%fused_computation.5 | convolution fusion | flops 1208156160 | bytes 8060932 | tf_op jit(solution)/shard_map/dot_general | solution.py:25
  257.9 0.1 copy.29
  258.1 0.3 fusion.12
  258.4 0.5 multiply_reduce_fusion
  258.9 0.1 multiply_convert_fusion
  259.0 0.3 fusion.2
  259.3 0.2 fusion.3
  259.5 0.3 convolution_convert_fusion
  259.8 0.8 copy.38
  260.7 0.8 copy.36
  261.5 0.8 copy.37
  (2 shorter events, 0.0 us)
Async XLA Ops:
  7.2 115.7 %all-gather.3.cloned.1.call-start = ((), (), s32[]{:S(2)}) async-start(), calls=%async_computation | async-start | bytes 3342336 | tf_op jit(solution)/shard_map/all_gather | solution.py:24
  7.9 244.3 %all-gather.5.cloned.1.call-start = ((), (), s32[]{:S(2)}) async-start(), calls=%async_computation.1 | async-start | bytes 4792320 | tf_op jit(solution)/shard_map/all_gather | solution.py:27
Sparse Core Ops, SparseCore 0:
  12.1 95.8 all-gather.2
  110.8 141.3 all-gather.4
where the time goes:
time: 269 us
  waiting for transfers between devices  131 us (49%)
  blocking collectives  106 us (39%)
  between operations  15.4 us (6%)
  matrix products  7.66 us (3%)
  local copies, waits for them, and re-layouts  5.78 us (2%)
  other arithmetic  3.16 us (1%)
    all_gather x1, waiting for transfers between devices, per_device(): lax.all_gather(out_weight, 'dp', axis=1, tiled=True)  129 us
    psum x1, blocking collectives, per_device(): lax.psum((jnp.sum(member, axis=0), jnp.sum(member * image_loss[:, None],...  106 us
    dot_general x1, matrix products, per_device(): lax.dot_general(full_rows, lax.all_gather(out_weight, 'dp', axis=1, tiled...  5.74 us
    unnamed x6, local copies, waits for them, and re-layouts  5.63 us
  transfers between devices with their start and end apart: 2, of which 1 were waited for; matrix products, arithmetic and copies ran while one was open for 2% of the time, Pallas kernels for 0%

commit v1 on v0

v1 whole, which is shorter than its diff:
```python
import functools

import jax
import jax.numpy as jnp
from jax import lax
from jax.experimental import pallas as pl
from jax.experimental.pallas import tpu as pltpu
from jax.sharding import PartitionSpec as P

HD = 128
PATCHES = 256
ROBUST_RATE = 0.5
SIDE = 4
FAR = 8
UNIT = 96
STATS = 4
ALL = ("dp", "mp")


def along_z(x, step0, step1, pairs_z):
    pairs = [
        (2 * z + c, 2 * ((z + step) % pairs_z) + c)
        for z in range(pairs_z)
        for c, step in ((0, step0), (1, step1))
    ]
    return lax.ppermute(x, "dp", pairs)


def to_sibling(x, pairs_z):
    return lax.ppermute(x, "dp", [(i, i ^ 1) for i in range(2 * pairs_z)])


def in_plane(x, step, first_axis, pairs_z):
    pairs = []
    for d in range(2 * pairs_z):
        on_x = (d % 2 == 0) == first_axis
        for m in range(SIDE * SIDE):
            i, j = divmod(m, SIDE)
            if on_x:
                i = (i + step) % SIDE
            else:
                j = (j + step) % SIDE
            pairs.append((d * SIDE * SIDE + m, d * SIDE * SIDE + i * SIDE + j))
    return lax.ppermute(x, ALL, pairs)


def ring_of_four(block, first_axis, pairs_z):
    half = block.shape[0] // 2
    ahead = in_plane(block, 1, first_axis, pairs_z)
    back = in_plane(block, -1, first_axis, pairs_z)
    ahead2 = in_plane(ahead[:half], 1, first_axis, pairs_z)
    back2 = in_plane(back[half:], -1, first_axis, pairs_z)
    return jnp.concatenate([block, ahead, ahead2, back2, back])


def gather_weight(unit, first, pairs_z):
    other = to_sibling(unit, pairs_z)
    chip = jnp.concatenate([jnp.where(first, unit, other), jnp.where(first, other, unit)])
    got = along_z(chip, FAR, -FAR, pairs_z)
    rows = unit.shape[0]
    got0, got1 = got[:rows], got[rows:]
    mine = jnp.where(first, got0, got1)
    opposite = to_sibling(jnp.where(first, got1, got0), pairs_z)
    farthest = along_z(mine, FAR, -FAR, pairs_z)
    held = (unit, opposite, farthest, mine)
    bundle = jnp.concatenate([h[:UNIT] for h in held] + [h[UNIT:] for h in held])
    pieces = [bundle]
    p = q = bundle
    for _ in range(FAR // 2 - 1):
        p = along_z(p, 1, -1, pairs_z)
        q = along_z(q, -1, 1, pairs_z)
        pieces += [p, q]
    p = along_z(jnp.concatenate([p[: 2 * UNIT], p[4 * UNIT :]]), 1, -1, pairs_z)
    q = along_z(jnp.concatenate([q[UNIT : 3 * UNIT], q[4 * UNIT :]]), -1, 1, pairs_z)
    return pieces + [p, q]


def piece_offsets():
    slots = [0, FAR, 2 * FAR, -FAR]
    offsets = [slots]
    for k in range(1, FAR // 2):
        offsets += [[o - k for o in slots], [o + k for o in slots]]
    k = FAR // 2
    offsets += [[o - k for o in slots[:2]], [o + k for o in slots[1:3]]]
    return offsets


def matmul_kernel(starts, core, x_ref, *refs):
    pieces, (mine_ref, send_ref, xs_ref, acc_ref) = refs[:9], refs[9:]
    slot = 0
    stats = jnp.zeros((16, mine_ref.shape[1]), jnp.float32)
    row = lax.broadcasted_iota(jnp.int32, stats.shape, 0)
    for i, piece in enumerate(pieces):
        units = 4 if i < 7 else 2
        depth = units * UNIT
        for k in range(units):
            at = pl.multiple_of(starts[slot], 32)
            xs_ref[pl.ds(k * UNIT, UNIT), :] = x_ref[pl.ds(at, UNIT), :]
            slot += 1
        product = lax.dot_general(
            xs_ref[pl.ds(0, depth), :],
            piece[pl.ds(0, depth), :],
            (((0,), (0,)), ((), ())),
            preferred_element_type=jnp.float32,
        )
        if i == 0:
            acc_ref[...] = product
        else:
            acc_ref[...] += product
        extra = piece[pl.ds(depth, 16), :].astype(jnp.float32)
        if i == 7:
            extra = jnp.where(row < 8, extra, 0.0)
        if i == 8:
            extra = jnp.where((row >= 4) & (row < 12), extra, 0.0)
        stats += extra
    count = jnp.sum(jnp.where(row % 4 == 0, stats, 0.0), axis=0, keepdims=True)
    total = jnp.sum(jnp.where(row % 4 == 0, 0.0, stats), axis=0, keepdims=True)
    row8 = row[:8]
    tail = jnp.where(row8 == 0, count, jnp.where(row8 == 1, total, 0.0))
    here = pl.multiple_of(core[0] * PATCHES, PATCHES)
    there = pl.multiple_of((1 - core[0]) * PATCHES, PATCHES)
    mine_ref[pl.ds(0, PATCHES), :] = acc_ref[pl.ds(here, PATCHES), :]
    send_ref[pl.ds(0, PATCHES), :] = acc_ref[pl.ds(there, PATCHES), :]
    mine_ref[pl.ds(PATCHES, 8), :] = tail
    send_ref[pl.ds(PATCHES, 8), :] = tail


def attention_kernel(group, mine_ref, got_ref, gw_ref, q_ref, k_ref, v_ref, dq_ref, dk_ref, dv_ref, nw_ref):
    f32, bf16 = jnp.float32, jnp.bfloat16
    width = gw_ref.shape[1]
    tail = mine_ref[pl.ds(PATCHES, 8), :width] + got_ref[pl.ds(PATCHES, 8), :width]
    counts, totals = tail[0:1], tail[1:2]
    floored = jnp.maximum(counts, 1.0)
    raised = gw_ref[...] * jnp.exp(ROBUST_RATE * (totals / floored))
    new_weights = raised / jnp.sum(raised, axis=1, keepdims=True)
    nw_ref[...] = new_weights
    label = lax.broadcasted_iota(jnp.int32, (1, width), 1)
    scale = jnp.sum(
        jnp.where(label == group[0], new_weights / floored, 0.0), axis=1, keepdims=True
    )
    product = mine_ref[pl.ds(0, PATCHES), :] + got_ref[pl.ds(0, PATCHES), :]
    head_grad = (product * scale).astype(bf16)
    factor = 1.0 / jnp.sqrt(f32(HD))
    rows_by_rows = (((1,), (1,)), ((), ()))
    columns = (((0,), (0,)), ((), ()))
    plain = (((1,), (0,)), ((), ()))
    dot = functools.partial(lax.dot_general, preferred_element_type=f32)
    for h in range(q_ref.shape[1] // HD):
        cols = slice(h * HD, (h + 1) * HD)
        q, k, v, g = q_ref[:, cols], k_ref[:, cols], v_ref[:, cols], head_grad[:, cols]
        raised_scores = jnp.exp(dot(q, k, rows_by_rows) * factor)
        probs = raised_scores / jnp.sum(raised_scores, axis=1, keepdims=True)
        dv_ref[:, cols] = dot(probs.astype(bf16), g, columns).astype(bf16)
        prob_grad = dot(g, v, rows_by_rows)
        centre = jnp.sum(probs * prob_grad, axis=1, keepdims=True)
        score = (probs * (prob_grad - centre)).astype(bf16)
        dq_ref[:, cols] = (dot(score, k, plain) * factor).astype(bf16)
        dk_ref[:, cols] = (dot(score, q, columns) * factor).astype(bf16)


VM = pl.BlockSpec(memory_space=pltpu.VMEM)
SM = pl.BlockSpec(memory_space=pltpu.SMEM)


def per_device(pairs_z, cotangent, out_weight, queries, keys, values, image_loss, group_ids, group_weights):
    f32, bf16 = jnp.float32, jnp.bfloat16
    groups = group_weights.shape[0]
    heads = queries.shape[1]
    core = lax.axis_index("dp") % 2
    first = core == 0
    z = lax.axis_index("dp") // 2
    mp = lax.axis_index("mp")
    at_x, at_y = mp // SIDE, mp % SIDE

    loss = image_loss[0]
    high = lax.reduce_precision(loss, 8, 7)
    middle = lax.reduce_precision(loss - high, 8, 7)
    low = loss - high - middle
    member = (jnp.arange(heads) == group_ids[0]).astype(f32)
    stats = jnp.stack([member, member * high, member * middle, member * low]).astype(bf16)
    unit = jnp.concatenate([out_weight.T, stats])
    pieces = gather_weight(unit, first, pairs_z)

    turned = cotangent.T.reshape(2, 2, UNIT, PATCHES)
    keep = jnp.where(first, turned[:, 0], turned[:, 1])
    give = jnp.where(first, turned[:, 1], turned[:, 0])
    got = to_sibling(give, pairs_z)
    block = jnp.concatenate([jnp.where(first, keep, got), jnp.where(first, got, keep)], axis=2)
    block = block.reshape(2 * UNIT, 2 * PATCHES)
    block = ring_of_four(block, True, pairs_z)
    features = ring_of_four(block, False, pairs_z)

    offsets = jnp.array([o for piece in piece_offsets() for o in piece], jnp.int32)
    source = (z + jnp.where(first, offsets, -offsets)) % pairs_z
    from_x, from_y = (at_x - source // 2 // SIDE) % SIDE, (at_y - source // 2 % SIDE) % SIDE
    inner = jnp.where(first, from_x, from_y)
    outer = jnp.where(first, from_y, from_x)
    starts = ((outer * SIDE + inner) * 2 + source % 2) * UNIT

    rows = PATCHES + 8
    partial = jax.ShapeDtypeStruct((rows, heads), f32)
    mine, send = pl.pallas_call(
        matmul_kernel,
        out_shape=(partial, partial),
        in_specs=[SM, SM] + [VM] * 10,
        out_specs=(VM, VM),
        scratch_shapes=[
            pltpu.VMEM((4 * UNIT, 2 * PATCHES), bf16),
            pltpu.VMEM((2 * PATCHES, heads), f32),
        ],
        compiler_params=pltpu.CompilerParams(vmem_limit_bytes=40 * 2**20),
        cost_estimate=pl.CostEstimate(
            flops=2 * 512 * 3072 * heads, bytes_accessed=7 * 2**20, transcendentals=0
        ),
        name="project",
    )(starts, core.reshape(1), features, *pieces)
    received = to_sibling(send, pairs_z)

    width = 128
    grown = jnp.pad(group_weights, (0, width - groups)).reshape(1, width)
    out = jax.ShapeDtypeStruct(queries.shape, bf16)
    query_grad, key_grad, value_grad, new_weights = pl.pallas_call(
        attention_kernel,
        out_shape=(out, out, out, jax.ShapeDtypeStruct((1, width), f32)),
        in_specs=[SM] + [VM] * 6,
        out_specs=(VM,) * 4,
        compiler_params=pltpu.CompilerParams(vmem_limit_bytes=40 * 2**20),
        cost_estimate=pl.CostEstimate(
            flops=10 * 256 * 256 * heads, bytes_accessed=2 * 2**20, transcendentals=3 * 65536
        ),
        name="attention",
    )(group_ids, mine, received, grown, queries, keys, values)
    return query_grad, key_grad, value_grad, new_weights[0, :groups]


def solution(mesh):
    placed = (
        P("dp", "mp"),
        P("mp", "dp"),
        P("dp", "mp"),
        P("dp", "mp"),
        P("dp", "mp"),
        P("dp"),
        P("dp"),
        P(),
    )
    return jax.shard_map(
        functools.partial(per_device, mesh.shape["dp"] // 2),
        mesh=mesh,
        in_specs=placed,
        out_specs=(P("dp", "mp"), P("dp", "mp"), P("dp", "mp"), P()),
        check_vma=False,
    )
```

time: 269 us -> 146 us (0.54)
  waiting for transfers between devices: 131 us -> 14.2 us
  blocking collectives: 106 us -> 0 us
  starting transfers between devices: 0.08 us -> 102 us
  between operations: 15.4 us -> 4.82 us
  local copies, waits for them, and re-layouts: 5.78 us -> 15.2 us
  matrix products: 7.66 us -> 0 us
  Pallas kernels: 0 us -> 6.01 us
    all_gather x2 -> x0, waiting for transfers between devices: 129 us -> none  [the longest x1 129 us: per_device(): lax.all_gather(out_weight, 'dp', axis=1, tiled=True)]
    psum x1 -> x0, blocking collectives: 106 us -> none  [per_device(): lax.psum((jnp.sum(member, axis=0), jnp.sum(member * image_loss[:, None],...]
    ppermute x0 -> x22, starting transfers between devices: none -> 102 us  [the longest x10 50.3 us: along_z(): return lax.ppermute(x, 'dp', pairs)]
    ppermute x0 -> x22, waiting for transfers between devices: none -> 14.2 us  [the longest x10 11 us: along_z(): return lax.ppermute(x, 'dp', pairs)]
    dot_general x6 -> x0, matrix products: 7.2 us -> none  [the longest x1 5.74 us: per_device(): lax.dot_general(full_rows, lax.all_gather(out_weight, 'dp', axis=1, tiled...]
    pallas_call x0 -> x2, Pallas kernels: none -> 6.01 us  [the longest x1 3.45 us: per_device(): pl.pallas_call(matmul_kernel, out_shape=(partial, partial), in_specs=[SM,...]
    concatenate x0 -> x4, local copies, waits for them, and re-layouts: none -> 5.6 us  [the longest x1 2.78 us: gather_weight(): jnp.concatenate([h[:UNIT] for h in held] + [h[UNIT:] for h in held])]
    slice x0 -> x14, local copies, waits for them, and re-layouts: none -> 4.04 us  [the longest x3 1.92 us: gather_weight(): h[:UNIT]]
  transfers between devices with their start and end apart: 2 -> 22, of which waited for: 1 -> 7; matrix products, arithmetic and copies ran while one was open for 2% -> 10% of each run, Pallas kernels for 0% -> 0%
where the time goes in v1:
time: 146 us; the launch traced here: 144 us
  starting transfers between devices  102 us (70%)
  local copies, waits for them, and re-layouts  15.2 us (10%)
  waiting for transfers between devices  14.2 us (10%)
  Pallas kernels  6.01 us (4%)
  between operations  4.82 us (3%)
  other arithmetic  2.18 us (1%)
    ppermute x10, starting transfers between devices, along_z(): return lax.ppermute(x, 'dp', pairs)  50.3 us
    ppermute x8, starting transfers between devices, in_plane(): return lax.ppermute(x, ALL, pairs)  29.4 us
    ppermute x4, starting transfers between devices, to_sibling(): return lax.ppermute(x, 'dp', [(i, i ^ 1) for i in range(2 * pairs_z)])  21.8 us
    ppermute x10, waiting for transfers between devices, along_z(): return lax.ppermute(x, 'dp', pairs)  11 us
    unnamed x18, local copies, waits for them, and re-layouts  5.03 us
    pallas_call x1, Pallas kernels, per_device(): pl.pallas_call(matmul_kernel, out_shape=(partial, partial), in_specs=[SM,...  3.45 us
  transfers between devices with their start and end apart: 22, of which 7 were waited for; matrix products, arithmetic and copies ran while one was open for 10% of the time, Pallas kernels for 0%

profile of v1, /device:TPU:1, one launch (start us, length us, event | category | flops | bytes accessed | tf_op | source)
XLA Modules:
  0.0 143.9 jit_solution(16943735784953338065)
XLA Ops:
  6.5 16.1 %collective-permute-start.9 = (bf16[100,384]{1,0:T(8,128)(2,1)S(1)}, bf16[100,384]{1,0:T(8,128)(2,1)S(1)}, u32[]{:S(2)}, u32[]{:S(2)}) collective-permute-start(bf16[100,384]{1,0:T(8,128)(2,1)S(1)} %concatenate.30), channel_id=1, source_target_pairs={{0,16},{16,0},{32,48},{48,32},{64,80},{80,64},{96,112},{112,96},{1... | collective-permute-start | bytes 230408 | tf_op jit(solution)/shard_map/ppermute | solution.py:30
  23.7 1.9 %collective-permute-start = (bf16[2,96,256]{2,1,0:T(8,128)(2,1)S(1)}, bf16[2,96,256]{2,1,0:T(8,128)(2,1)S(1)}, u32[]{:S(2)}, u32[]{:S(2)}) collective-permute-start(bf16[2,96,256]{2,1,0:T(8,128)(2,1)S(1)} %fusion), channel_id=1, source_target_pairs={{0,16},{16,0},{32,48},{48,32},{64,80},{80,64},{96,112},{112,96},{1... | collective-permute-start | bytes 294920 | tf_op jit(solution)/shard_map/ppermute | solution.py:30
  27.0 1.9 %collective-permute-start.1 = (bf16[192,512]{1,0:T(8,128)(2,1)S(1)}, bf16[192,512]{1,0:T(8,128)(2,1)S(1)}, u32[]{:S(2)}, u32[]{:S(2)}) collective-permute-start(bf16[192,512]{1,0:T(8,128)(2,1)S(1)} %bitcast.47), channel_id=1, source_target_pairs={{0,4},{1,5},{2,6},{3,7},{4,8},{5,9},{6,10},{7,11},{8,12},{9,13},{1... | collective-permute-start | bytes 589832 | tf_op jit(solution)/shard_map/ppermute | solution.py:44
  28.9 4.6 %collective-permute-start.3 = (bf16[192,512]{1,0:T(8,128)(2,1)S(1)}, bf16[192,512]{1,0:T(8,128)(2,1)S(1)}, u32[]{:S(2)}, u32[]{:S(2)}) collective-permute-start(bf16[192,512]{1,0:T(8,128)(2,1)S(1)} %bitcast.48), channel_id=1, source_target_pairs={{0,12},{1,13},{2,14},{3,15},{4,0},{5,1},{6,2},{7,3},{8,4},{9,5},{1... | collective-permute-start | bytes 589832 | tf_op jit(solution)/shard_map/ppermute | solution.py:44
  33.5 10.1 %collective-permute-start.10 = (bf16[200,384]{1,0:T(8,128)(2,1)S(1)}, bf16[200,384]{1,0:T(8,128)(2,1)S(1)}, u32[]{:S(2)}, u32[]{:S(2)}) collective-permute-start(bf16[200,384]{1,0:T(8,128)(2,1)S(1)} %pad_maximum_fusion.3), channel_id=1, source_target_pairs={{0,256},{16,784},{32,288},{48,816},{64,320},{80,848},{96,352},{112... | collective-permute-start | bytes 460808 | tf_op jit(solution)/shard_map/ppermute | solution.py:26
  44.4 1.9 %collective-permute-start.2 = (bf16[96,512]{1,0:T(8,128)(2,1)S(1)}, bf16[96,512]{1,0:T(8,128)(2,1)S(1)}, u32[]{:S(2)}, u32[]{:S(2)}) collective-permute-start(bf16[96,512]{1,0:T(8,128)(2,1)S(1)} %slice.80), channel_id=1, source_target_pairs={{0,4},{1,5},{2,6},{3,7},{4,8},{5,9},{6,10},{7,11},{8,12},{9,13},{1... | collective-permute-start | bytes 294920 | tf_op jit(solution)/shard_map/ppermute | solution.py:44
  46.3 4.6 %collective-permute-start.4 = (bf16[96,512]{1,0:T(8,128)(2,1)S(1)}, bf16[96,512]{1,0:T(8,128)(2,1)S(1)}, u32[]{:S(2)}, u32[]{:S(2)}) collective-permute-start(bf16[96,512]{1,0:T(8,128)(2,1)S(1)} %slice.81), channel_id=1, source_target_pairs={{0,12},{1,13},{2,14},{3,15},{4,0},{5,1},{6,2},{7,3},{8,4},{9,5},{1... | collective-permute-start | bytes 294920 | tf_op jit(solution)/shard_map/ppermute | solution.py:44
  53.9 3.1 %collective-permute-start.5 = (bf16[768,512]{1,0:T(8,128)(2,1)}, bf16[768,512]{1,0:T(8,128)(2,1)}, u32[]{:S(2)}, u32[]{:S(2)}) collective-permute-start(bf16[768,512]{1,0:T(8,128)(2,1)} %get-tuple-element.18), channel_id=1, source_target_pairs={{0,1},{1,2},{2,3},{3,0},{4,5},{5,6},{6,7},{7,4},{8,9},{9,10},{10,1... | collective-permute-start | bytes 2359304 | tf_op jit(solution)/shard_map/ppermute | solution.py:44
  59.0 8.2 %collective-permute-start.12 = (bf16[100,384]{1,0:T(8,128)(2,1)S(1)}, bf16[100,384]{1,0:T(8,128)(2,1)S(1)}, u32[]{:S(2)}, u32[]{:S(2)}) collective-permute-start(bf16[100,384]{1,0:T(8,128)(2,1)S(1)} %get-tuple-element.26), channel_id=1, source_target_pairs={{0,256},{16,784},{32,288},{48,816},{64,320},{80,848},{96,352},{112... | collective-permute-start | bytes 230408 | tf_op jit(solution)/shard_map/ppermute | solution.py:26
  68.4 4.5 %collective-permute-done.12 = bf16[100,384]{1,0:T(8,128)(2,1)S(1)} collective-permute-done((bf16[100,384]{1,0:T(8,128)(2,1)S(1)}, bf16[100,384]{1,0:T(8,128)(2,1)S(1)}, u32[]{:S(2)}, u32[]{:S(2)}) %collective-permute-start.12) | collective-permute-done | bytes 76832 | tf_op jit(solution)/shard_map/ppermute | solution.py:26
  73.6 2.8 %concatenate.32.refs_0_ = bf16[400,384]{1,0:T(8,128)(2,1)S(1)} concatenate(bf16[96,384]{1,0:T(8,128)(2,1)S(1)} %bitcast.51, bf16[96,384]{1,0:T(8,128)(2,1)} %slice.86, bf16[96,384]{1,0:T(8,128)(2,1)} %slice.87, bf16[96,384]{1,0:T(8,128)(2,1)} %slice.88, bf16[1,384]{1,0:T(2,128)(2,1)S(1)} %convert_convert_fusion, bf16[1,384]{1,0:T(2,128)(2,1)S(1)} %select_convert_fusion.2, ...), dimensions={0} | concatenate | bytes 614400 | tf_op jit(solution)/shard_map/concatenate | solution.py:66
  76.4 10.2 %collective-permute-start.13 = (bf16[400,384]{1,0:T(8,128)(2,1)S(1)}, bf16[400,384]{1,0:T(8,128)(2,1)}, u32[]{:S(2)}, u32[]{:S(2)}) collective-permute-start(bf16[400,384]{1,0:T(8,128)(2,1)S(1)} %concatenate.32.refs_0_), channel_id=1, source_target_pairs={{0,32},{16,1008},{32,64},{48,16},{64,96},{80,48},{96,128},{112,80}... | collective-permute-start | bytes 921608 | tf_op jit(solution)/shard_map/ppermute | solution.py:26
  86.6 1.9 %collective-permute-start.14 = (bf16[400,384]{1,0:T(8,128)(2,1)S(1)}, bf16[400,384]{1,0:T(8,128)(2,1)}, u32[]{:S(2)}, u32[]{:S(2)}) collective-permute-start(bf16[400,384]{1,0:T(8,128)(2,1)S(1)} %concatenate.32.refs_0_), channel_id=1, source_target_pairs={{0,992},{16,48},{32,0},{48,80},{64,32},{80,112},{96,64},{112,144},... | collective-permute-start | bytes 921608 | tf_op jit(solution)/shard_map/ppermute | solution.py:26
  88.5 4.2 %collective-permute-start.7 = (bf16[768,512]{1,0:T(8,128)(2,1)}, bf16[768,512]{1,0:T(8,128)(2,1)}, u32[]{:S(2)}, u32[]{:S(2)}) collective-permute-start(bf16[768,512]{1,0:T(8,128)(2,1)} %get-tuple-element.18), channel_id=1, source_target_pairs={{0,3},{1,0},{2,1},{3,2},{4,7},{5,4},{6,5},{7,6},{8,11},{9,8},{10,9... | collective-permute-start | bytes 2359304 | tf_op jit(solution)/shard_map/ppermute | solution.py:44
  92.8 4.6 %collective-permute-start.15 = (bf16[400,384]{1,0:T(8,128)(2,1)}, bf16[400,384]{1,0:T(8,128)(2,1)}, u32[]{:S(2)}, u32[]{:S(2)}) collective-permute-start(bf16[400,384]{1,0:T(8,128)(2,1)} %collective-permute-done.13.refs_1_), channel_id=1, source_target_pairs={{0,32},{16,1008},{32,64},{48,16},{64,96},{80,48},{96,128},{112,80}... | collective-permute-start | bytes 921608 | tf_op jit(solution)/shard_map/ppermute | solution.py:26
  97.3 1.9 %collective-permute-start.16 = (bf16[400,384]{1,0:T(8,128)(2,1)}, bf16[400,384]{1,0:T(8,128)(2,1)}, u32[]{:S(2)}, u32[]{:S(2)}) collective-permute-start(bf16[400,384]{1,0:T(8,128)(2,1)} %collective-permute-done.14.refs_2_), channel_id=1, source_target_pairs={{0,992},{16,48},{32,0},{48,80},{64,32},{80,112},{96,64},{112,144},... | collective-permute-start | bytes 921608 | tf_op jit(solution)/shard_map/ppermute | solution.py:26
  99.3 2.1 %collective-permute-done.15.refs_3_ = bf16[400,384]{1,0:T(8,128)(2,1)} collective-permute-done((bf16[400,384]{1,0:T(8,128)(2,1)}, bf16[400,384]{1,0:T(8,128)(2,1)}, u32[]{:S(2)}, u32[]{:S(2)}) %collective-permute-start.15) | collective-permute-done | bytes 307232 | tf_op jit(solution)/shard_map/ppermute | solution.py:26
  101.4 5.0 %collective-permute-start.17 = (bf16[400,384]{1,0:T(8,128)(2,1)}, bf16[400,384]{1,0:T(8,128)(2,1)S(1)}, u32[]{:S(2)}, u32[]{:S(2)}) collective-permute-start(bf16[400,384]{1,0:T(8,128)(2,1)} %collective-permute-done.15.refs_3_), channel_id=1, source_target_pairs={{0,32},{16,1008},{32,64},{48,16},{64,96},{80,48},{96,128},{112,80}... | collective-permute-start | bytes 921608 | tf_op jit(solution)/shard_map/ppermute | solution.py:26
  109.8 3.7 %collective-permute-start.6 = (bf16[384,512]{1,0:T(8,128)(2,1)S(1)}, bf16[384,512]{1,0:T(8,128)(2,1)S(1)}, u32[]{:S(2)}, u32[]{:S(2)}) collective-permute-start(bf16[384,512]{1,0:T(8,128)(2,1)S(1)} %slice.82), channel_id=1, source_target_pairs={{0,1},{1,2},{2,3},{3,0},{4,5},{5,6},{6,7},{7,4},{8,9},{9,10},{10,1... | collective-permute-start | bytes 1179656 | tf_op jit(solution)/shard_map/ppermute | solution.py:44
  115.3 5.3 %collective-permute-start.8 = (bf16[384,512]{1,0:T(8,128)(2,1)S(1)}, bf16[384,512]{1,0:T(8,128)(2,1)S(1)}, u32[]{:S(2)}, u32[]{:S(2)}) collective-permute-start(bf16[384,512]{1,0:T(8,128)(2,1)S(1)} %slice.83), channel_id=1, source_target_pairs={{0,3},{1,0},{2,1},{3,2},{4,7},{5,4},{6,5},{7,6},{8,11},{9,8},{10,9... | collective-permute-start | bytes 1179656 | tf_op jit(solution)/shard_map/ppermute | solution.py:44
  121.8 4.6 %collective-permute-start.19 = (bf16[208,384]{1,0:T(8,128)(2,1)S(1)}, bf16[208,384]{1,0:T(8,128)(2,1)S(1)}, u32[]{:S(2)}, u32[]{:S(2)}) collective-permute-start(bf16[208,384]{1,0:T(8,128)(2,1)S(1)} %pad_maximum_fusion.1), channel_id=1, source_target_pairs={{0,32},{16,1008},{32,64},{48,16},{64,96},{80,48},{96,128},{112,80}... | collective-permute-start | bytes 479240 | tf_op jit(solution)/shard_map/ppermute | solution.py:26
  129.8 4.0 %collective-permute-done.20.refs_8_ = bf16[208,384]{1,0:T(8,128)(2,1)S(1)} collective-permute-done((bf16[208,384]{1,0:T(8,128)(2,1)S(1)}, bf16[208,384]{1,0:T(8,128)(2,1)S(1)}, u32[]{:S(2)}, u32[]{:S(2)}) %collective-permute-start.20) | collective-permute-done | bytes 159776 | tf_op jit(solution)/shard_map/ppermute | solution.py:26
  133.7 3.5 %project.1 = (f32[264,384]{1,0:T(8,128)S(1)}, f32[264,384]{1,0:T(8,128)S(1)}) custom-call(s32[32]{0:T(128)S(1)} %fusion.10.starts, s32[1]{0:T(128)} %bitcast.core, bf16[3072,512]{1,0:T(8,128)(2,1)S(1)} %constant_dynamic-update-slice_fusion.5.x_ref, bf16[400,384]{1,0:T(8,128)(2,1)S(1)} %concatenate.32.refs_0_, ...), custom_call_target="tpu_custom_call" | custom-call | flops 1207959552 | bytes 7340032 | tf_op jit(solution)/shard_map/project/pallas_call | solution.py:202
  140.8 2.6 %attention.1 = (bf16[256,384]{1,0:T(8,128)(2,1)}, bf16[256,384]{1,0:T(8,128)(2,1)}, bf16[256,384]{1,0:T(8,128)(2,1)}, f32[1,128]{1,0:T(1,128)S(1)}) custom-call(s32[1]{0:T(128)} %copy.34.group, f32[264,384]{1,0:T(8,128)S(1)} %get-tuple-element.10.mine_ref, f32[264,384]{1,0:T(8,128)S(1)} %collective-permute-done.21.got_ref, ...), custom_call_target="tpu_custom_call" | custom-call | flops 251658240 | bytes 2097152 | tf_op jit(solution)/shard_map/attention/pallas_call | solution.py:222
  (72 shorter events, 25.9 us)
Async XLA Ops:
  0.6 73.0 %copy-start.3 = (bf16[384,96]{0,1:T(8,128)(2,1)S(1)}, bf16[384,96]{0,1:T(8,128)(2,1)}, u32[]{:S(2)}) copy-start(bf16[384,96]{0,1:T(8,128)(2,1)} %param.10) | copy-start | bytes 221188
  6.5 19.1 %collective-permute-start.9 = (bf16[100,384]{1,0:T(8,128)(2,1)S(1)}, bf16[100,384]{1,0:T(8,128)(2,1)S(1)}, u32[]{:S(2)}, u32[]{:S(2)}) collective-permute-start(bf16[100,384]{1,0:T(8,128)(2,1)S(1)} %concatenate.30), channel_id=1, source_target_pairs={{0,16},{16,0},{32,48},{48,32},{64,80},{80,64},{96,112},{112,96},{1... | collective-permute-start | bytes 230408 | tf_op jit(solution)/shard_map/ppermute | solution.py:30
  23.7 3.2 %collective-permute-start = (bf16[2,96,256]{2,1,0:T(8,128)(2,1)S(1)}, bf16[2,96,256]{2,1,0:T(8,128)(2,1)S(1)}, u32[]{:S(2)}, u32[]{:S(2)}) collective-permute-start(bf16[2,96,256]{2,1,0:T(8,128)(2,1)S(1)} %fusion), channel_id=1, source_target_pairs={{0,16},{16,0},{32,48},{48,32},{64,80},{80,64},{96,112},{112,96},{1... | collective-permute-start | bytes 294920 | tf_op jit(solution)/shard_map/ppermute | solution.py:30
  27.0 17.4 %collective-permute-start.1 = (bf16[192,512]{1,0:T(8,128)(2,1)S(1)}, bf16[192,512]{1,0:T(8,128)(2,1)S(1)}, u32[]{:S(2)}, u32[]{:S(2)}) collective-permute-start(bf16[192,512]{1,0:T(8,128)(2,1)S(1)} %bitcast.47), channel_id=1, source_target_pairs={{0,4},{1,5},{2,6},{3,7},{4,8},{5,9},{6,10},{7,11},{8,12},{9,13},{1... | collective-permute-start | bytes 589832 | tf_op jit(solution)/shard_map/ppermute | solution.py:44
  28.9 17.4 %collective-permute-start.3 = (bf16[192,512]{1,0:T(8,128)(2,1)S(1)}, bf16[192,512]{1,0:T(8,128)(2,1)S(1)}, u32[]{:S(2)}, u32[]{:S(2)}) collective-permute-start(bf16[192,512]{1,0:T(8,128)(2,1)S(1)} %bitcast.48), channel_id=1, source_target_pairs={{0,12},{1,13},{2,14},{3,15},{4,0},{5,1},{6,2},{7,3},{8,4},{9,5},{1... | collective-permute-start | bytes 589832 | tf_op jit(solution)/shard_map/ppermute | solution.py:44
  33.5 23.5 %collective-permute-start.10 = (bf16[200,384]{1,0:T(8,128)(2,1)S(1)}, bf16[200,384]{1,0:T(8,128)(2,1)S(1)}, u32[]{:S(2)}, u32[]{:S(2)}) collective-permute-start(bf16[200,384]{1,0:T(8,128)(2,1)S(1)} %pad_maximum_fusion.3), channel_id=1, source_target_pairs={{0,256},{16,784},{32,288},{48,816},{64,320},{80,848},{96,352},{112... | collective-permute-start | bytes 460808 | tf_op jit(solution)/shard_map/ppermute | solution.py:26
  44.4 7.2 %collective-permute-start.2 = (bf16[96,512]{1,0:T(8,128)(2,1)S(1)}, bf16[96,512]{1,0:T(8,128)(2,1)S(1)}, u32[]{:S(2)}, u32[]{:S(2)}) collective-permute-start(bf16[96,512]{1,0:T(8,128)(2,1)S(1)} %slice.80), channel_id=1, source_target_pairs={{0,4},{1,5},{2,6},{3,7},{4,8},{5,9},{6,10},{7,11},{8,12},{9,13},{1... | collective-permute-start | bytes 294920 | tf_op jit(solution)/shard_map/ppermute | solution.py:44
  46.3 6.2 %collective-permute-start.4 = (bf16[96,512]{1,0:T(8,128)(2,1)S(1)}, bf16[96,512]{1,0:T(8,128)(2,1)S(1)}, u32[]{:S(2)}, u32[]{:S(2)}) collective-permute-start(bf16[96,512]{1,0:T(8,128)(2,1)S(1)} %slice.81), channel_id=1, source_target_pairs={{0,12},{1,13},{2,14},{3,15},{4,0},{5,1},{6,2},{7,3},{8,4},{9,5},{1... | collective-permute-start | bytes 294920 | tf_op jit(solution)/shard_map/ppermute | solution.py:44
  53.9 54.9 %collective-permute-start.5 = (bf16[768,512]{1,0:T(8,128)(2,1)}, bf16[768,512]{1,0:T(8,128)(2,1)}, u32[]{:S(2)}, u32[]{:S(2)}) collective-permute-start(bf16[768,512]{1,0:T(8,128)(2,1)} %get-tuple-element.18), channel_id=1, source_target_pairs={{0,1},{1,2},{2,3},{3,0},{4,5},{5,6},{6,7},{7,4},{8,9},{9,10},{10,1... | collective-permute-start | bytes 2359304 | tf_op jit(solution)/shard_map/ppermute | solution.py:44
  57.0 10.8 %collective-permute-start.11 = (bf16[100,384]{1,0:T(8,128)(2,1)S(1)}, bf16[100,384]{1,0:T(8,128)(2,1)S(1)}, u32[]{:S(2)}, u32[]{:S(2)}) collective-permute-start(bf16[100,384]{1,0:T(8,128)(2,1)S(1)} %get-tuple-element.27), channel_id=1, source_target_pairs={{0,16},{16,0},{32,48},{48,32},{64,80},{80,64},{96,112},{112,96},{1... | collective-permute-start | bytes 230408 | tf_op jit(solution)/shard_map/ppermute | solution.py:30
  59.0 14.0 %collective-permute-start.12 = (bf16[100,384]{1,0:T(8,128)(2,1)S(1)}, bf16[100,384]{1,0:T(8,128)(2,1)S(1)}, u32[]{:S(2)}, u32[]{:S(2)}) collective-permute-start(bf16[100,384]{1,0:T(8,128)(2,1)S(1)} %get-tuple-element.26), channel_id=1, source_target_pairs={{0,256},{16,784},{32,288},{48,816},{64,320},{80,848},{96,352},{112... | collective-permute-start | bytes 230408 | tf_op jit(solution)/shard_map/ppermute | solution.py:26
  76.4 16.4 %collective-permute-start.13 = (bf16[400,384]{1,0:T(8,128)(2,1)S(1)}, bf16[400,384]{1,0:T(8,128)(2,1)}, u32[]{:S(2)}, u32[]{:S(2)}) collective-permute-start(bf16[400,384]{1,0:T(8,128)(2,1)S(1)} %concatenate.32.refs_0_), channel_id=1, source_target_pairs={{0,32},{16,1008},{32,64},{48,16},{64,96},{80,48},{96,128},{112,80}... | collective-permute-start | bytes 921608 | tf_op jit(solution)/shard_map/ppermute | solution.py:26
  86.6 10.7 %collective-permute-start.14 = (bf16[400,384]{1,0:T(8,128)(2,1)S(1)}, bf16[400,384]{1,0:T(8,128)(2,1)}, u32[]{:S(2)}, u32[]{:S(2)}) collective-permute-start(bf16[400,384]{1,0:T(8,128)(2,1)S(1)} %concatenate.32.refs_0_), channel_id=1, source_target_pairs={{0,992},{16,48},{32,0},{48,80},{64,32},{80,112},{96,64},{112,144},... | collective-permute-start | bytes 921608 | tf_op jit(solution)/shard_map/ppermute | solution.py:26
  88.5 25.7 %collective-permute-start.7 = (bf16[768,512]{1,0:T(8,128)(2,1)}, bf16[768,512]{1,0:T(8,128)(2,1)}, u32[]{:S(2)}, u32[]{:S(2)}) collective-permute-start(bf16[768,512]{1,0:T(8,128)(2,1)} %get-tuple-element.18), channel_id=1, source_target_pairs={{0,3},{1,0},{2,1},{3,2},{4,7},{5,4},{6,5},{7,6},{8,11},{9,8},{10,9... | collective-permute-start | bytes 2359304 | tf_op jit(solution)/shard_map/ppermute | solution.py:44
  92.8 8.7 %collective-permute-start.15 = (bf16[400,384]{1,0:T(8,128)(2,1)}, bf16[400,384]{1,0:T(8,128)(2,1)}, u32[]{:S(2)}, u32[]{:S(2)}) collective-permute-start(bf16[400,384]{1,0:T(8,128)(2,1)} %collective-permute-done.13.refs_1_), channel_id=1, source_target_pairs={{0,32},{16,1008},{32,64},{48,16},{64,96},{80,48},{96,128},{112,80}... | collective-permute-start | bytes 921608 | tf_op jit(solution)/shard_map/ppermute | solution.py:26
  97.3 9.5 %collective-permute-start.16 = (bf16[400,384]{1,0:T(8,128)(2,1)}, bf16[400,384]{1,0:T(8,128)(2,1)}, u32[]{:S(2)}, u32[]{:S(2)}) collective-permute-start(bf16[400,384]{1,0:T(8,128)(2,1)} %collective-permute-done.14.refs_2_), channel_id=1, source_target_pairs={{0,992},{16,48},{32,0},{48,80},{64,32},{80,112},{96,64},{112,144},... | collective-permute-start | bytes 921608 | tf_op jit(solution)/shard_map/ppermute | solution.py:26
  101.4 20.3 %collective-permute-start.17 = (bf16[400,384]{1,0:T(8,128)(2,1)}, bf16[400,384]{1,0:T(8,128)(2,1)S(1)}, u32[]{:S(2)}, u32[]{:S(2)}) collective-permute-start(bf16[400,384]{1,0:T(8,128)(2,1)} %collective-permute-done.15.refs_3_), channel_id=1, source_target_pairs={{0,32},{16,1008},{32,64},{48,16},{64,96},{80,48},{96,128},{112,80}... | collective-permute-start | bytes 921608 | tf_op jit(solution)/shard_map/ppermute | solution.py:26
  106.8 19.6 %collective-permute-start.18 = (bf16[400,384]{1,0:T(8,128)(2,1)}, bf16[400,384]{1,0:T(8,128)(2,1)S(1)}, u32[]{:S(2)}, u32[]{:S(2)}) collective-permute-start(bf16[400,384]{1,0:T(8,128)(2,1)} %collective-permute-done.16.refs_4_), channel_id=1, source_target_pairs={{0,992},{16,48},{32,0},{48,80},{64,32},{80,112},{96,64},{112,144},... | collective-permute-start | bytes 921608 | tf_op jit(solution)/shard_map/ppermute | solution.py:26
  109.8 18.7 %collective-permute-start.6 = (bf16[384,512]{1,0:T(8,128)(2,1)S(1)}, bf16[384,512]{1,0:T(8,128)(2,1)S(1)}, u32[]{:S(2)}, u32[]{:S(2)}) collective-permute-start(bf16[384,512]{1,0:T(8,128)(2,1)S(1)} %slice.82), channel_id=1, source_target_pairs={{0,1},{1,2},{2,3},{3,0},{4,5},{5,6},{6,7},{7,4},{8,9},{9,10},{10,1... | collective-permute-start | bytes 1179656 | tf_op jit(solution)/shard_map/ppermute | solution.py:44
  115.3 13.2 %collective-permute-start.8 = (bf16[384,512]{1,0:T(8,128)(2,1)S(1)}, bf16[384,512]{1,0:T(8,128)(2,1)S(1)}, u32[]{:S(2)}, u32[]{:S(2)}) collective-permute-start(bf16[384,512]{1,0:T(8,128)(2,1)S(1)} %slice.83), channel_id=1, source_target_pairs={{0,3},{1,0},{2,1},{3,2},{4,7},{5,4},{6,5},{7,6},{8,11},{9,8},{10,9... | collective-permute-start | bytes 1179656 | tf_op jit(solution)/shard_map/ppermute | solution.py:44
  121.8 7.9 %collective-permute-start.19 = (bf16[208,384]{1,0:T(8,128)(2,1)S(1)}, bf16[208,384]{1,0:T(8,128)(2,1)S(1)}, u32[]{:S(2)}, u32[]{:S(2)}) collective-permute-start(bf16[208,384]{1,0:T(8,128)(2,1)S(1)} %pad_maximum_fusion.1), channel_id=1, source_target_pairs={{0,32},{16,1008},{32,64},{48,16},{64,96},{80,48},{96,128},{112,80}... | collective-permute-start | bytes 479240 | tf_op jit(solution)/shard_map/ppermute | solution.py:26
  126.5 7.2 %collective-permute-start.20 = (bf16[208,384]{1,0:T(8,128)(2,1)S(1)}, bf16[208,384]{1,0:T(8,128)(2,1)S(1)}, u32[]{:S(2)}, u32[]{:S(2)}) collective-permute-start(bf16[208,384]{1,0:T(8,128)(2,1)S(1)} %pad_maximum_fusion.2), channel_id=1, source_target_pairs={{0,992},{16,48},{32,0},{48,80},{64,32},{80,112},{96,64},{112,144},... | collective-permute-start | bytes 479240 | tf_op jit(solution)/shard_map/ppermute | solution.py:26
  129.7 11.1 %copy-start = (bf16[256,384]{1,0:T(8,128)(2,1)S(1)}, bf16[256,384]{1,0:T(8,128)(2,1)}, u32[]{:S(2)}) copy-start(bf16[256,384]{1,0:T(8,128)(2,1)} %q_ref.1) | copy-start | bytes 589828
  137.2 3.6 %collective-permute-start.21 = (f32[264,384]{1,0:T(8,128)S(1)}, f32[264,384]{1,0:T(8,128)S(1)}, u32[]{:S(2)}, u32[]{:S(2)}) collective-permute-start(f32[264,384]{1,0:T(8,128)S(1)} %get-tuple-element.11), channel_id=1, source_target_pairs={{0,16},{16,0},{32,48},{48,32},{64,80},{80,64},{96,112},{112,96},{1... | collective-permute-start | bytes 1216520 | tf_op jit(solution)/shard_map/ppermute | solution.py:30
  (3 other events, 31.6 us)

commit v2 on v1

v2 whole, which is shorter than its diff:
```python
import functools

import jax
import jax.numpy as jnp
from jax import lax
from jax.experimental import pallas as pl
from jax.experimental.pallas import tpu as pltpu
from jax.sharding import PartitionSpec as P

HD = 128
PATCHES = 256
ROBUST_RATE = 0.5
SIDE = 4
FAR = 8
UNIT = 96
STATS = 4
TAIL = 16
ALL = ("dp", "mp")


def along_z(x, step0, step1, pairs_z):
    pairs = [
        (2 * z + c, 2 * ((z + step) % pairs_z) + c)
        for z in range(pairs_z)
        for c, step in ((0, step0), (1, step1))
    ]
    return lax.ppermute(x, "dp", pairs)


def to_sibling(x, pairs_z):
    return lax.ppermute(x, "dp", [(i, i ^ 1) for i in range(2 * pairs_z)])


def in_plane(x, step, first_axis, pairs_z):
    pairs = []
    for d in range(2 * pairs_z):
        on_x = (d % 2 == 0) == first_axis
        for m in range(SIDE * SIDE):
            i, j = divmod(m, SIDE)
            if on_x:
                i = (i + step) % SIDE
            else:
                j = (j + step) % SIDE
            pairs.append((d * SIDE * SIDE + m, d * SIDE * SIDE + i * SIDE + j))
    return lax.ppermute(x, ALL, pairs)


def ring_of_four(block, first_axis, pairs_z):
    return [block] + [in_plane(block, step, first_axis, pairs_z) for step in (1, 2, -1)]


def gather_weight(unit, other, first, pairs_z):
    chip = jnp.concatenate([jnp.where(first, unit, other), jnp.where(first, other, unit)])
    got = along_z(chip, FAR, -FAR, pairs_z)
    rows = unit.shape[0]
    got0, got1 = got[:rows], got[rows:]
    mine = jnp.where(first, got0, got1)
    farthest = along_z(mine, FAR, -FAR, pairs_z)
    opposite = to_sibling(jnp.where(first, got1, got0), pairs_z)
    bundle = join_units(unit, opposite, farthest, mine)
    pieces = [bundle]
    p = q = bundle
    for _ in range(FAR // 2 - 1):
        p = along_z(p, 1, -1, pairs_z)
        q = along_z(q, -1, 1, pairs_z)
        pieces += [p, q]
    p = along_z(jnp.concatenate([p[: 2 * UNIT], p[4 * UNIT :]]), 1, -1, pairs_z)
    q = along_z(jnp.concatenate([q[UNIT : 3 * UNIT], q[4 * UNIT :]]), -1, 1, pairs_z)
    return pieces + [p, q]


def piece_offsets():
    slots = [0, FAR, 2 * FAR, -FAR]
    offsets = [slots]
    for k in range(1, FAR // 2):
        offsets += [[o - k for o in slots], [o + k for o in slots]]
    k = FAR // 2
    offsets += [[o - k for o in slots[:2]], [o + k for o in slots[1:3]]]
    return offsets


def unit_kernel(group, loss, weight_ref, unit_ref):
    heads = weight_ref.shape[1]
    unit_ref[pl.ds(0, UNIT), :] = weight_ref[...]
    x = jnp.full((TAIL, heads), loss[0], jnp.float32)
    high = x.astype(jnp.bfloat16).astype(jnp.float32)
    middle = (x - high).astype(jnp.bfloat16).astype(jnp.float32)
    low = x - high - middle
    row = lax.broadcasted_iota(jnp.int32, x.shape, 0)
    lane = lax.broadcasted_iota(jnp.int32, x.shape, 1)
    value = jnp.where(row == 0, 1.0, jnp.where(row == 1, high, jnp.where(row == 2, middle, low)))
    value = jnp.where((row < STATS) & (lane == group[0]), value, 0.0)
    unit_ref[pl.ds(UNIT, TAIL), :] = value.astype(jnp.bfloat16)


def join_kernel(*refs):
    *units, out = refs
    tail = jnp.zeros((TAIL, out.shape[1]), jnp.float32)
    for i, ref in enumerate(units):
        out[pl.ds(i * UNIT, UNIT), :] = ref[pl.ds(0, UNIT), :]
        rows = ref[pl.ds(UNIT, TAIL), :].astype(jnp.float32)
        tail += pltpu.roll(rows, STATS * i, 0) if i else rows
    out[pl.ds(len(units) * UNIT, TAIL), :] = tail.astype(jnp.bfloat16)


def stack_kernel(*refs):
    *blocks, out = refs
    rows = blocks[0].shape[0]
    for i, ref in enumerate(blocks):
        out[pl.ds(i * rows, rows), :] = ref[...]


def scores_kernel(q_ref, k_ref, probs_ref):
    factor = 1.0 / jnp.sqrt(jnp.float32(HD))
    for h in range(q_ref.shape[1] // HD):
        cols = slice(h * HD, (h + 1) * HD)
        scores = lax.dot_general(
            q_ref[:, cols],
            k_ref[:, cols],
            (((1,), (1,)), ((), ())),
            preferred_element_type=jnp.float32,
        )
        raised = jnp.exp(scores * factor)
        probs_ref[h] = raised / jnp.sum(raised, axis=1, keepdims=True)


def pick_rows(starts, outers, slot, blocks, xs_ref, at):
    row = pl.multiple_of(starts[slot], 32)
    for i, block in enumerate(blocks):

        @pl.when(outers[slot] == i)
        def _():
            xs_ref[pl.ds(at, UNIT), :] = block[pl.ds(row, UNIT), :]


def product_of(xs, weight):
    return lax.dot_general(
        xs, weight, (((0,), (0,)), ((), ())), preferred_element_type=jnp.float32
    )


def first_kernel(starts, outers, *refs):
    blocks, pieces, (acc_ref, stats_ref, xs_ref) = refs[:4], refs[4:-3], refs[-3:]
    depth = 4 * UNIT
    stats_ref[...] = jnp.zeros_like(stats_ref)
    for i, piece in enumerate(pieces):
        for k in range(4):
            pick_rows(starts, outers, 4 * i + k, blocks, xs_ref, k * UNIT)
        product = product_of(xs_ref[...], piece[pl.ds(0, depth), :])
        if i == 0:
            acc_ref[...] = product
        else:
            acc_ref[...] += product
        stats_ref[...] += piece[pl.ds(depth, TAIL), :].astype(jnp.float32)


def last_kernel(starts, outers, core, *refs):
    blocks, (p_ref, q_ref, acc_ref, stats_ref, mine_ref, send_ref, xs_ref, w_ref, sum_ref) = refs[:4], refs[4:]
    depth = 2 * UNIT
    for k in range(4):
        pick_rows(starts, outers, 28 + k, blocks, xs_ref, k * UNIT)
    w_ref[pl.ds(0, depth), :] = p_ref[pl.ds(0, depth), :]
    w_ref[pl.ds(depth, depth), :] = q_ref[pl.ds(0, depth), :]
    sum_ref[...] = acc_ref[...] + product_of(xs_ref[...], w_ref[...])
    stats = stats_ref[...]
    row = lax.broadcasted_iota(jnp.int32, stats.shape, 0)
    stats += jnp.where(row < 8, p_ref[pl.ds(depth, TAIL), :].astype(jnp.float32), 0.0)
    middle = (row >= 4) & (row < 12)
    stats += jnp.where(middle, q_ref[pl.ds(depth, TAIL), :].astype(jnp.float32), 0.0)
    count = jnp.sum(jnp.where(row % 4 == 0, stats, 0.0), axis=0, keepdims=True)
    total = jnp.sum(jnp.where(row % 4 == 0, 0.0, stats), axis=0, keepdims=True)
    row8 = row[:8]
    tail = jnp.where(row8 == 0, count, jnp.where(row8 == 1, total, 0.0))
    here = pl.multiple_of(core[0] * PATCHES, PATCHES)
    there = pl.multiple_of((1 - core[0]) * PATCHES, PATCHES)
    mine_ref[pl.ds(0, PATCHES), :] = sum_ref[pl.ds(here, PATCHES), :]
    send_ref[pl.ds(0, PATCHES), :] = sum_ref[pl.ds(there, PATCHES), :]
    mine_ref[pl.ds(PATCHES, 8), :] = tail
    send_ref[pl.ds(PATCHES, 8), :] = tail


def attention_kernel(group, mine_ref, got_ref, gw_ref, probs_ref, q_ref, k_ref, v_ref, dq_ref, dk_ref, dv_ref, nw_ref):
    f32, bf16 = jnp.float32, jnp.bfloat16
    width = gw_ref.shape[1]
    tail = mine_ref[pl.ds(PATCHES, 8), :] + got_ref[pl.ds(PATCHES, 8), :]
    counts, totals = tail[0:1, :width], tail[1:2, :width]
    floored = jnp.maximum(counts, 1.0)
    raised = gw_ref[...] * jnp.exp(ROBUST_RATE * (totals / floored))
    new_weights = raised / jnp.sum(raised, axis=1, keepdims=True)
    nw_ref[...] = new_weights
    label = lax.broadcasted_iota(jnp.int32, (1, width), 1)
    scale = jnp.sum(
        jnp.where(label == group[0], new_weights / floored, 0.0), axis=1, keepdims=True
    )
    product = mine_ref[pl.ds(0, PATCHES), :] + got_ref[pl.ds(0, PATCHES), :]
    head_grad = (product * scale).astype(bf16)
    factor = 1.0 / jnp.sqrt(f32(HD))
    rows_by_rows = (((1,), (1,)), ((), ()))
    columns = (((0,), (0,)), ((), ()))
    plain = (((1,), (0,)), ((), ()))
    dot = functools.partial(lax.dot_general, preferred_element_type=f32)
    for h in range(q_ref.shape[1] // HD):
        cols = slice(h * HD, (h + 1) * HD)
        q, k, v, g = q_ref[:, cols], k_ref[:, cols], v_ref[:, cols], head_grad[:, cols]
        probs = probs_ref[h]
        dv_ref[:, cols] = dot(probs.astype(bf16), g, columns).astype(bf16)
        prob_grad = dot(g, v, rows_by_rows)
        centre = jnp.sum(probs * prob_grad, axis=1, keepdims=True)
        score = (probs * (prob_grad - centre)).astype(bf16)
        dq_ref[:, cols] = (dot(score, k, plain) * factor).astype(bf16)
        dk_ref[:, cols] = (dot(score, q, columns) * factor).astype(bf16)


VM = pl.BlockSpec(memory_space=pltpu.VMEM)
SM = pl.BlockSpec(memory_space=pltpu.SMEM)


def call(kernel, name, out_shape, operands, scalars=0, scratch=(), flops=0, moved=2**20):
    outs = jax.tree.map(lambda _: VM, out_shape)
    return pl.pallas_call(
        kernel,
        out_shape=out_shape,
        in_specs=[SM] * scalars + [VM] * (len(operands) - scalars),
        out_specs=outs,
        scratch_shapes=scratch,
        compiler_params=pltpu.CompilerParams(vmem_limit_bytes=40 * 2**20),
        cost_estimate=pl.CostEstimate(flops=flops, bytes_accessed=moved, transcendentals=0),
        name=name,
    )(*operands)


def join_units(*units):
    rows = len(units) * UNIT + TAIL
    shape = jax.ShapeDtypeStruct((rows, units[0].shape[1]), units[0].dtype)
    return call(join_kernel, "join_units", shape, units)


def per_device(pairs_z, cotangent, out_weight, queries, keys, values, image_loss, group_ids, group_weights):
    f32, bf16 = jnp.float32, jnp.bfloat16
    groups = group_weights.shape[0]
    heads = queries.shape[1]
    core = lax.axis_index("dp") % 2
    first = core == 0
    z = lax.axis_index("dp") // 2
    mp = lax.axis_index("mp")
    at_x, at_y = mp // SIDE, mp % SIDE

    unit = call(
        unit_kernel,
        "make_unit",
        jax.ShapeDtypeStruct((UNIT + TAIL, heads), bf16),
        (group_ids, image_loss, out_weight.T),
        2,
        moved=2**17,
    )
    other = to_sibling(unit, pairs_z)

    turned = cotangent.T.reshape(2, 2, UNIT, PATCHES)
    keep = jnp.where(first, turned[:, 0], turned[:, 1])
    give = jnp.where(first, turned[:, 1], turned[:, 0])
    got = to_sibling(give, pairs_z)
    block = jnp.concatenate([jnp.where(first, keep, got), jnp.where(first, got, keep)], axis=2)
    block = block.reshape(2 * UNIT, 2 * PATCHES)
    row_of_blocks = call(
        stack_kernel,
        "stack",
        jax.ShapeDtypeStruct((8 * UNIT, 2 * PATCHES), bf16),
        ring_of_four(block, True, pairs_z),
    )
    features = ring_of_four(row_of_blocks, False, pairs_z)
    pieces = gather_weight(unit, other, first, pairs_z)

    offsets = jnp.array([o for piece in piece_offsets() for o in piece], jnp.int32)
    source = (z + jnp.where(first, offsets, -offsets)) % pairs_z
    from_x, from_y = (at_x - source // 2 // SIDE) % SIDE, (at_y - source // 2 % SIDE) % SIDE
    inner = jnp.where(first, from_x, from_y)
    outer = jnp.where(first, from_y, from_x)
    starts = (inner * 2 + source % 2) * UNIT

    total = jax.ShapeDtypeStruct((2 * PATCHES, heads), f32)
    summed, stats = call(
        first_kernel,
        "project_first",
        (total, jax.ShapeDtypeStruct((TAIL, heads), f32)),
        (starts, outer, *features, *pieces[:7]),
        2,
        [pltpu.VMEM((4 * UNIT, 2 * PATCHES), bf16)],
        2 * 512 * 2688 * heads,
        6 * 2**20,
    )
    partial = jax.ShapeDtypeStruct((PATCHES + 8, heads), f32)
    mine, send = call(
        last_kernel,
        "project_last",
        (partial, partial),
        (starts, outer, core.reshape(1), *features, *pieces[7:], summed, stats),
        3,
        [
            pltpu.VMEM((4 * UNIT, 2 * PATCHES), bf16),
            pltpu.VMEM((4 * UNIT, heads), bf16),
            pltpu.VMEM((2 * PATCHES, heads), f32),
        ],
        2 * 512 * 384 * heads,
        2 * 2**20,
    )
    received = to_sibling(send, pairs_z)

    probs = call(
        scores_kernel,
        "scores",
        jax.ShapeDtypeStruct((heads // HD, PATCHES, PATCHES), f32),
        (queries, keys),
        flops=2 * PATCHES * PATCHES * heads,
    )
    out = jax.ShapeDtypeStruct(queries.shape, bf16)
    query_grad, key_grad, value_grad, new_weights = call(
        attention_kernel,
        "attention",
        (out, out, out, jax.ShapeDtypeStruct((1, groups), f32)),
        (group_ids, mine, received, group_weights.reshape(1, groups), probs, queries, keys, values),
        1,
        flops=8 * PATCHES * PATCHES * heads,
        moved=3 * 2**20,
    )
    return query_grad, key_grad, value_grad, new_weights.reshape(groups)


def solution(mesh):
    placed = (
        P("dp", "mp"),
        P("mp", "dp"),
        P("dp", "mp"),
        P("dp", "mp"),
        P("dp", "mp"),
        P("dp"),
        P("dp"),
        P(),
    )
    return jax.shard_map(
        functools.partial(per_device, mesh.shape["dp"] // 2),
        mesh=mesh,
        in_specs=placed,
        out_specs=(P("dp", "mp"), P("dp", "mp"), P("dp", "mp"), P()),
        check_vma=False,
    )
```

time: 146 us -> 146 us (level)
  the two profiles are of different devices: /device:TPU:1 before, /device:TPU:99 now
where the time goes in v2:
time: 146 us; the launch traced here: 145 us
  starting transfers between devices  111 us (76%)
  waiting for transfers between devices  18.7 us (13%)
  Pallas kernels  9.23 us (6%)
  local copies, waits for them, and re-layouts  3.37 us (2%)
  between operations  2.45 us (2%)
    ppermute x10, starting transfers between devices, along_z(): return lax.ppermute(x, 'dp', pairs)  57.9 us
    ppermute x4, starting transfers between devices, to_sibling(): return lax.ppermute(x, 'dp', [(i, i ^ 1) for i in range(2 * pairs_z)])  32.7 us
    ppermute x6, starting transfers between devices, in_plane(): return lax.ppermute(x, ALL, pairs)  20.4 us
    ppermute x10, waiting for transfers between devices, along_z(): return lax.ppermute(x, 'dp', pairs)  16.8 us
    pallas_call x7, Pallas kernels, call(): pl.pallas_call(kernel, out_shape=out_shape, in_specs=[SM] * scalars + [VM...  9.23 us
  transfers between devices with their start and end apart: 20, of which 6 were waited for; matrix products, arithmetic and copies ran while one was open for 1% of the time, Pallas kernels for 4%

profile of v2, /device:TPU:99, one launch (start us, length us, event | category | flops | bytes accessed | tf_op | source)
XLA Modules:
  0.0 144.8 jit_solution(6856825249494017994)
XLA Ops:
  2.8 2.6 %collective-permute-start.7 = (bf16[112,384]{1,0:T(8,128)(2,1)S(1)}, bf16[112,384]{1,0:T(8,128)(2,1)S(1)}, u32[]{:S(2)}, u32[]{:S(2)}) collective-permute-start(bf16[112,384]{1,0:T(8,128)(2,1)S(1)} %make_unit.1.refs_0_), channel_id=1, source_target_pairs={{0,16},{16,0},{32,48},{48,32},{64,80},{80,64},{96,112},{112,96},{1... | collective-permute-start | bytes 258056 | tf_op jit(solution)/shard_map/ppermute | solution.py:31
  6.4 20.2 %collective-permute-start.8 = (bf16[224,384]{1,0:T(8,128)(2,1)S(1)}, bf16[224,384]{1,0:T(8,128)(2,1)S(1)}, u32[]{:S(2)}, u32[]{:S(2)}) collective-permute-start(bf16[224,384]{1,0:T(8,128)(2,1)S(1)} %pad_maximum_fusion.1), channel_id=1, source_target_pairs={{0,256},{16,784},{32,288},{48,816},{64,320},{80,848},{96,352},{112... | collective-permute-start | bytes 516104 | tf_op jit(solution)/shard_map/ppermute | solution.py:27
  26.7 10.5 %collective-permute-done.8 = bf16[224,384]{1,0:T(8,128)(2,1)S(1)} collective-permute-done((bf16[224,384]{1,0:T(8,128)(2,1)S(1)}, bf16[224,384]{1,0:T(8,128)(2,1)S(1)}, u32[]{:S(2)}, u32[]{:S(2)}) %collective-permute-start.8) | collective-permute-done | bytes 172064 | tf_op jit(solution)/shard_map/ppermute | solution.py:27
  37.3 12.8 %collective-permute-start.10 = (bf16[112,384]{1,0:T(8,128)(2,1)S(1)}, bf16[112,384]{1,0:T(8,128)(2,1)S(1)}, u32[]{:S(2)}, u32[]{:S(2)}) collective-permute-start(bf16[112,384]{1,0:T(8,128)(2,1)S(1)} %get-tuple-element.27.refs_3_), channel_id=1, source_target_pairs={{0,256},{16,784},{32,288},{48,816},{64,320},{80,848},{96,352},{112... | collective-permute-start | bytes 258056 | tf_op jit(solution)/shard_map/ppermute | solution.py:27
  50.1 1.9 %collective-permute-start.9 = (bf16[112,384]{1,0:T(8,128)(2,1)S(1)}, bf16[112,384]{1,0:T(8,128)(2,1)S(1)}, u32[]{:S(2)}, u32[]{:S(2)}) collective-permute-start(bf16[112,384]{1,0:T(8,128)(2,1)S(1)} %get-tuple-element.28), channel_id=1, source_target_pairs={{0,16},{16,0},{32,48},{48,32},{64,80},{80,64},{96,112},{112,96},{1... | collective-permute-start | bytes 258056 | tf_op jit(solution)/shard_map/ppermute | solution.py:31
  52.1 2.4 %collective-permute-start = (bf16[2,96,256]{2,1,0:T(8,128)(2,1)S(1)}, bf16[2,96,256]{2,1,0:T(8,128)(2,1)S(1)}, u32[]{:S(2)}, u32[]{:S(2)}) collective-permute-start(bf16[2,96,256]{2,1,0:T(8,128)(2,1)S(1)} %fusion), channel_id=1, source_target_pairs={{0,16},{16,0},{32,48},{48,32},{64,80},{80,64},{96,112},{112,96},{1... | collective-permute-start | bytes 294920 | tf_op jit(solution)/shard_map/ppermute | solution.py:31
  54.5 1.9 %collective-permute-start.15 = (bf16[400,384]{1,0:T(8,128)(2,1)S(1)}, bf16[400,384]{1,0:T(8,128)(2,1)}, u32[]{:S(2)}, u32[]{:S(2)}) collective-permute-start(bf16[400,384]{1,0:T(8,128)(2,1)S(1)} %join_units.1.refs_4_), channel_id=1, source_target_pairs={{0,992},{16,48},{32,0},{48,80},{64,32},{80,112},{96,64},{112,144},... | collective-permute-start | bytes 921608 | tf_op jit(solution)/shard_map/ppermute | solution.py:27
  56.5 4.4 %collective-permute-start.11 = (bf16[400,384]{1,0:T(8,128)(2,1)S(1)}, bf16[400,384]{1,0:T(8,128)(2,1)}, u32[]{:S(2)}, u32[]{:S(2)}) collective-permute-start(bf16[400,384]{1,0:T(8,128)(2,1)S(1)} %join_units.1.refs_4_), channel_id=1, source_target_pairs={{0,32},{16,1008},{32,64},{48,16},{64,96},{80,48},{96,128},{112,80}... | collective-permute-start | bytes 921608 | tf_op jit(solution)/shard_map/ppermute | solution.py:27
  60.9 3.0 %collective-permute-done.15.refs_6_ = bf16[400,384]{1,0:T(8,128)(2,1)} collective-permute-done((bf16[400,384]{1,0:T(8,128)(2,1)S(1)}, bf16[400,384]{1,0:T(8,128)(2,1)}, u32[]{:S(2)}, u32[]{:S(2)}) %collective-permute-start.15) | collective-permute-done | bytes 307232 | tf_op jit(solution)/shard_map/ppermute | solution.py:27
  65.9 3.2 %collective-permute-start.1 = (bf16[192,512]{1,0:T(8,128)(2,1)S(1)}, bf16[192,512]{1,0:T(8,128)(2,1)S(1)}, u32[]{:S(2)}, u32[]{:S(2)}) collective-permute-start(bf16[192,512]{1,0:T(8,128)(2,1)S(1)} %bitcast.36), channel_id=1, source_target_pairs={{0,4},{1,5},{2,6},{3,7},{4,8},{5,9},{6,10},{7,11},{8,12},{9,13},{1... | collective-permute-start | bytes 589832 | tf_op jit(solution)/shard_map/ppermute | solution.py:45
  69.1 4.5 %collective-permute-start.2 = (bf16[192,512]{1,0:T(8,128)(2,1)S(1)}, bf16[192,512]{1,0:T(8,128)(2,1)S(1)}, u32[]{:S(2)}, u32[]{:S(2)}) collective-permute-start(bf16[192,512]{1,0:T(8,128)(2,1)S(1)} %bitcast.37), channel_id=1, source_target_pairs={{0,8},{1,9},{2,10},{3,11},{4,12},{5,13},{6,14},{7,15},{8,0},{9,1},... | collective-permute-start | bytes 589832 | tf_op jit(solution)/shard_map/ppermute | solution.py:45
  73.7 3.0 %collective-permute-start.3 = (bf16[192,512]{1,0:T(8,128)(2,1)S(1)}, bf16[192,512]{1,0:T(8,128)(2,1)S(1)}, u32[]{:S(2)}, u32[]{:S(2)}) collective-permute-start(bf16[192,512]{1,0:T(8,128)(2,1)S(1)} %bitcast.38), channel_id=1, source_target_pairs={{0,12},{1,13},{2,14},{3,15},{4,0},{5,1},{6,2},{7,3},{8,4},{9,5},{1... | collective-permute-start | bytes 589832 | tf_op jit(solution)/shard_map/ppermute | solution.py:45
  76.7 4.1 %collective-permute-start.12 = (bf16[400,384]{1,0:T(8,128)(2,1)}, bf16[400,384]{1,0:T(8,128)(2,1)}, u32[]{:S(2)}, u32[]{:S(2)}) collective-permute-start(bf16[400,384]{1,0:T(8,128)(2,1)} %collective-permute-done.11.refs_5_), channel_id=1, source_target_pairs={{0,32},{16,1008},{32,64},{48,16},{64,96},{80,48},{96,128},{112,80}... | collective-permute-start | bytes 921608 | tf_op jit(solution)/shard_map/ppermute | solution.py:27
  81.0 3.1 %collective-permute-start.4 = (bf16[768,512]{1,0:T(8,128)(2,1)S(1)}, bf16[768,512]{1,0:T(8,128)(2,1)S(1)}, u32[]{:S(2)}, u32[]{:S(2)}) collective-permute-start(bf16[768,512]{1,0:T(8,128)(2,1)S(1)} %stack.1.refs_0_), channel_id=1, source_target_pairs={{0,1},{1,2},{2,3},{3,0},{4,5},{5,6},{6,7},{7,4},{8,9},{9,10},{10,1... | collective-permute-start | bytes 2359304 | tf_op jit(solution)/shard_map/ppermute | solution.py:45
  84.1 2.7 %collective-permute-start.5 = (bf16[768,512]{1,0:T(8,128)(2,1)S(1)}, bf16[768,512]{1,0:T(8,128)(2,1)S(1)}, u32[]{:S(2)}, u32[]{:S(2)}) collective-permute-start(bf16[768,512]{1,0:T(8,128)(2,1)S(1)} %stack.1.refs_0_), channel_id=1, source_target_pairs={{0,2},{1,3},{2,0},{3,1},{4,6},{5,7},{6,4},{7,5},{8,10},{9,11},{10,... | collective-permute-start | bytes 2359304 | tf_op jit(solution)/shard_map/ppermute | solution.py:45
  86.8 3.8 %collective-permute-start.6 = (bf16[768,512]{1,0:T(8,128)(2,1)S(1)}, bf16[768,512]{1,0:T(8,128)(2,1)S(1)}, u32[]{:S(2)}, u32[]{:S(2)}) collective-permute-start(bf16[768,512]{1,0:T(8,128)(2,1)S(1)} %stack.1.refs_0_), channel_id=1, source_target_pairs={{0,3},{1,0},{2,1},{3,2},{4,7},{5,4},{6,5},{7,6},{8,11},{9,8},{10,9... | collective-permute-start | bytes 2359304 | tf_op jit(solution)/shard_map/ppermute | solution.py:45
  90.6 2.4 %collective-permute-start.17 = (bf16[400,384]{1,0:T(8,128)(2,1)}, bf16[400,384]{1,0:T(8,128)(2,1)}, u32[]{:S(2)}, u32[]{:S(2)}) collective-permute-start(bf16[400,384]{1,0:T(8,128)(2,1)} %collective-permute-done.16.refs_8_), channel_id=1, source_target_pairs={{0,992},{16,48},{32,0},{48,80},{64,32},{80,112},{96,64},{112,144},... | collective-permute-start | bytes 921608 | tf_op jit(solution)/shard_map/ppermute | solution.py:27
  93.1 3.2 %collective-permute-start.13 = (bf16[400,384]{1,0:T(8,128)(2,1)}, bf16[400,384]{1,0:T(8,128)(2,1)S(1)}, u32[]{:S(2)}, u32[]{:S(2)}) collective-permute-start(bf16[400,384]{1,0:T(8,128)(2,1)} %collective-permute-done.12.refs_7_), channel_id=1, source_target_pairs={{0,32},{16,1008},{32,64},{48,16},{64,96},{80,48},{96,128},{112,80}... | collective-permute-start | bytes 921608 | tf_op jit(solution)/shard_map/ppermute | solution.py:27
  96.3 3.1 %collective-permute-done.17.refs_10_ = bf16[400,384]{1,0:T(8,128)(2,1)} collective-permute-done((bf16[400,384]{1,0:T(8,128)(2,1)}, bf16[400,384]{1,0:T(8,128)(2,1)}, u32[]{:S(2)}, u32[]{:S(2)}) %collective-permute-start.17) | collective-permute-done | bytes 307232 | tf_op jit(solution)/shard_map/ppermute | solution.py:27
  101.1 5.0 %collective-permute-start.18 = (bf16[208,384]{1,0:T(8,128)(2,1)S(1)}, bf16[208,384]{1,0:T(8,128)(2,1)S(1)}, u32[]{:S(2)}, u32[]{:S(2)}) collective-permute-start(bf16[208,384]{1,0:T(8,128)(2,1)S(1)} %pad_maximum_fusion.3), channel_id=1, source_target_pairs={{0,992},{16,48},{32,0},{48,80},{64,32},{80,112},{96,64},{112,144},... | collective-permute-start | bytes 479240 | tf_op jit(solution)/shard_map/ppermute | solution.py:27
  106.2 1.9 %collective-permute-start.14 = (bf16[208,384]{1,0:T(8,128)(2,1)S(1)}, bf16[208,384]{1,0:T(8,128)(2,1)S(1)}, u32[]{:S(2)}, u32[]{:S(2)}) collective-permute-start(bf16[208,384]{1,0:T(8,128)(2,1)S(1)} %pad_maximum_fusion.2), channel_id=1, source_target_pairs={{0,32},{16,1008},{32,64},{48,16},{64,96},{80,48},{96,128},{112,80}... | collective-permute-start | bytes 479240 | tf_op jit(solution)/shard_map/ppermute | solution.py:27
  108.2 5.4 %project_first.1 = (f32[512,384]{1,0:T(8,128)S(1)}, f32[16,384]{1,0:T(8,128)S(1)}) custom-call(s32[32]{0:T(128)S(1)} %fusion.9.starts, s32[32]{0:T(128)S(1)} %get-tuple-element.20.outers, bf16[768,512]{1,0:T(8,128)(2,1)S(1)} %stack.1.refs_0_, bf16[768,512]{1,0:T(8,128)(2,1)S(1)} %collective-permute-done.4.refs_1_, ...), custom_call_target="tpu_custom_call" | custom-call | flops 1056964608 | bytes 6291456 | tf_op jit(solution)/shard_map/project_first/pallas_call | solution.py:220
  114.9 25.7 %collective-permute-start.19 = (f32[264,384]{1,0:T(8,128)S(1)}, f32[264,384]{1,0:T(8,128)S(1)}, u32[]{:S(2)}, u32[]{:S(2)}) collective-permute-start(f32[264,384]{1,0:T(8,128)S(1)} %get-tuple-element.15), channel_id=1, source_target_pairs={{0,16},{16,0},{32,48},{48,32},{64,80},{80,64},{96,112},{112,96},{1... | collective-permute-start | bytes 1216520 | tf_op jit(solution)/shard_map/ppermute | solution.py:31
  142.7 2.2 %attention.1 = (bf16[256,384]{1,0:T(8,128)(2,1)}, bf16[256,384]{1,0:T(8,128)(2,1)}, bf16[256,384]{1,0:T(8,128)(2,1)}, f32[1,32]{1,0:T(1,128)}) custom-call(s32[1]{0:T(128)S(6)} %copy.22.group, f32[264,384]{1,0:T(8,128)S(1)} %get-tuple-element.14.mine_ref, f32[264,384]{1,0:T(8,128)S(1)} %collective-permute-done.19.got_ref, f32[1,32]{1,0:T(1,128)S(1)} %bitcast.41, ...), custom_call_target="tpu_custom_call" | custom-call | flops 201326592 | bytes 3145728 | tf_op jit(solution)/shard_map/attention/pallas_call | solution.py:220
  (55 shorter events, 9.2 us)
Async XLA Ops:
  2.8 3.5 %collective-permute-start.7 = (bf16[112,384]{1,0:T(8,128)(2,1)S(1)}, bf16[112,384]{1,0:T(8,128)(2,1)S(1)}, u32[]{:S(2)}, u32[]{:S(2)}) collective-permute-start(bf16[112,384]{1,0:T(8,128)(2,1)S(1)} %make_unit.1.refs_0_), channel_id=1, source_target_pairs={{0,16},{16,0},{32,48},{48,32},{64,80},{80,64},{96,112},{112,96},{1... | collective-permute-start | bytes 258056 | tf_op jit(solution)/shard_map/ppermute | solution.py:31
  6.3 20.2 %copy-start.5 = (bf16[256,384]{1,0:T(8,128)(2,1)S(1)}, bf16[256,384]{1,0:T(8,128)(2,1)}, u32[]{:S(2)}) copy-start(bf16[256,384]{1,0:T(8,128)(2,1)} %param.9) | copy-start | bytes 589828
  6.4 30.9 %collective-permute-start.8 = (bf16[224,384]{1,0:T(8,128)(2,1)S(1)}, bf16[224,384]{1,0:T(8,128)(2,1)S(1)}, u32[]{:S(2)}, u32[]{:S(2)}) collective-permute-start(bf16[224,384]{1,0:T(8,128)(2,1)S(1)} %pad_maximum_fusion.1), channel_id=1, source_target_pairs={{0,256},{16,784},{32,288},{48,816},{64,320},{80,848},{96,352},{112... | collective-permute-start | bytes 516104 | tf_op jit(solution)/shard_map/ppermute | solution.py:27
  37.3 17.2 %collective-permute-start.10 = (bf16[112,384]{1,0:T(8,128)(2,1)S(1)}, bf16[112,384]{1,0:T(8,128)(2,1)S(1)}, u32[]{:S(2)}, u32[]{:S(2)}) collective-permute-start(bf16[112,384]{1,0:T(8,128)(2,1)S(1)} %get-tuple-element.27.refs_3_), channel_id=1, source_target_pairs={{0,256},{16,784},{32,288},{48,816},{64,320},{80,848},{96,352},{112... | collective-permute-start | bytes 258056 | tf_op jit(solution)/shard_map/ppermute | solution.py:27
  50.1 4.4 %collective-permute-start.9 = (bf16[112,384]{1,0:T(8,128)(2,1)S(1)}, bf16[112,384]{1,0:T(8,128)(2,1)S(1)}, u32[]{:S(2)}, u32[]{:S(2)}) collective-permute-start(bf16[112,384]{1,0:T(8,128)(2,1)S(1)} %get-tuple-element.28), channel_id=1, source_target_pairs={{0,16},{16,0},{32,48},{48,32},{64,80},{80,64},{96,112},{112,96},{1... | collective-permute-start | bytes 258056 | tf_op jit(solution)/shard_map/ppermute | solution.py:31
  52.1 8.9 %collective-permute-start = (bf16[2,96,256]{2,1,0:T(8,128)(2,1)S(1)}, bf16[2,96,256]{2,1,0:T(8,128)(2,1)S(1)}, u32[]{:S(2)}, u32[]{:S(2)}) collective-permute-start(bf16[2,96,256]{2,1,0:T(8,128)(2,1)S(1)} %fusion), channel_id=1, source_target_pairs={{0,16},{16,0},{32,48},{48,32},{64,80},{80,64},{96,112},{112,96},{1... | collective-permute-start | bytes 294920 | tf_op jit(solution)/shard_map/ppermute | solution.py:31
  54.5 9.5 %collective-permute-start.15 = (bf16[400,384]{1,0:T(8,128)(2,1)S(1)}, bf16[400,384]{1,0:T(8,128)(2,1)}, u32[]{:S(2)}, u32[]{:S(2)}) collective-permute-start(bf16[400,384]{1,0:T(8,128)(2,1)S(1)} %join_units.1.refs_4_), channel_id=1, source_target_pairs={{0,992},{16,48},{32,0},{48,80},{64,32},{80,112},{96,64},{112,144},... | collective-permute-start | bytes 921608 | tf_op jit(solution)/shard_map/ppermute | solution.py:27
  56.5 20.2 %collective-permute-start.11 = (bf16[400,384]{1,0:T(8,128)(2,1)S(1)}, bf16[400,384]{1,0:T(8,128)(2,1)}, u32[]{:S(2)}, u32[]{:S(2)}) collective-permute-start(bf16[400,384]{1,0:T(8,128)(2,1)S(1)} %join_units.1.refs_4_), channel_id=1, source_target_pairs={{0,32},{16,1008},{32,64},{48,16},{64,96},{80,48},{96,128},{112,80}... | collective-permute-start | bytes 921608 | tf_op jit(solution)/shard_map/ppermute | solution.py:27
  64.0 26.6 %collective-permute-start.16 = (bf16[400,384]{1,0:T(8,128)(2,1)}, bf16[400,384]{1,0:T(8,128)(2,1)}, u32[]{:S(2)}, u32[]{:S(2)}) collective-permute-start(bf16[400,384]{1,0:T(8,128)(2,1)} %collective-permute-done.15.refs_6_), channel_id=1, source_target_pairs={{0,992},{16,48},{32,0},{48,80},{64,32},{80,112},{96,64},{112,144},... | collective-permute-start | bytes 921608 | tf_op jit(solution)/shard_map/ppermute | solution.py:27
  65.9 14.9 %collective-permute-start.1 = (bf16[192,512]{1,0:T(8,128)(2,1)S(1)}, bf16[192,512]{1,0:T(8,128)(2,1)S(1)}, u32[]{:S(2)}, u32[]{:S(2)}) collective-permute-start(bf16[192,512]{1,0:T(8,128)(2,1)S(1)} %bitcast.36), channel_id=1, source_target_pairs={{0,4},{1,5},{2,6},{3,7},{4,8},{5,9},{6,10},{7,11},{8,12},{9,13},{1... | collective-permute-start | bytes 589832 | tf_op jit(solution)/shard_map/ppermute | solution.py:45
  69.1 11.7 %collective-permute-start.2 = (bf16[192,512]{1,0:T(8,128)(2,1)S(1)}, bf16[192,512]{1,0:T(8,128)(2,1)S(1)}, u32[]{:S(2)}, u32[]{:S(2)}) collective-permute-start(bf16[192,512]{1,0:T(8,128)(2,1)S(1)} %bitcast.37), channel_id=1, source_target_pairs={{0,8},{1,9},{2,10},{3,11},{4,12},{5,13},{6,14},{7,15},{8,0},{9,1},... | collective-permute-start | bytes 589832 | tf_op jit(solution)/shard_map/ppermute | solution.py:45
  73.7 7.2 %collective-permute-start.3 = (bf16[192,512]{1,0:T(8,128)(2,1)S(1)}, bf16[192,512]{1,0:T(8,128)(2,1)S(1)}, u32[]{:S(2)}, u32[]{:S(2)}) collective-permute-start(bf16[192,512]{1,0:T(8,128)(2,1)S(1)} %bitcast.38), channel_id=1, source_target_pairs={{0,12},{1,13},{2,14},{3,15},{4,0},{5,1},{6,2},{7,3},{8,4},{9,5},{1... | collective-permute-start | bytes 589832 | tf_op jit(solution)/shard_map/ppermute | solution.py:45
  76.7 16.4 %collective-permute-start.12 = (bf16[400,384]{1,0:T(8,128)(2,1)}, bf16[400,384]{1,0:T(8,128)(2,1)}, u32[]{:S(2)}, u32[]{:S(2)}) collective-permute-start(bf16[400,384]{1,0:T(8,128)(2,1)} %collective-permute-done.11.refs_5_), channel_id=1, source_target_pairs={{0,32},{16,1008},{32,64},{48,16},{64,96},{80,48},{96,128},{112,80}... | collective-permute-start | bytes 921608 | tf_op jit(solution)/shard_map/ppermute | solution.py:27
  81.0 27.2 %collective-permute-start.4 = (bf16[768,512]{1,0:T(8,128)(2,1)S(1)}, bf16[768,512]{1,0:T(8,128)(2,1)S(1)}, u32[]{:S(2)}, u32[]{:S(2)}) collective-permute-start(bf16[768,512]{1,0:T(8,128)(2,1)S(1)} %stack.1.refs_0_), channel_id=1, source_target_pairs={{0,1},{1,2},{2,3},{3,0},{4,5},{5,6},{6,7},{7,4},{8,9},{9,10},{10,1... | collective-permute-start | bytes 2359304 | tf_op jit(solution)/shard_map/ppermute | solution.py:45
  84.1 24.1 %collective-permute-start.5 = (bf16[768,512]{1,0:T(8,128)(2,1)S(1)}, bf16[768,512]{1,0:T(8,128)(2,1)S(1)}, u32[]{:S(2)}, u32[]{:S(2)}) collective-permute-start(bf16[768,512]{1,0:T(8,128)(2,1)S(1)} %stack.1.refs_0_), channel_id=1, source_target_pairs={{0,2},{1,3},{2,0},{3,1},{4,6},{5,7},{6,4},{7,5},{8,10},{9,11},{10,... | collective-permute-start | bytes 2359304 | tf_op jit(solution)/shard_map/ppermute | solution.py:45
  86.8 21.3 %collective-permute-start.6 = (bf16[768,512]{1,0:T(8,128)(2,1)S(1)}, bf16[768,512]{1,0:T(8,128)(2,1)S(1)}, u32[]{:S(2)}, u32[]{:S(2)}) collective-permute-start(bf16[768,512]{1,0:T(8,128)(2,1)S(1)} %stack.1.refs_0_), channel_id=1, source_target_pairs={{0,3},{1,0},{2,1},{3,2},{4,7},{5,4},{6,5},{7,6},{8,11},{9,8},{10,9... | collective-permute-start | bytes 2359304 | tf_op jit(solution)/shard_map/ppermute | solution.py:45
  90.6 8.8 %collective-permute-start.17 = (bf16[400,384]{1,0:T(8,128)(2,1)}, bf16[400,384]{1,0:T(8,128)(2,1)}, u32[]{:S(2)}, u32[]{:S(2)}) collective-permute-start(bf16[400,384]{1,0:T(8,128)(2,1)} %collective-permute-done.16.refs_8_), channel_id=1, source_target_pairs={{0,992},{16,48},{32,0},{48,80},{64,32},{80,112},{96,64},{112,144},... | collective-permute-start | bytes 921608 | tf_op jit(solution)/shard_map/ppermute | solution.py:27
  93.1 13.0 %collective-permute-start.13 = (bf16[400,384]{1,0:T(8,128)(2,1)}, bf16[400,384]{1,0:T(8,128)(2,1)S(1)}, u32[]{:S(2)}, u32[]{:S(2)}) collective-permute-start(bf16[400,384]{1,0:T(8,128)(2,1)} %collective-permute-done.12.refs_7_), channel_id=1, source_target_pairs={{0,32},{16,1008},{32,64},{48,16},{64,96},{80,48},{96,128},{112,80}... | collective-permute-start | bytes 921608 | tf_op jit(solution)/shard_map/ppermute | solution.py:27
  101.1 12.5 %collective-permute-start.18 = (bf16[208,384]{1,0:T(8,128)(2,1)S(1)}, bf16[208,384]{1,0:T(8,128)(2,1)S(1)}, u32[]{:S(2)}, u32[]{:S(2)}) collective-permute-start(bf16[208,384]{1,0:T(8,128)(2,1)S(1)} %pad_maximum_fusion.3), channel_id=1, source_target_pairs={{0,992},{16,48},{32,0},{48,80},{64,32},{80,112},{96,64},{112,144},... | collective-permute-start | bytes 479240 | tf_op jit(solution)/shard_map/ppermute | solution.py:27
  106.2 7.5 %collective-permute-start.14 = (bf16[208,384]{1,0:T(8,128)(2,1)S(1)}, bf16[208,384]{1,0:T(8,128)(2,1)S(1)}, u32[]{:S(2)}, u32[]{:S(2)}) collective-permute-start(bf16[208,384]{1,0:T(8,128)(2,1)S(1)} %pad_maximum_fusion.2), channel_id=1, source_target_pairs={{0,32},{16,1008},{32,64},{48,16},{64,96},{80,48},{96,128},{112,80}... | collective-permute-start | bytes 479240 | tf_op jit(solution)/shard_map/ppermute | solution.py:27
  113.7 27.0 %copy-start = (bf16[256,384]{1,0:T(8,128)(2,1)S(1)}, bf16[256,384]{1,0:T(8,128)(2,1)}, u32[]{:S(2)}) copy-start(bf16[256,384]{1,0:T(8,128)(2,1)} %q_ref.3) | copy-start | bytes 589828
  113.7 27.0 %copy-start.1 = (bf16[256,384]{1,0:T(8,128)(2,1)S(1)}, bf16[256,384]{1,0:T(8,128)(2,1)}, u32[]{:S(2)}) copy-start(bf16[256,384]{1,0:T(8,128)(2,1)} %k_ref.3) | copy-start | bytes 589828
  114.9 27.1 %copy-start.2 = (bf16[256,384]{1,0:T(8,128)(2,1)S(1)}, bf16[256,384]{1,0:T(8,128)(2,1)}, u32[]{:S(2)}) copy-start(bf16[256,384]{1,0:T(8,128)(2,1)} %v_ref.1) | copy-start | bytes 589828
  114.9 27.1 %collective-permute-start.19 = (f32[264,384]{1,0:T(8,128)S(1)}, f32[264,384]{1,0:T(8,128)S(1)}, u32[]{:S(2)}, u32[]{:S(2)}) collective-permute-start(f32[264,384]{1,0:T(8,128)S(1)} %get-tuple-element.15), channel_id=1, source_target_pairs={{0,16},{16,0},{32,48},{48,32},{64,80},{80,64},{96,112},{112,96},{1... | collective-permute-start | bytes 1216520 | tf_op jit(solution)/shard_map/ppermute | solution.py:31
  (4 other events, 25.9 us)

commit v3 on v2

--- a/solution.py
+++ b/solution.py
@@ -15,6 +15,8 @@
 UNIT = 96
 STATS = 4
 TAIL = 16
+HALF = 2 * UNIT + TAIL
+FULL = 4 * UNIT + TAIL
 ALL = ("dp", "mp")
 
 
@@ -49,24 +51,29 @@
     return [block] + [in_plane(block, step, first_axis, pairs_z) for step in (1, 2, -1)]
 
 
-def gather_weight(unit, other, first, pairs_z):
+def gather(unit, other, block, first, pairs_z):
     chip = jnp.concatenate([jnp.where(first, unit, other), jnp.where(first, other, unit)])
     got = along_z(chip, FAR, -FAR, pairs_z)
     rows = unit.shape[0]
     got0, got1 = got[:rows], got[rows:]
     mine = jnp.where(first, got0, got1)
+    row = ring_of_four(block, True, pairs_z)
+    mine, *row = lax.optimization_barrier((mine, *row))
     farthest = along_z(mine, FAR, -FAR, pairs_z)
     opposite = to_sibling(jnp.where(first, got1, got0), pairs_z)
     bundle = join_units(unit, opposite, farthest, mine)
-    pieces = [bundle]
+    row = stack(row)
+    pieces, features = [bundle], [row]
     p = q = bundle
-    for _ in range(FAR // 2 - 1):
+    for step in (2, 1, -1):
+        features.append(in_plane(row, step, False, pairs_z))
         p = along_z(p, 1, -1, pairs_z)
         q = along_z(q, -1, 1, pairs_z)
+        row, p = lax.optimization_barrier((row, p))
         pieces += [p, q]
-    p = along_z(jnp.concatenate([p[: 2 * UNIT], p[4 * UNIT :]]), 1, -1, pairs_z)
-    q = along_z(jnp.concatenate([q[UNIT : 3 * UNIT], q[4 * UNIT :]]), -1, 1, pairs_z)
-    return pieces + [p, q]
+    p = along_z(p[:HALF], 1, -1, pairs_z)
+    q = along_z(q[UNIT : UNIT + HALF], -1, 1, pairs_z)
+    return pieces + [p, q], [features[i] for i in (0, 2, 1, 3)]
 
 
 def piece_offsets():
@@ -97,10 +104,14 @@
     *units, out = refs
     tail = jnp.zeros((TAIL, out.shape[1]), jnp.float32)
     for i, ref in enumerate(units):
-        out[pl.ds(i * UNIT, UNIT), :] = ref[pl.ds(0, UNIT), :]
+        out[pl.ds(row_of(i), UNIT), :] = ref[pl.ds(0, UNIT), :]
         rows = ref[pl.ds(UNIT, TAIL), :].astype(jnp.float32)
         tail += pltpu.roll(rows, STATS * i, 0) if i else rows
-    out[pl.ds(len(units) * UNIT, TAIL), :] = tail.astype(jnp.bfloat16)
+    out[pl.ds(2 * UNIT, TAIL), :] = tail.astype(jnp.bfloat16)
+
+
+def row_of(i):
+    return i * UNIT + (TAIL if i >= 2 else 0)
 
 
 def stack_kernel(*refs):
@@ -110,7 +121,8 @@
         out[pl.ds(i * rows, rows), :] = ref[...]
 
 
-def scores_kernel(q_ref, k_ref, probs_ref):
+def scores_kernel(q_ref, k_ref, gw_ref, probs_ref, weights_ref):
+    weights_ref[...] = gw_ref[...]
     factor = 1.0 / jnp.sqrt(jnp.float32(HD))
     for h in range(q_ref.shape[1] // HD):
         cols = slice(h * HD, (h + 1) * HD)
@@ -141,32 +153,33 @@
 
 def first_kernel(starts, outers, *refs):
     blocks, pieces, (acc_ref, stats_ref, xs_ref) = refs[:4], refs[4:-3], refs[-3:]
-    depth = 4 * UNIT
+    xs_ref[pl.ds(2 * UNIT, TAIL), :] = jnp.zeros((TAIL, xs_ref.shape[1]), xs_ref.dtype)
     stats_ref[...] = jnp.zeros_like(stats_ref)
     for i, piece in enumerate(pieces):
         for k in range(4):
-            pick_rows(starts, outers, 4 * i + k, blocks, xs_ref, k * UNIT)
-        product = product_of(xs_ref[...], piece[pl.ds(0, depth), :])
+            pick_rows(starts, outers, 4 * i + k, blocks, xs_ref, row_of(k))
+        product = product_of(xs_ref[...], piece[...])
         if i == 0:
             acc_ref[...] = product
         else:
             acc_ref[...] += product
-        stats_ref[...] += piece[pl.ds(depth, TAIL), :].astype(jnp.float32)
+        stats_ref[...] += piece[pl.ds(2 * UNIT, TAIL), :].astype(jnp.float32)
 
 
 def last_kernel(starts, outers, core, *refs):
     blocks, (p_ref, q_ref, acc_ref, stats_ref, mine_ref, send_ref, xs_ref, w_ref, sum_ref) = refs[:4], refs[4:]
-    depth = 2 * UNIT
-    for k in range(4):
-        pick_rows(starts, outers, 28 + k, blocks, xs_ref, k * UNIT)
-    w_ref[pl.ds(0, depth), :] = p_ref[pl.ds(0, depth), :]
-    w_ref[pl.ds(depth, depth), :] = q_ref[pl.ds(0, depth), :]
+    for k, at in enumerate((0, UNIT, HALF, HALF + UNIT + TAIL)):
+        pick_rows(starts, outers, 28 + k, blocks, xs_ref, at)
+    for at in (2 * UNIT, HALF + UNIT):
+        xs_ref[pl.ds(at, TAIL), :] = jnp.zeros((TAIL, xs_ref.shape[1]), xs_ref.dtype)
+    w_ref[pl.ds(0, HALF), :] = p_ref[...]
+    w_ref[pl.ds(HALF, HALF), :] = q_ref[...]
     sum_ref[...] = acc_ref[...] + product_of(xs_ref[...], w_ref[...])
     stats = stats_ref[...]
     row = lax.broadcasted_iota(jnp.int32, stats.shape, 0)
-    stats += jnp.where(row < 8, p_ref[pl.ds(depth, TAIL), :].astype(jnp.float32), 0.0)
+    stats += jnp.where(row < 8, p_ref[pl.ds(2 * UNIT, TAIL), :].astype(jnp.float32), 0.0)
     middle = (row >= 4) & (row < 12)
-    stats += jnp.where(middle, q_ref[pl.ds(depth, TAIL), :].astype(jnp.float32), 0.0)
+    stats += jnp.where(middle, q_ref[pl.ds(UNIT, TAIL), :].astype(jnp.float32), 0.0)
     count = jnp.sum(jnp.where(row % 4 == 0, stats, 0.0), axis=0, keepdims=True)
     total = jnp.sum(jnp.where(row % 4 == 0, 0.0, stats), axis=0, keepdims=True)
     row8 = row[:8]
@@ -223,16 +236,21 @@
         in_specs=[SM] * scalars + [VM] * (len(operands) - scalars),
         out_specs=outs,
         scratch_shapes=scratch,
-        compiler_params=pltpu.CompilerParams(vmem_limit_bytes=40 * 2**20),
+        compiler_params=pltpu.CompilerParams(vmem_limit_bytes=16 * 2**20),
         cost_estimate=pl.CostEstimate(flops=flops, bytes_accessed=moved, transcendentals=0),
         name=name,
     )(*operands)
 
 
 def join_units(*units):
-    rows = len(units) * UNIT + TAIL
-    shape = jax.ShapeDtypeStruct((rows, units[0].shape[1]), units[0].dtype)
+    shape = jax.ShapeDtypeStruct((FULL, units[0].shape[1]), units[0].dtype)
     return call(join_kernel, "join_units", shape, units)
+
+
+def stack(blocks):
+    rows, width = blocks[0].shape
+    shape = jax.ShapeDtypeStruct((len(blocks) * rows, width), blocks[0].dtype)
+    return call(stack_kernel, "stack", shape, blocks)
 
 
 def per_device(pairs_z, cotangent, out_weight, queries, keys, values, image_loss, group_ids, group_weights):
@@ -261,14 +279,7 @@
     got = to_sibling(give, pairs_z)
     block = jnp.concatenate([jnp.where(first, keep, got), jnp.where(first, got, keep)], axis=2)
     block = block.reshape(2 * UNIT, 2 * PATCHES)
-    row_of_blocks = call(
-        stack_kernel,
-        "stack",
-        jax.ShapeDtypeStruct((8 * UNIT, 2 * PATCHES), bf16),
-        ring_of_four(block, True, pairs_z),
-    )
-    features = ring_of_four(row_of_blocks, False, pairs_z)
-    pieces = gather_weight(unit, other, first, pairs_z)
+    pieces, features = gather(unit, other, block, first, pairs_z)
 
     offsets = jnp.array([o for piece in piece_offsets() for o in piece], jnp.int32)
     source = (z + jnp.where(first, offsets, -offsets)) % pairs_z
@@ -284,7 +295,7 @@
         (total, jax.ShapeDtypeStruct((TAIL, heads), f32)),
         (starts, outer, *features, *pieces[:7]),
         2,
-        [pltpu.VMEM((4 * UNIT, 2 * PATCHES), bf16)],
+        [pltpu.VMEM((FULL, 2 * PATCHES), bf16)],
         2 * 512 * 2688 * heads,
         6 * 2**20,
     )
@@ -296,8 +307,8 @@
         (starts, outer, core.reshape(1), *features, *pieces[7:], summed, stats),
         3,
         [
-            pltpu.VMEM((4 * UNIT, 2 * PATCHES), bf16),
-            pltpu.VMEM((4 * UNIT, heads), bf16),
+            pltpu.VMEM((2 * HALF, 2 * PATCHES), bf16),
+            pltpu.VMEM((2 * HALF, heads), bf16),
             pltpu.VMEM((2 * PATCHES, heads), f32),
         ],
         2 * 512 * 384 * heads,
@@ -305,19 +316,20 @@
     )
     received = to_sibling(send, pairs_z)
 
-    probs = call(
+    group_row = jax.ShapeDtypeStruct((1, groups), f32)
+    probs, old_weights = call(
         scores_kernel,
         "scores",
-        jax.ShapeDtypeStruct((heads // HD, PATCHES, PATCHES), f32),
-        (queries, keys),
+        (jax.ShapeDtypeStruct((heads // HD, PATCHES, PATCHES), f32), group_row),
+        (queries, keys, group_weights.reshape(1, groups)),
         flops=2 * PATCHES * PATCHES * heads,
     )
     out = jax.ShapeDtypeStruct(queries.shape, bf16)
     query_grad, key_grad, value_grad, new_weights = call(
         attention_kernel,
         "attention",
-        (out, out, out, jax.ShapeDtypeStruct((1, groups), f32)),
-        (group_ids, mine, received, group_weights.reshape(1, groups), probs, queries, keys, values),
+        (out, out, out, group_row),
+        (group_ids, mine, received, old_weights, probs, queries, keys, values),
         1,
         flops=8 * PATCHES * PATCHES * heads,
         moved=3 * 2**20,

time: 146 us -> 134 us (0.918)
  the two profiles are of different devices: /device:TPU:99 before, /device:TPU:1 now
where the time goes in v3:
time: 134 us
  starting transfers between devices  106 us (79%)
  waiting for transfers between devices  12 us (9%)
  Pallas kernels  8.61 us (6%)
  local copies, waits for them, and re-layouts  4.54 us (3%)
  between operations  2.44 us (2%)
    ppermute x10, starting transfers between devices, along_z(): return lax.ppermute(x, 'dp', pairs)  57.6 us
    ppermute x4, starting transfers between devices, to_sibling(): return lax.ppermute(x, 'dp', [(i, i ^ 1) for i in range(2 * pairs_z)])  26.7 us
    ppermute x6, starting transfers between devices, in_plane(): return lax.ppermute(x, ALL, pairs)  21.7 us
    ppermute x10, waiting for transfers between devices, along_z(): return lax.ppermute(x, 'dp', pairs)  9.61 us
    pallas_call x7, Pallas kernels, call(): pl.pallas_call(kernel, out_shape=out_shape, in_specs=[SM] * scalars + [VM...  8.61 us
    unnamed x19, local copies, waits for them, and re-layouts  2.68 us
  transfers between devices with their start and end apart: 20, of which 7 were waited for; matrix products, arithmetic and copies ran while one was open for 2% of the time, Pallas kernels for 4%

profile of v3, /device:TPU:1, one launch (start us, length us, event | category | flops | bytes accessed | tf_op | source)
XLA Modules:
  0.0 133.7 jit_solution(4577700578328372308)
XLA Ops:
  2.8 16.1 %collective-permute-start = (bf16[112,384]{1,0:T(8,128)(2,1)S(1)}, bf16[112,384]{1,0:T(8,128)(2,1)S(1)}, u32[]{:S(2)}, u32[]{:S(2)}) collective-permute-start(bf16[112,384]{1,0:T(8,128)(2,1)S(1)} %make_unit.1.refs_0_), channel_id=1, source_target_pairs={{0,16},{16,0},{32,48},{48,32},{64,80},{80,64},{96,112},{112,96},{1... | collective-permute-start | bytes 258056 | tf_op jit(solution)/shard_map/ppermute | solution.py:33
  20.0 1.9 %collective-permute-start.2 = (bf16[2,96,256]{2,1,0:T(8,128)(2,1)S(1)}, bf16[2,96,256]{2,1,0:T(8,128)(2,1)S(1)}, u32[]{:S(2)}, u32[]{:S(2)}) collective-permute-start(bf16[2,96,256]{2,1,0:T(8,128)(2,1)S(1)} %fusion), channel_id=1, source_target_pairs={{0,16},{16,0},{32,48},{48,32},{64,80},{80,64},{96,112},{112,96},{1... | collective-permute-start | bytes 294920 | tf_op jit(solution)/shard_map/ppermute | solution.py:33
  22.0 10.1 %collective-permute-start.1 = (bf16[224,384]{1,0:T(8,128)(2,1)S(1)}, bf16[224,384]{1,0:T(8,128)(2,1)S(1)}, u32[]{:S(2)}, u32[]{:S(2)}) collective-permute-start(bf16[224,384]{1,0:T(8,128)(2,1)S(1)} %pad_maximum_fusion.1), channel_id=1, source_target_pairs={{0,256},{16,784},{32,288},{48,816},{64,320},{80,848},{96,352},{112... | collective-permute-start | bytes 516104 | tf_op jit(solution)/shard_map/ppermute | solution.py:29
  32.1 3.2 %collective-permute-start.3 = (bf16[192,512]{1,0:T(8,128)(2,1)S(1)}, bf16[192,512]{1,0:T(8,128)(2,1)S(1)}, u32[]{:S(2)}, u32[]{:S(2)}) collective-permute-start(bf16[192,512]{1,0:T(8,128)(2,1)S(1)} %bitcast.36), channel_id=1, source_target_pairs={{0,4},{1,5},{2,6},{3,7},{4,8},{5,9},{6,10},{7,11},{8,12},{9,13},{1... | collective-permute-start | bytes 589832 | tf_op jit(solution)/shard_map/ppermute | solution.py:47
  35.3 4.5 %collective-permute-start.4 = (bf16[192,512]{1,0:T(8,128)(2,1)S(1)}, bf16[192,512]{1,0:T(8,128)(2,1)S(1)}, u32[]{:S(2)}, u32[]{:S(2)}) collective-permute-start(bf16[192,512]{1,0:T(8,128)(2,1)S(1)} %bitcast.37), channel_id=1, source_target_pairs={{0,8},{1,9},{2,10},{3,11},{4,12},{5,13},{6,14},{7,15},{8,0},{9,1},... | collective-permute-start | bytes 589832 | tf_op jit(solution)/shard_map/ppermute | solution.py:47
  39.9 3.0 %collective-permute-start.5 = (bf16[192,512]{1,0:T(8,128)(2,1)S(1)}, bf16[192,512]{1,0:T(8,128)(2,1)S(1)}, u32[]{:S(2)}, u32[]{:S(2)}) collective-permute-start(bf16[192,512]{1,0:T(8,128)(2,1)S(1)} %bitcast.38), channel_id=1, source_target_pairs={{0,12},{1,13},{2,14},{3,15},{4,0},{5,1},{6,2},{7,3},{8,4},{9,5},{1... | collective-permute-start | bytes 589832 | tf_op jit(solution)/shard_map/ppermute | solution.py:47
  42.9 1.9 %collective-permute-start.6 = (bf16[112,384]{1,0:T(8,128)(2,1)S(1)}, bf16[112,384]{1,0:T(8,128)(2,1)S(1)}, u32[]{:S(2)}, u32[]{:S(2)}) collective-permute-start(bf16[112,384]{1,0:T(8,128)(2,1)S(1)} %get-tuple-element.51), channel_id=1, source_target_pairs={{0,16},{16,0},{32,48},{48,32},{64,80},{80,64},{96,112},{112,96},{1... | collective-permute-start | bytes 258056 | tf_op jit(solution)/shard_map/ppermute | solution.py:33
  46.3 15.4 %collective-permute-start.7 = (bf16[112,384]{1,0:T(8,128)(2,1)S(1)}, bf16[112,384]{1,0:T(8,128)(2,1)S(1)}, u32[]{:S(2)}, u32[]{:S(2)}) collective-permute-start(bf16[112,384]{1,0:T(8,128)(2,1)S(1)} %get-tuple-element.28.refs_3_), channel_id=1, source_target_pairs={{0,256},{16,784},{32,288},{48,816},{64,320},{80,848},{96,352},{112... | collective-permute-start | bytes 258056 | tf_op jit(solution)/shard_map/ppermute | solution.py:29
  63.3 9.2 %collective-permute-start.8 = (bf16[400,384]{1,0:T(8,128)(2,1)S(1)}, bf16[400,384]{1,0:T(8,128)(2,1)S(1)}, u32[]{:S(2)}, u32[]{:S(2)}) collective-permute-start(bf16[400,384]{1,0:T(8,128)(2,1)S(1)} %join_units.1.refs_4_), channel_id=1, source_target_pairs={{0,32},{16,1008},{32,64},{48,16},{64,96},{80,48},{96,128},{112,80}... | collective-permute-start | bytes 921608 | tf_op jit(solution)/shard_map/ppermute | solution.py:29
  72.5 1.9 %collective-permute-start.15 = (bf16[400,384]{1,0:T(8,128)(2,1)S(1)}, bf16[400,384]{1,0:T(8,128)(2,1)}, u32[]{:S(2)}, u32[]{:S(2)}) collective-permute-start(bf16[400,384]{1,0:T(8,128)(2,1)S(1)} %join_units.1.refs_4_), channel_id=1, source_target_pairs={{0,992},{16,48},{32,0},{48,80},{64,32},{80,112},{96,64},{112,144},... | collective-permute-start | bytes 921608 | tf_op jit(solution)/shard_map/ppermute | solution.py:29
  74.5 2.4 %collective-permute-done.8.refs_5_ = bf16[400,384]{1,0:T(8,128)(2,1)S(1)} collective-permute-done((bf16[400,384]{1,0:T(8,128)(2,1)S(1)}, bf16[400,384]{1,0:T(8,128)(2,1)S(1)}, u32[]{:S(2)}, u32[]{:S(2)}) %collective-permute-start.8) | collective-permute-done | bytes 307232 | tf_op jit(solution)/shard_map/ppermute | solution.py:29
  76.9 5.4 %collective-permute-start.11 = (bf16[400,384]{1,0:T(8,128)(2,1)S(1)}, bf16[400,384]{1,0:T(8,128)(2,1)}, u32[]{:S(2)}, u32[]{:S(2)}) collective-permute-start(bf16[400,384]{1,0:T(8,128)(2,1)S(1)} %collective-permute-done.8.refs_5_), channel_id=1, source_target_pairs={{0,32},{16,1008},{32,64},{48,16},{64,96},{80,48},{96,128},{112,80}... | collective-permute-start | bytes 921608 | tf_op jit(solution)/shard_map/ppermute | solution.py:29
  84.9 4.5 %collective-permute-start.10 = (bf16[768,512]{1,0:T(8,128)(2,1)S(1)}, bf16[768,512]{1,0:T(8,128)(2,1)S(1)}, u32[]{:S(2)}, u32[]{:S(2)}) collective-permute-start(bf16[768,512]{1,0:T(8,128)(2,1)S(1)} %stack.1.refs_0_), channel_id=1, source_target_pairs={{0,2},{1,3},{2,0},{3,1},{4,6},{5,7},{6,4},{7,5},{8,10},{9,11},{10,... | collective-permute-start | bytes 2359304 | tf_op jit(solution)/shard_map/ppermute | solution.py:47
  89.4 2.2 %collective-permute-start.9 = (bf16[768,512]{1,0:T(8,128)(2,1)S(1)}, bf16[768,512]{1,0:T(8,128)(2,1)S(1)}, u32[]{:S(2)}, u32[]{:S(2)}) collective-permute-start(bf16[768,512]{1,0:T(8,128)(2,1)S(1)} %stack.1.refs_0_), channel_id=1, source_target_pairs={{0,1},{1,2},{2,3},{3,0},{4,5},{5,6},{6,7},{7,4},{8,9},{9,10},{10,1... | collective-permute-start | bytes 2359304 | tf_op jit(solution)/shard_map/ppermute | solution.py:47
  91.7 4.3 %collective-permute-start.12 = (bf16[768,512]{1,0:T(8,128)(2,1)S(1)}, bf16[768,512]{1,0:T(8,128)(2,1)S(1)}, u32[]{:S(2)}, u32[]{:S(2)}) collective-permute-start(bf16[768,512]{1,0:T(8,128)(2,1)S(1)} %stack.1.refs_0_), channel_id=1, source_target_pairs={{0,3},{1,0},{2,1},{3,2},{4,7},{5,4},{6,5},{7,6},{8,11},{9,8},{10,9... | collective-permute-start | bytes 2359304 | tf_op jit(solution)/shard_map/ppermute | solution.py:47
  96.0 4.6 %collective-permute-start.13 = (bf16[400,384]{1,0:T(8,128)(2,1)}, bf16[400,384]{1,0:T(8,128)(2,1)}, u32[]{:S(2)}, u32[]{:S(2)}) collective-permute-start(bf16[400,384]{1,0:T(8,128)(2,1)} %collective-permute-done.11.refs_7_), channel_id=1, source_target_pairs={{0,32},{16,1008},{32,64},{48,16},{64,96},{80,48},{96,128},{112,80}... | collective-permute-start | bytes 921608 | tf_op jit(solution)/shard_map/ppermute | solution.py:29
  100.6 1.9 %collective-permute-start.17 = (bf16[400,384]{1,0:T(8,128)(2,1)}, bf16[400,384]{1,0:T(8,128)(2,1)}, u32[]{:S(2)}, u32[]{:S(2)}) collective-permute-start(bf16[400,384]{1,0:T(8,128)(2,1)} %collective-permute-done.16.refs_8_), channel_id=1, source_target_pairs={{0,992},{16,48},{32,0},{48,80},{64,32},{80,112},{96,64},{112,144},... | collective-permute-start | bytes 921608 | tf_op jit(solution)/shard_map/ppermute | solution.py:29
  102.6 2.1 %collective-permute-done.13.refs_9_ = bf16[400,384]{1,0:T(8,128)(2,1)} collective-permute-done((bf16[400,384]{1,0:T(8,128)(2,1)}, bf16[400,384]{1,0:T(8,128)(2,1)}, u32[]{:S(2)}, u32[]{:S(2)}) %collective-permute-start.13) | collective-permute-done | bytes 307232 | tf_op jit(solution)/shard_map/ppermute | solution.py:29
  105.6 5.2 %collective-permute-start.14 = (bf16[208,384]{1,0:T(8,128)(2,1)S(1)}, bf16[208,384]{1,0:T(8,128)(2,1)S(1)}, u32[]{:S(2)}, u32[]{:S(2)}) collective-permute-start(bf16[208,384]{1,0:T(8,128)(2,1)S(1)} %slice.24), channel_id=1, source_target_pairs={{0,32},{16,1008},{32,64},{48,16},{64,96},{80,48},{96,128},{112,80}... | collective-permute-start | bytes 479240 | tf_op jit(solution)/shard_map/ppermute | solution.py:29
  110.8 2.0 %collective-permute-done.17.refs_10_ = bf16[400,384]{1,0:T(8,128)(2,1)} collective-permute-done((bf16[400,384]{1,0:T(8,128)(2,1)}, bf16[400,384]{1,0:T(8,128)(2,1)}, u32[]{:S(2)}, u32[]{:S(2)}) %collective-permute-start.17) | collective-permute-done | bytes 307232 | tf_op jit(solution)/shard_map/ppermute | solution.py:29
  113.7 1.9 %collective-permute-start.18 = (bf16[208,384]{1,0:T(8,128)(2,1)S(1)}, bf16[208,384]{1,0:T(8,128)(2,1)S(1)}, u32[]{:S(2)}, u32[]{:S(2)}) collective-permute-start(bf16[208,384]{1,0:T(8,128)(2,1)S(1)} %slice.30), channel_id=1, source_target_pairs={{0,992},{16,48},{32,0},{48,80},{64,32},{80,112},{96,64},{112,144},... | collective-permute-start | bytes 479240 | tf_op jit(solution)/shard_map/ppermute | solution.py:29
  115.7 4.7 %project_first.1 = (f32[512,384]{1,0:T(8,128)S(1)}, f32[16,384]{1,0:T(8,128)S(1)}) custom-call(s32[32]{0:T(128)S(1)} %fusion.9.starts, s32[32]{0:T(128)S(1)} %get-tuple-element.44.outers, bf16[768,512]{1,0:T(8,128)(2,1)S(1)} %stack.1.refs_0_, bf16[768,512]{1,0:T(8,128)(2,1)S(1)} %collective-permute-done.9.refs_1_, ...), custom_call_target="tpu_custom_call" | custom-call | flops 1056964608 | bytes 6291456 | tf_op jit(solution)/shard_map/project_first/pallas_call | solution.py:233
  123.4 6.8 %collective-permute-start.19 = (f32[264,384]{1,0:T(8,128)S(1)}, f32[264,384]{1,0:T(8,128)S(1)}, u32[]{:S(2)}, u32[]{:S(2)}) collective-permute-start(f32[264,384]{1,0:T(8,128)S(1)} %get-tuple-element.37), channel_id=1, source_target_pairs={{0,16},{16,0},{32,48},{48,32},{64,80},{80,64},{96,112},{112,96},{1... | collective-permute-start | bytes 1216520 | tf_op jit(solution)/shard_map/ppermute | solution.py:33
  131.5 2.2 %attention.1 = (bf16[256,384]{1,0:T(8,128)(2,1)}, bf16[256,384]{1,0:T(8,128)(2,1)}, bf16[256,384]{1,0:T(8,128)(2,1)}, f32[1,32]{1,0:T(1,128)}) custom-call(s32[1]{0:T(128)S(6)} %copy.22.group, f32[264,384]{1,0:T(8,128)S(1)} %get-tuple-element.36.mine_ref, f32[264,384]{1,0:T(8,128)S(1)} %collective-permute-done.19.got_ref, ...), custom_call_target="tpu_custom_call" | custom-call | flops 201326592 | bytes 3145728 | tf_op jit(solution)/shard_map/attention/pallas_call | solution.py:233
  (53 shorter events, 13.9 us)
Async XLA Ops:
  2.8 19.1 %collective-permute-start = (bf16[112,384]{1,0:T(8,128)(2,1)S(1)}, bf16[112,384]{1,0:T(8,128)(2,1)S(1)}, u32[]{:S(2)}, u32[]{:S(2)}) collective-permute-start(bf16[112,384]{1,0:T(8,128)(2,1)S(1)} %make_unit.1.refs_0_), channel_id=1, source_target_pairs={{0,16},{16,0},{32,48},{48,32},{64,80},{80,64},{96,112},{112,96},{1... | collective-permute-start | bytes 258056 | tf_op jit(solution)/shard_map/ppermute | solution.py:33
  20.0 12.1 %collective-permute-start.2 = (bf16[2,96,256]{2,1,0:T(8,128)(2,1)S(1)}, bf16[2,96,256]{2,1,0:T(8,128)(2,1)S(1)}, u32[]{:S(2)}, u32[]{:S(2)}) collective-permute-start(bf16[2,96,256]{2,1,0:T(8,128)(2,1)S(1)} %fusion), channel_id=1, source_target_pairs={{0,16},{16,0},{32,48},{48,32},{64,80},{80,64},{96,112},{112,96},{1... | collective-permute-start | bytes 294920 | tf_op jit(solution)/shard_map/ppermute | solution.py:33
  22.0 20.9 %collective-permute-start.1 = (bf16[224,384]{1,0:T(8,128)(2,1)S(1)}, bf16[224,384]{1,0:T(8,128)(2,1)S(1)}, u32[]{:S(2)}, u32[]{:S(2)}) collective-permute-start(bf16[224,384]{1,0:T(8,128)(2,1)S(1)} %pad_maximum_fusion.1), channel_id=1, source_target_pairs={{0,256},{16,784},{32,288},{48,816},{64,320},{80,848},{96,352},{112... | collective-permute-start | bytes 516104 | tf_op jit(solution)/shard_map/ppermute | solution.py:29
  32.1 12.7 %collective-permute-start.3 = (bf16[192,512]{1,0:T(8,128)(2,1)S(1)}, bf16[192,512]{1,0:T(8,128)(2,1)S(1)}, u32[]{:S(2)}, u32[]{:S(2)}) collective-permute-start(bf16[192,512]{1,0:T(8,128)(2,1)S(1)} %bitcast.36), channel_id=1, source_target_pairs={{0,4},{1,5},{2,6},{3,7},{4,8},{5,9},{6,10},{7,11},{8,12},{9,13},{1... | collective-permute-start | bytes 589832 | tf_op jit(solution)/shard_map/ppermute | solution.py:47
  35.3 9.5 %collective-permute-start.4 = (bf16[192,512]{1,0:T(8,128)(2,1)S(1)}, bf16[192,512]{1,0:T(8,128)(2,1)S(1)}, u32[]{:S(2)}, u32[]{:S(2)}) collective-permute-start(bf16[192,512]{1,0:T(8,128)(2,1)S(1)} %bitcast.37), channel_id=1, source_target_pairs={{0,8},{1,9},{2,10},{3,11},{4,12},{5,13},{6,14},{7,15},{8,0},{9,1},... | collective-permute-start | bytes 589832 | tf_op jit(solution)/shard_map/ppermute | solution.py:47
  39.9 6.4 %collective-permute-start.5 = (bf16[192,512]{1,0:T(8,128)(2,1)S(1)}, bf16[192,512]{1,0:T(8,128)(2,1)S(1)}, u32[]{:S(2)}, u32[]{:S(2)}) collective-permute-start(bf16[192,512]{1,0:T(8,128)(2,1)S(1)} %bitcast.38), channel_id=1, source_target_pairs={{0,12},{1,13},{2,14},{3,15},{4,0},{5,1},{6,2},{7,3},{8,4},{9,5},{1... | collective-permute-start | bytes 589832 | tf_op jit(solution)/shard_map/ppermute | solution.py:47
  42.9 18.8 %collective-permute-start.6 = (bf16[112,384]{1,0:T(8,128)(2,1)S(1)}, bf16[112,384]{1,0:T(8,128)(2,1)S(1)}, u32[]{:S(2)}, u32[]{:S(2)}) collective-permute-start(bf16[112,384]{1,0:T(8,128)(2,1)S(1)} %get-tuple-element.51), channel_id=1, source_target_pairs={{0,16},{16,0},{32,48},{48,32},{64,80},{80,64},{96,112},{112,96},{1... | collective-permute-start | bytes 258056 | tf_op jit(solution)/shard_map/ppermute | solution.py:33
  46.3 16.9 %collective-permute-start.7 = (bf16[112,384]{1,0:T(8,128)(2,1)S(1)}, bf16[112,384]{1,0:T(8,128)(2,1)S(1)}, u32[]{:S(2)}, u32[]{:S(2)}) collective-permute-start(bf16[112,384]{1,0:T(8,128)(2,1)S(1)} %get-tuple-element.28.refs_3_), channel_id=1, source_target_pairs={{0,256},{16,784},{32,288},{48,816},{64,320},{80,848},{96,352},{112... | collective-permute-start | bytes 258056 | tf_op jit(solution)/shard_map/ppermute | solution.py:29
  63.3 13.6 %collective-permute-start.8 = (bf16[400,384]{1,0:T(8,128)(2,1)S(1)}, bf16[400,384]{1,0:T(8,128)(2,1)S(1)}, u32[]{:S(2)}, u32[]{:S(2)}) collective-permute-start(bf16[400,384]{1,0:T(8,128)(2,1)S(1)} %join_units.1.refs_4_), channel_id=1, source_target_pairs={{0,32},{16,1008},{32,64},{48,16},{64,96},{80,48},{96,128},{112,80}... | collective-permute-start | bytes 921608 | tf_op jit(solution)/shard_map/ppermute | solution.py:29
  72.5 10.5 %collective-permute-start.15 = (bf16[400,384]{1,0:T(8,128)(2,1)S(1)}, bf16[400,384]{1,0:T(8,128)(2,1)}, u32[]{:S(2)}, u32[]{:S(2)}) collective-permute-start(bf16[400,384]{1,0:T(8,128)(2,1)S(1)} %join_units.1.refs_4_), channel_id=1, source_target_pairs={{0,992},{16,48},{32,0},{48,80},{64,32},{80,112},{96,64},{112,144},... | collective-permute-start | bytes 921608 | tf_op jit(solution)/shard_map/ppermute | solution.py:29
  76.9 14.8 %collective-permute-start.11 = (bf16[400,384]{1,0:T(8,128)(2,1)S(1)}, bf16[400,384]{1,0:T(8,128)(2,1)}, u32[]{:S(2)}, u32[]{:S(2)}) collective-permute-start(bf16[400,384]{1,0:T(8,128)(2,1)S(1)} %collective-permute-done.8.refs_5_), channel_id=1, source_target_pairs={{0,32},{16,1008},{32,64},{48,16},{64,96},{80,48},{96,128},{112,80}... | collective-permute-start | bytes 921608 | tf_op jit(solution)/shard_map/ppermute | solution.py:29
  83.0 17.5 %collective-permute-start.16 = (bf16[400,384]{1,0:T(8,128)(2,1)}, bf16[400,384]{1,0:T(8,128)(2,1)}, u32[]{:S(2)}, u32[]{:S(2)}) collective-permute-start(bf16[400,384]{1,0:T(8,128)(2,1)} %collective-permute-done.15.refs_6_), channel_id=1, source_target_pairs={{0,992},{16,48},{32,0},{48,80},{64,32},{80,112},{96,64},{112,144},... | collective-permute-start | bytes 921608 | tf_op jit(solution)/shard_map/ppermute | solution.py:29
  84.9 30.7 %collective-permute-start.10 = (bf16[768,512]{1,0:T(8,128)(2,1)S(1)}, bf16[768,512]{1,0:T(8,128)(2,1)S(1)}, u32[]{:S(2)}, u32[]{:S(2)}) collective-permute-start(bf16[768,512]{1,0:T(8,128)(2,1)S(1)} %stack.1.refs_0_), channel_id=1, source_target_pairs={{0,2},{1,3},{2,0},{3,1},{4,6},{5,7},{6,4},{7,5},{8,10},{9,11},{10,... | collective-permute-start | bytes 2359304 | tf_op jit(solution)/shard_map/ppermute | solution.py:47
  89.4 26.3 %collective-permute-start.9 = (bf16[768,512]{1,0:T(8,128)(2,1)S(1)}, bf16[768,512]{1,0:T(8,128)(2,1)S(1)}, u32[]{:S(2)}, u32[]{:S(2)}) collective-permute-start(bf16[768,512]{1,0:T(8,128)(2,1)S(1)} %stack.1.refs_0_), channel_id=1, source_target_pairs={{0,1},{1,2},{2,3},{3,0},{4,5},{5,6},{6,7},{7,4},{8,9},{9,10},{10,1... | collective-permute-start | bytes 2359304 | tf_op jit(solution)/shard_map/ppermute | solution.py:47
  91.7 24.0 %collective-permute-start.12 = (bf16[768,512]{1,0:T(8,128)(2,1)S(1)}, bf16[768,512]{1,0:T(8,128)(2,1)S(1)}, u32[]{:S(2)}, u32[]{:S(2)}) collective-permute-start(bf16[768,512]{1,0:T(8,128)(2,1)S(1)} %stack.1.refs_0_), channel_id=1, source_target_pairs={{0,3},{1,0},{2,1},{3,2},{4,7},{5,4},{6,5},{7,6},{8,11},{9,8},{10,9... | collective-permute-start | bytes 2359304 | tf_op jit(solution)/shard_map/ppermute | solution.py:47
  96.0 8.7 %collective-permute-start.13 = (bf16[400,384]{1,0:T(8,128)(2,1)}, bf16[400,384]{1,0:T(8,128)(2,1)}, u32[]{:S(2)}, u32[]{:S(2)}) collective-permute-start(bf16[400,384]{1,0:T(8,128)(2,1)} %collective-permute-done.11.refs_7_), channel_id=1, source_target_pairs={{0,32},{16,1008},{32,64},{48,16},{64,96},{80,48},{96,128},{112,80}... | collective-permute-start | bytes 921608 | tf_op jit(solution)/shard_map/ppermute | solution.py:29
  100.6 12.2 %collective-permute-start.17 = (bf16[400,384]{1,0:T(8,128)(2,1)}, bf16[400,384]{1,0:T(8,128)(2,1)}, u32[]{:S(2)}, u32[]{:S(2)}) collective-permute-start(bf16[400,384]{1,0:T(8,128)(2,1)} %collective-permute-done.16.refs_8_), channel_id=1, source_target_pairs={{0,992},{16,48},{32,0},{48,80},{64,32},{80,112},{96,64},{112,144},... | collective-permute-start | bytes 921608 | tf_op jit(solution)/shard_map/ppermute | solution.py:29
  102.6 13.1 %copy-start.3 = (bf16[400,384]{1,0:T(8,128)(2,1)S(1)}, bf16[400,384]{1,0:T(8,128)(2,1)}, u32[]{:S(2)}) copy-start(bf16[400,384]{1,0:T(8,128)(2,1)} %copy-done.2) | copy-start | bytes 921604
  105.6 14.9 %collective-permute-start.14 = (bf16[208,384]{1,0:T(8,128)(2,1)S(1)}, bf16[208,384]{1,0:T(8,128)(2,1)S(1)}, u32[]{:S(2)}, u32[]{:S(2)}) collective-permute-start(bf16[208,384]{1,0:T(8,128)(2,1)S(1)} %slice.24), channel_id=1, source_target_pairs={{0,32},{16,1008},{32,64},{48,16},{64,96},{80,48},{96,128},{112,80}... | collective-permute-start | bytes 479240 | tf_op jit(solution)/shard_map/ppermute | solution.py:29
  113.7 8.4 %collective-permute-start.18 = (bf16[208,384]{1,0:T(8,128)(2,1)S(1)}, bf16[208,384]{1,0:T(8,128)(2,1)S(1)}, u32[]{:S(2)}, u32[]{:S(2)}) collective-permute-start(bf16[208,384]{1,0:T(8,128)(2,1)S(1)} %slice.30), channel_id=1, source_target_pairs={{0,992},{16,48},{32,0},{48,80},{64,32},{80,112},{96,64},{112,144},... | collective-permute-start | bytes 479240 | tf_op jit(solution)/shard_map/ppermute | solution.py:29
  122.1 8.0 %copy-start = (bf16[256,384]{1,0:T(8,128)(2,1)S(1)}, bf16[256,384]{1,0:T(8,128)(2,1)}, u32[]{:S(2)}) copy-start(bf16[256,384]{1,0:T(8,128)(2,1)} %q_ref.3) | copy-start | bytes 589828
  122.1 8.0 %copy-start.1 = (bf16[256,384]{1,0:T(8,128)(2,1)S(1)}, bf16[256,384]{1,0:T(8,128)(2,1)}, u32[]{:S(2)}) copy-start(bf16[256,384]{1,0:T(8,128)(2,1)} %k_ref.3) | copy-start | bytes 589828
  123.4 6.8 %copy-start.6 = (f32[32]{0:T(128)S(1)}, f32[32]{0:T(128)}, u32[]{:S(2)}) copy-start(f32[32]{0:T(128)} %param.16) | copy-start | bytes 388
  123.4 8.1 %collective-permute-start.19 = (f32[264,384]{1,0:T(8,128)S(1)}, f32[264,384]{1,0:T(8,128)S(1)}, u32[]{:S(2)}, u32[]{:S(2)}) collective-permute-start(f32[264,384]{1,0:T(8,128)S(1)} %get-tuple-element.37), channel_id=1, source_target_pairs={{0,16},{16,0},{32,48},{48,32},{64,80},{80,64},{96,112},{112,96},{1... | collective-permute-start | bytes 1216520 | tf_op jit(solution)/shard_map/ppermute | solution.py:33
  (5 other events, 16.0 us)

commit v4 on v3

--- a/solution.py
+++ b/solution.py
@@ -33,47 +33,44 @@
     return lax.ppermute(x, "dp", [(i, i ^ 1) for i in range(2 * pairs_z)])
 
 
-def in_plane(x, step, first_axis, pairs_z):
+def exchange(x, flip, first_axis, pairs_z):
     pairs = []
     for d in range(2 * pairs_z):
         on_x = (d % 2 == 0) == first_axis
         for m in range(SIDE * SIDE):
             i, j = divmod(m, SIDE)
-            if on_x:
-                i = (i + step) % SIDE
-            else:
-                j = (j + step) % SIDE
-            pairs.append((d * SIDE * SIDE + m, d * SIDE * SIDE + i * SIDE + j))
+            to = (i ^ flip) * SIDE + j if on_x else i * SIDE + (j ^ flip)
+            pairs.append((d * SIDE * SIDE + m, d * SIDE * SIDE + to))
     return lax.ppermute(x, ALL, pairs)
 
 
-def ring_of_four(block, first_axis, pairs_z):
-    return [block] + [in_plane(block, step, first_axis, pairs_z) for step in (1, 2, -1)]
-
-
-def gather(unit, other, block, first, pairs_z):
-    chip = jnp.concatenate([jnp.where(first, unit, other), jnp.where(first, other, unit)])
-    got = along_z(chip, FAR, -FAR, pairs_z)
-    rows = unit.shape[0]
-    got0, got1 = got[:rows], got[rows:]
-    mine = jnp.where(first, got0, got1)
-    row = ring_of_four(block, True, pairs_z)
-    mine, *row = lax.optimization_barrier((mine, *row))
+def gather(unit, block, pairs_z):
+    tie = lax.optimization_barrier
+    mine = along_z(unit, FAR, -FAR, pairs_z)
+    opposite = along_z(unit, -FAR, FAR, pairs_z)
+    mine, opposite = meet(3300000000, mine, opposite)
+    mine, opposite, block = tie((mine, opposite, block))
+    passed = exchange(block, 1, True, pairs_z)
     farthest = along_z(mine, FAR, -FAR, pairs_z)
-    opposite = to_sibling(jnp.where(first, got1, got0), pairs_z)
+    (farthest,) = meet(3300000000, farthest)
+    farthest, passed = tie((farthest, passed))
+    block = stack([block, passed])
     bundle = join_units(unit, opposite, farthest, mine)
-    row = stack(row)
-    pieces, features = [bundle], [row]
+    pieces = [bundle]
     p = q = bundle
-    for step in (2, 1, -1):
-        features.append(in_plane(row, step, False, pairs_z))
+    for step, cost in enumerate((3300000000, 8800000000, 22000000000)):
         p = along_z(p, 1, -1, pairs_z)
         q = along_z(q, -1, 1, pairs_z)
-        row, p = lax.optimization_barrier((row, p))
+        passed = exchange(block, (3, 1, 3)[step], step == 0, pairs_z)
+        p, q = meet(cost, p, q)
+        if step < 2:
+            p, q, passed = tie((p, q, passed))
+            block = stack([block, passed])
         pieces += [p, q]
+    half = passed
     p = along_z(p[:HALF], 1, -1, pairs_z)
     q = along_z(q[UNIT : UNIT + HALF], -1, 1, pairs_z)
-    return pieces + [p, q], [features[i] for i in (0, 2, 1, 3)]
+    return pieces + [p, q], [block, half]
 
 
 def piece_offsets():
@@ -112,6 +109,12 @@
 
 def row_of(i):
     return i * UNIT + (TAIL if i >= 2 else 0)
+
+
+def copy_kernel(*refs):
+    half = len(refs) // 2
+    for given, out in zip(refs[:half], refs[half:]):
+        out[...] = given[...]
 
 
 def stack_kernel(*refs):
@@ -152,7 +155,7 @@
 
 
 def first_kernel(starts, outers, *refs):
-    blocks, pieces, (acc_ref, stats_ref, xs_ref) = refs[:4], refs[4:-3], refs[-3:]
+    blocks, pieces, (acc_ref, stats_ref, xs_ref) = refs[:2], refs[2:-3], refs[-3:]
     xs_ref[pl.ds(2 * UNIT, TAIL), :] = jnp.zeros((TAIL, xs_ref.shape[1]), xs_ref.dtype)
     stats_ref[...] = jnp.zeros_like(stats_ref)
     for i, piece in enumerate(pieces):
@@ -167,7 +170,7 @@
 
 
 def last_kernel(starts, outers, core, *refs):
-    blocks, (p_ref, q_ref, acc_ref, stats_ref, mine_ref, send_ref, xs_ref, w_ref, sum_ref) = refs[:4], refs[4:]
+    blocks, (p_ref, q_ref, acc_ref, stats_ref, mine_ref, send_ref, xs_ref, w_ref, sum_ref) = refs[:2], refs[2:]
     for k, at in enumerate((0, UNIT, HALF, HALF + UNIT + TAIL)):
         pick_rows(starts, outers, 28 + k, blocks, xs_ref, at)
     for at in (2 * UNIT, HALF + UNIT):
@@ -247,6 +250,11 @@
     return call(join_kernel, "join_units", shape, units)
 
 
+def meet(flops, *arrays):
+    shapes = tuple(jax.ShapeDtypeStruct(a.shape, a.dtype) for a in arrays)
+    return call(copy_kernel, "meet", shapes, arrays, flops=flops)
+
+
 def stack(blocks):
     rows, width = blocks[0].shape
     shape = jax.ShapeDtypeStruct((len(blocks) * rows, width), blocks[0].dtype)
@@ -271,7 +279,6 @@
         2,
         moved=2**17,
     )
-    other = to_sibling(unit, pairs_z)
 
     turned = cotangent.T.reshape(2, 2, UNIT, PATCHES)
     keep = jnp.where(first, turned[:, 0], turned[:, 1])
@@ -279,14 +286,16 @@
     got = to_sibling(give, pairs_z)
     block = jnp.concatenate([jnp.where(first, keep, got), jnp.where(first, got, keep)], axis=2)
     block = block.reshape(2 * UNIT, 2 * PATCHES)
-    pieces, features = gather(unit, other, block, first, pairs_z)
+    pieces, features = gather(unit, block, pairs_z)
 
     offsets = jnp.array([o for piece in piece_offsets() for o in piece], jnp.int32)
     source = (z + jnp.where(first, offsets, -offsets)) % pairs_z
-    from_x, from_y = (at_x - source // 2 // SIDE) % SIDE, (at_y - source // 2 % SIDE) % SIDE
+    from_x, from_y = at_x ^ (source // 2 // SIDE), at_y ^ (source // 2 % SIDE)
     inner = jnp.where(first, from_x, from_y)
     outer = jnp.where(first, from_y, from_x)
-    starts = (inner * 2 + source % 2) * UNIT
+    inner, outer = inner ^ (inner >> 1), outer ^ (outer >> 1)
+    starts = ((outer % 2 * SIDE + inner) * 2 + source % 2) * UNIT
+    outer = outer // 2
 
     total = jax.ShapeDtypeStruct((2 * PATCHES, heads), f32)
     summed, stats = call(

time: 134 us -> 144 us (1.075)
  waiting for transfers between devices: 12 us -> 40.5 us
  starting transfers between devices: 106 us -> 87.9 us
    ppermute x10 -> x11, waiting for transfers between devices: 9.61 us -> 26.9 us  [along_z(): return lax.ppermute(x, 'dp', pairs)]
    ppermute x4 -> x2, starting transfers between devices: 26.7 us -> 15.3 us  [to_sibling(): return lax.ppermute(x, 'dp', [(i, i ^ 1) for i in range(2 * pairs_z)])]
    ppermute x6 -> x4, waiting for transfers between devices: 1.45 us -> 12.7 us  [exchange(): return lax.ppermute(x, ALL, pairs)]
    ppermute x6 -> x4, starting transfers between devices: 21.7 us -> 16 us  [exchange(): return lax.ppermute(x, ALL, pairs)]
    ppermute x10 -> x11, starting transfers between devices: 57.6 us -> 56.6 us  [along_z(): return lax.ppermute(x, 'dp', pairs)]
    pallas_call x7 -> x14, Pallas kernels: 8.61 us -> 8.59 us  [call(): pl.pallas_call(kernel, out_shape=out_shape, in_specs=[SM] * scalars + [VM...]
  transfers between devices with their start and end apart: 20 -> 17, of which waited for: 7 -> 11; matrix products, arithmetic and copies ran while one was open for 2% -> 1% of each run, Pallas kernels for 4% -> 4%
where the time goes in v4:
time: 144 us; the launch traced here: 143 us
  starting transfers between devices  87.9 us (61%)
  waiting for transfers between devices  40.5 us (28%)
  Pallas kernels  8.59 us (6%)
  local copies, waits for them, and re-layouts  3.71 us (3%)
  between operations  2.37 us (2%)
    ppermute x11, starting transfers between devices, along_z(): return lax.ppermute(x, 'dp', pairs)  56.6 us
    ppermute x11, waiting for transfers between devices, along_z(): return lax.ppermute(x, 'dp', pairs)  26.9 us
    ppermute x4, starting transfers between devices, exchange(): return lax.ppermute(x, ALL, pairs)  16 us
    ppermute x2, starting transfers between devices, to_sibling(): return lax.ppermute(x, 'dp', [(i, i ^ 1) for i in range(2 * pairs_z)])  15.3 us
    ppermute x4, waiting for transfers between devices, exchange(): return lax.ppermute(x, ALL, pairs)  12.7 us
    pallas_call x14, Pallas kernels, call(): pl.pallas_call(kernel, out_shape=out_shape, in_specs=[SM] * scalars + [VM...  8.59 us
    unnamed x19, local copies, waits for them, and re-layouts  3.67 us
  transfers between devices with their start and end apart: 17, of which 11 were waited for; matrix products, arithmetic and copies ran while one was open for 1% of the time, Pallas kernels for 4%

profile of v4, /device:TPU:1, one launch (start us, length us, event | category | flops | bytes accessed | tf_op | source)
XLA Modules:
  0.0 143.2 jit_solution(12460376132672005268)
XLA Ops:
  2.8 23.5 %collective-permute-start = (bf16[112,384]{1,0:T(8,128)(2,1)S(1)}, bf16[112,384]{1,0:T(8,128)(2,1)S(1)}, u32[]{:S(2)}, u32[]{:S(2)}) collective-permute-start(bf16[112,384]{1,0:T(8,128)(2,1)S(1)} %make_unit.1.refs_0_), channel_id=1, source_target_pairs={{0,256},{16,784},{32,288},{48,816},{64,320},{80,848},{96,352},{112... | collective-permute-start | bytes 258056 | tf_op jit(solution)/shard_map/ppermute | solution.py:29
  29.4 5.2 %collective-permute-start.2 = (bf16[2,96,256]{2,1,0:T(8,128)(2,1)S(1)}, bf16[2,96,256]{2,1,0:T(8,128)(2,1)S(1)}, u32[]{:S(2)}, u32[]{:S(2)}) collective-permute-start(bf16[2,96,256]{2,1,0:T(8,128)(2,1)S(1)} %fusion), channel_id=1, source_target_pairs={{0,16},{16,0},{32,48},{48,32},{64,80},{80,64},{96,112},{112,96},{1... | collective-permute-start | bytes 294920 | tf_op jit(solution)/shard_map/ppermute | solution.py:33
  34.6 2.1 %collective-permute-done.refs_0_ = bf16[112,384]{1,0:T(8,128)(2,1)S(1)} collective-permute-done((bf16[112,384]{1,0:T(8,128)(2,1)S(1)}, bf16[112,384]{1,0:T(8,128)(2,1)S(1)}, u32[]{:S(2)}, u32[]{:S(2)}) %collective-permute-start) | collective-permute-done | bytes 86048 | tf_op jit(solution)/shard_map/ppermute | solution.py:29
  36.7 8.8 %collective-permute-done.1.refs_1_ = bf16[112,384]{1,0:T(8,128)(2,1)S(1)} collective-permute-done((bf16[112,384]{1,0:T(8,128)(2,1)S(1)}, bf16[112,384]{1,0:T(8,128)(2,1)S(1)}, u32[]{:S(2)}, u32[]{:S(2)}) %collective-permute-start.1) | collective-permute-done | bytes 86048 | tf_op jit(solution)/shard_map/ppermute | solution.py:29
  45.5 8.0 %collective-permute-start.3 = (bf16[112,384]{1,0:T(8,128)(2,1)S(1)}, bf16[112,384]{1,0:T(8,128)(2,1)S(1)}, u32[]{:S(2)}, u32[]{:S(2)}) collective-permute-start(bf16[112,384]{1,0:T(8,128)(2,1)S(1)} %get-tuple-element.36.refs_3_), channel_id=1, source_target_pairs={{0,256},{16,784},{32,288},{48,816},{64,320},{80,848},{96,352},{112... | collective-permute-start | bytes 258056 | tf_op jit(solution)/shard_map/ppermute | solution.py:29
  53.5 4.0 %collective-permute-start.4 = (bf16[192,512]{1,0:T(8,128)(2,1)S(1)}, bf16[192,512]{1,0:T(8,128)(2,1)S(1)}, u32[]{:S(2)}, u32[]{:S(2)}) collective-permute-start(bf16[192,512]{1,0:T(8,128)(2,1)S(1)} %bitcast.36), channel_id=1, source_target_pairs={{0,4},{1,5},{2,6},{3,7},{4,0},{5,1},{6,2},{7,3},{8,12},{9,13},{10,... | collective-permute-start | bytes 589832 | tf_op jit(solution)/shard_map/ppermute | solution.py:44
  57.5 2.2 %collective-permute-done.3.refs_0_ = bf16[112,384]{1,0:T(8,128)(2,1)S(1)} collective-permute-done((bf16[112,384]{1,0:T(8,128)(2,1)S(1)}, bf16[112,384]{1,0:T(8,128)(2,1)S(1)}, u32[]{:S(2)}, u32[]{:S(2)}) %collective-permute-start.3) | collective-permute-done | bytes 86048 | tf_op jit(solution)/shard_map/ppermute | solution.py:29
  60.9 2.9 %collective-permute-start.5 = (bf16[400,384]{1,0:T(8,128)(2,1)S(1)}, bf16[400,384]{1,0:T(8,128)(2,1)S(1)}, u32[]{:S(2)}, u32[]{:S(2)}) collective-permute-start(bf16[400,384]{1,0:T(8,128)(2,1)S(1)} %join_units.1.refs_2_), channel_id=1, source_target_pairs={{0,32},{16,1008},{32,64},{48,16},{64,96},{80,48},{96,128},{112,80}... | collective-permute-start | bytes 921608 | tf_op jit(solution)/shard_map/ppermute | solution.py:29
  63.8 2.4 %collective-permute-start.6 = (bf16[400,384]{1,0:T(8,128)(2,1)S(1)}, bf16[400,384]{1,0:T(8,128)(2,1)S(1)}, u32[]{:S(2)}, u32[]{:S(2)}) collective-permute-start(bf16[400,384]{1,0:T(8,128)(2,1)S(1)} %join_units.1.refs_2_), channel_id=1, source_target_pairs={{0,992},{16,48},{32,0},{48,80},{64,32},{80,112},{96,64},{112,144},... | collective-permute-start | bytes 921608 | tf_op jit(solution)/shard_map/ppermute | solution.py:29
  66.2 4.8 %collective-permute-start.7 = (bf16[384,512]{1,0:T(8,128)(2,1)S(1)}, bf16[384,512]{1,0:T(8,128)(2,1)S(1)}, u32[]{:S(2)}, u32[]{:S(2)}) collective-permute-start(bf16[384,512]{1,0:T(8,128)(2,1)S(1)} %stack.3.refs_0_), channel_id=1, source_target_pairs={{0,12},{1,13},{2,14},{3,15},{4,8},{5,9},{6,10},{7,11},{8,4},{9,5},... | collective-permute-start | bytes 1179656 | tf_op jit(solution)/shard_map/ppermute | solution.py:44
  71.0 4.9 %collective-permute-done.6.refs_1_ = bf16[400,384]{1,0:T(8,128)(2,1)S(1)} collective-permute-done((bf16[400,384]{1,0:T(8,128)(2,1)S(1)}, bf16[400,384]{1,0:T(8,128)(2,1)S(1)}, u32[]{:S(2)}, u32[]{:S(2)}) %collective-permute-start.6) | collective-permute-done | bytes 307232 | tf_op jit(solution)/shard_map/ppermute | solution.py:29
  76.2 4.2 %collective-permute-start.8 = (bf16[400,384]{1,0:T(8,128)(2,1)S(1)}, bf16[400,384]{1,0:T(8,128)(2,1)S(1)}, u32[]{:S(2)}, u32[]{:S(2)}) collective-permute-start(bf16[400,384]{1,0:T(8,128)(2,1)S(1)} %get-tuple-element.43.refs_3_), channel_id=1, source_target_pairs={{0,32},{16,1008},{32,64},{48,16},{64,96},{80,48},{96,128},{112,80}... | collective-permute-start | bytes 921608 | tf_op jit(solution)/shard_map/ppermute | solution.py:29
  80.4 2.3 %collective-permute-start.9 = (bf16[400,384]{1,0:T(8,128)(2,1)S(1)}, bf16[400,384]{1,0:T(8,128)(2,1)S(1)}, u32[]{:S(2)}, u32[]{:S(2)}) collective-permute-start(bf16[400,384]{1,0:T(8,128)(2,1)S(1)} %get-tuple-element.44.refs_4_), channel_id=1, source_target_pairs={{0,992},{16,48},{32,0},{48,80},{64,32},{80,112},{96,64},{112,144},... | collective-permute-start | bytes 921608 | tf_op jit(solution)/shard_map/ppermute | solution.py:29
  82.8 2.8 %collective-permute-start.10 = (bf16[768,512]{1,0:T(8,128)(2,1)S(1)}, bf16[768,512]{1,0:T(8,128)(2,1)S(1)}, u32[]{:S(2)}, u32[]{:S(2)}) collective-permute-start(bf16[768,512]{1,0:T(8,128)(2,1)S(1)} %stack.4.refs_0_), channel_id=1, source_target_pairs={{0,1},{1,0},{2,3},{3,2},{4,5},{5,4},{6,7},{7,6},{8,9},{9,8},{10,11... | collective-permute-start | bytes 2359304 | tf_op jit(solution)/shard_map/ppermute | solution.py:44
  85.6 5.8 %collective-permute-done.9.refs_1_ = bf16[400,384]{1,0:T(8,128)(2,1)S(1)} collective-permute-done((bf16[400,384]{1,0:T(8,128)(2,1)S(1)}, bf16[400,384]{1,0:T(8,128)(2,1)S(1)}, u32[]{:S(2)}, u32[]{:S(2)}) %collective-permute-start.9) | collective-permute-done | bytes 307232 | tf_op jit(solution)/shard_map/ppermute | solution.py:29
  93.2 2.6 %collective-permute-done.10.refs_1_ = bf16[768,512]{1,0:T(8,128)(2,1)S(1)} collective-permute-done((bf16[768,512]{1,0:T(8,128)(2,1)S(1)}, bf16[768,512]{1,0:T(8,128)(2,1)S(1)}, u32[]{:S(2)}, u32[]{:S(2)}) %collective-permute-start.10) | collective-permute-done | bytes 786464 | tf_op jit(solution)/shard_map/ppermute | solution.py:44
  95.8 4.2 %collective-permute-start.12 = (bf16[400,384]{1,0:T(8,128)(2,1)S(1)}, bf16[400,384]{1,0:T(8,128)(2,1)S(1)}, u32[]{:S(2)}, u32[]{:S(2)}) collective-permute-start(bf16[400,384]{1,0:T(8,128)(2,1)S(1)} %get-tuple-element.48.refs_5_), channel_id=1, source_target_pairs={{0,32},{16,1008},{32,64},{48,16},{64,96},{80,48},{96,128},{112,80}... | collective-permute-start | bytes 921608 | tf_op jit(solution)/shard_map/ppermute | solution.py:29
  102.1 4.4 %collective-permute-start.11 = (bf16[1536,512]{1,0:T(8,128)(2,1)S(1)}, bf16[1536,512]{1,0:T(8,128)(2,1)S(1)}, u32[]{:S(2)}, u32[]{:S(2)}) collective-permute-start(bf16[1536,512]{1,0:T(8,128)(2,1)S(1)} %stack.5.refs_0_), channel_id=1, source_target_pairs={{0,3},{1,2},{2,1},{3,0},{4,7},{5,6},{6,5},{7,4},{8,11},{9,10},{10,... | collective-permute-start | bytes 4718600 | tf_op jit(solution)/shard_map/ppermute | solution.py:44
  106.5 3.1 %collective-permute-done.13.refs_1_ = bf16[400,384]{1,0:T(8,128)(2,1)} collective-permute-done((bf16[400,384]{1,0:T(8,128)(2,1)S(1)}, bf16[400,384]{1,0:T(8,128)(2,1)}, u32[]{:S(2)}, u32[]{:S(2)}) %collective-permute-start.13) | collective-permute-done | bytes 307232 | tf_op jit(solution)/shard_map/ppermute | solution.py:29
  112.6 3.4 %collective-permute-start.15 = (bf16[208,384]{1,0:T(8,128)(2,1)S(1)}, bf16[208,384]{1,0:T(8,128)(2,1)S(1)}, u32[]{:S(2)}, u32[]{:S(2)}) collective-permute-start(bf16[208,384]{1,0:T(8,128)(2,1)S(1)} %slice.17), channel_id=1, source_target_pairs={{0,992},{16,48},{32,0},{48,80},{64,32},{80,112},{96,64},{112,144},... | collective-permute-start | bytes 479240 | tf_op jit(solution)/shard_map/ppermute | solution.py:29
  116.0 8.8 %collective-permute-done.11.refs_1_ = bf16[1536,512]{1,0:T(8,128)(2,1)S(1)} collective-permute-done((bf16[1536,512]{1,0:T(8,128)(2,1)S(1)}, bf16[1536,512]{1,0:T(8,128)(2,1)S(1)}, u32[]{:S(2)}, u32[]{:S(2)}) %collective-permute-start.11) | collective-permute-done | bytes 1572896 | tf_op jit(solution)/shard_map/ppermute | solution.py:44
  124.8 3.5 %project_first.1 = (f32[512,384]{1,0:T(8,128)S(1)}, f32[16,384]{1,0:T(8,128)S(1)}) custom-call(s32[32]{0:T(128)S(1)} %fusion.8.starts, s32[32]{0:T(128)S(1)} %get-tuple-element.62.outers, bf16[1536,512]{1,0:T(8,128)(2,1)S(1)} %stack.5.refs_0_, bf16[1536,512]{1,0:T(8,128)(2,1)S(1)} %collective-permute-done.11.refs_1_, ...), custom_call_target="tpu_custom_call" | custom-call | flops 1056964608 | bytes 6291456 | tf_op jit(solution)/shard_map/project_first/pallas_call | solution.py:236
  129.5 10.1 %collective-permute-start.16 = (f32[264,384]{1,0:T(8,128)S(1)}, f32[264,384]{1,0:T(8,128)S(1)}, u32[]{:S(2)}, u32[]{:S(2)}) collective-permute-start(f32[264,384]{1,0:T(8,128)S(1)} %get-tuple-element.55), channel_id=1, source_target_pairs={{0,16},{16,0},{32,48},{48,32},{64,80},{80,64},{96,112},{112,96},{1... | collective-permute-start | bytes 1216520 | tf_op jit(solution)/shard_map/ppermute | solution.py:33
  141.0 2.2 %attention.1 = (bf16[256,384]{1,0:T(8,128)(2,1)}, bf16[256,384]{1,0:T(8,128)(2,1)}, bf16[256,384]{1,0:T(8,128)(2,1)}, f32[1,32]{1,0:T(1,128)}) custom-call(s32[1]{0:T(128)S(6)} %copy.22.group, f32[264,384]{1,0:T(8,128)S(1)} %get-tuple-element.54.mine_ref, f32[264,384]{1,0:T(8,128)S(1)} %collective-permute-done.16.got_ref, ...), custom_call_target="tpu_custom_call" | custom-call | flops 201326592 | bytes 3145728 | tf_op jit(solution)/shard_map/attention/pallas_call | solution.py:236
  (51 shorter events, 14.8 us)
Async XLA Ops:
  2.8 33.8 %collective-permute-start = (bf16[112,384]{1,0:T(8,128)(2,1)S(1)}, bf16[112,384]{1,0:T(8,128)(2,1)S(1)}, u32[]{:S(2)}, u32[]{:S(2)}) collective-permute-start(bf16[112,384]{1,0:T(8,128)(2,1)S(1)} %make_unit.1.refs_0_), channel_id=1, source_target_pairs={{0,256},{16,784},{32,288},{48,816},{64,320},{80,848},{96,352},{112... | collective-permute-start | bytes 258056 | tf_op jit(solution)/shard_map/ppermute | solution.py:29
  26.4 19.0 %collective-permute-start.1 = (bf16[112,384]{1,0:T(8,128)(2,1)S(1)}, bf16[112,384]{1,0:T(8,128)(2,1)S(1)}, u32[]{:S(2)}, u32[]{:S(2)}) collective-permute-start(bf16[112,384]{1,0:T(8,128)(2,1)S(1)} %make_unit.1.refs_0_), channel_id=1, source_target_pairs={{0,768},{16,272},{32,800},{48,304},{64,832},{80,336},{96,864},{112... | collective-permute-start | bytes 258056 | tf_op jit(solution)/shard_map/ppermute | solution.py:29
  29.4 16.0 %collective-permute-start.2 = (bf16[2,96,256]{2,1,0:T(8,128)(2,1)S(1)}, bf16[2,96,256]{2,1,0:T(8,128)(2,1)S(1)}, u32[]{:S(2)}, u32[]{:S(2)}) collective-permute-start(bf16[2,96,256]{2,1,0:T(8,128)(2,1)S(1)} %fusion), channel_id=1, source_target_pairs={{0,16},{16,0},{32,48},{48,32},{64,80},{80,64},{96,112},{112,96},{1... | collective-permute-start | bytes 294920 | tf_op jit(solution)/shard_map/ppermute | solution.py:33
  45.5 14.2 %collective-permute-start.3 = (bf16[112,384]{1,0:T(8,128)(2,1)S(1)}, bf16[112,384]{1,0:T(8,128)(2,1)S(1)}, u32[]{:S(2)}, u32[]{:S(2)}) collective-permute-start(bf16[112,384]{1,0:T(8,128)(2,1)S(1)} %get-tuple-element.36.refs_3_), channel_id=1, source_target_pairs={{0,256},{16,784},{32,288},{48,816},{64,320},{80,848},{96,352},{112... | collective-permute-start | bytes 258056 | tf_op jit(solution)/shard_map/ppermute | solution.py:29
  53.5 7.4 %collective-permute-start.4 = (bf16[192,512]{1,0:T(8,128)(2,1)S(1)}, bf16[192,512]{1,0:T(8,128)(2,1)S(1)}, u32[]{:S(2)}, u32[]{:S(2)}) collective-permute-start(bf16[192,512]{1,0:T(8,128)(2,1)S(1)} %bitcast.36), channel_id=1, source_target_pairs={{0,4},{1,5},{2,6},{3,7},{4,0},{5,1},{6,2},{7,3},{8,12},{9,13},{10,... | collective-permute-start | bytes 589832 | tf_op jit(solution)/shard_map/ppermute | solution.py:44
  60.9 10.1 %collective-permute-start.5 = (bf16[400,384]{1,0:T(8,128)(2,1)S(1)}, bf16[400,384]{1,0:T(8,128)(2,1)S(1)}, u32[]{:S(2)}, u32[]{:S(2)}) collective-permute-start(bf16[400,384]{1,0:T(8,128)(2,1)S(1)} %join_units.1.refs_2_), channel_id=1, source_target_pairs={{0,32},{16,1008},{32,64},{48,16},{64,96},{80,48},{96,128},{112,80}... | collective-permute-start | bytes 921608 | tf_op jit(solution)/shard_map/ppermute | solution.py:29
  63.8 12.1 %collective-permute-start.6 = (bf16[400,384]{1,0:T(8,128)(2,1)S(1)}, bf16[400,384]{1,0:T(8,128)(2,1)S(1)}, u32[]{:S(2)}, u32[]{:S(2)}) collective-permute-start(bf16[400,384]{1,0:T(8,128)(2,1)S(1)} %join_units.1.refs_2_), channel_id=1, source_target_pairs={{0,992},{16,48},{32,0},{48,80},{64,32},{80,112},{96,64},{112,144},... | collective-permute-start | bytes 921608 | tf_op jit(solution)/shard_map/ppermute | solution.py:29
  66.2 10.0 %collective-permute-start.7 = (bf16[384,512]{1,0:T(8,128)(2,1)S(1)}, bf16[384,512]{1,0:T(8,128)(2,1)S(1)}, u32[]{:S(2)}, u32[]{:S(2)}) collective-permute-start(bf16[384,512]{1,0:T(8,128)(2,1)S(1)} %stack.3.refs_0_), channel_id=1, source_target_pairs={{0,12},{1,13},{2,14},{3,15},{4,8},{5,9},{6,10},{7,11},{8,4},{9,5},... | collective-permute-start | bytes 1179656 | tf_op jit(solution)/shard_map/ppermute | solution.py:44
  76.2 9.4 %collective-permute-start.8 = (bf16[400,384]{1,0:T(8,128)(2,1)S(1)}, bf16[400,384]{1,0:T(8,128)(2,1)S(1)}, u32[]{:S(2)}, u32[]{:S(2)}) collective-permute-start(bf16[400,384]{1,0:T(8,128)(2,1)S(1)} %get-tuple-element.43.refs_3_), channel_id=1, source_target_pairs={{0,32},{16,1008},{32,64},{48,16},{64,96},{80,48},{96,128},{112,80}... | collective-permute-start | bytes 921608 | tf_op jit(solution)/shard_map/ppermute | solution.py:29
  80.4 11.1 %collective-permute-start.9 = (bf16[400,384]{1,0:T(8,128)(2,1)S(1)}, bf16[400,384]{1,0:T(8,128)(2,1)S(1)}, u32[]{:S(2)}, u32[]{:S(2)}) collective-permute-start(bf16[400,384]{1,0:T(8,128)(2,1)S(1)} %get-tuple-element.44.refs_4_), channel_id=1, source_target_pairs={{0,992},{16,48},{32,0},{48,80},{64,32},{80,112},{96,64},{112,144},... | collective-permute-start | bytes 921608 | tf_op jit(solution)/shard_map/ppermute | solution.py:29
  82.7 19.2 %copy-start.7 = (s32[32]{0:T(128)S(1)}, s32[32]{0:T(128)}, u32[]{:S(2)}) copy-start(s32[32]{0:T(128)} %constant.113.clone) | copy-start | bytes 388
  82.7 19.2 %copy-start.8 = (s32[32]{0:T(128)S(1)}, s32[32]{0:T(128)}, u32[]{:S(2)}) copy-start(s32[32]{0:T(128)} %constant.117) | copy-start | bytes 388
  82.8 13.0 %collective-permute-start.10 = (bf16[768,512]{1,0:T(8,128)(2,1)S(1)}, bf16[768,512]{1,0:T(8,128)(2,1)S(1)}, u32[]{:S(2)}, u32[]{:S(2)}) collective-permute-start(bf16[768,512]{1,0:T(8,128)(2,1)S(1)} %stack.4.refs_0_), channel_id=1, source_target_pairs={{0,1},{1,0},{2,3},{3,2},{4,5},{5,4},{6,7},{7,6},{8,9},{9,8},{10,11... | collective-permute-start | bytes 2359304 | tf_op jit(solution)/shard_map/ppermute | solution.py:44
  92.2 1.0 copy-start.6
  95.8 10.7 %collective-permute-start.12 = (bf16[400,384]{1,0:T(8,128)(2,1)S(1)}, bf16[400,384]{1,0:T(8,128)(2,1)S(1)}, u32[]{:S(2)}, u32[]{:S(2)}) collective-permute-start(bf16[400,384]{1,0:T(8,128)(2,1)S(1)} %get-tuple-element.48.refs_5_), channel_id=1, source_target_pairs={{0,32},{16,1008},{32,64},{48,16},{64,96},{80,48},{96,128},{112,80}... | collective-permute-start | bytes 921608 | tf_op jit(solution)/shard_map/ppermute | solution.py:29
  100.0 9.6 %collective-permute-start.13 = (bf16[400,384]{1,0:T(8,128)(2,1)S(1)}, bf16[400,384]{1,0:T(8,128)(2,1)}, u32[]{:S(2)}, u32[]{:S(2)}) collective-permute-start(bf16[400,384]{1,0:T(8,128)(2,1)S(1)} %get-tuple-element.49.refs_6_), channel_id=1, source_target_pairs={{0,992},{16,48},{32,0},{48,80},{64,32},{80,112},{96,64},{112,144},... | collective-permute-start | bytes 921608 | tf_op jit(solution)/shard_map/ppermute | solution.py:29
  102.1 22.7 %collective-permute-start.11 = (bf16[1536,512]{1,0:T(8,128)(2,1)S(1)}, bf16[1536,512]{1,0:T(8,128)(2,1)S(1)}, u32[]{:S(2)}, u32[]{:S(2)}) collective-permute-start(bf16[1536,512]{1,0:T(8,128)(2,1)S(1)} %stack.5.refs_0_), channel_id=1, source_target_pairs={{0,3},{1,2},{2,1},{3,0},{4,7},{5,6},{6,5},{7,4},{8,11},{9,10},{10,... | collective-permute-start | bytes 4718600 | tf_op jit(solution)/shard_map/ppermute | solution.py:44
  110.7 17.6 %collective-permute-start.14 = (bf16[208,384]{1,0:T(8,128)(2,1)S(1)}, bf16[208,384]{1,0:T(8,128)(2,1)S(1)}, u32[]{:S(2)}, u32[]{:S(2)}) collective-permute-start(bf16[208,384]{1,0:T(8,128)(2,1)S(1)} %slice.16), channel_id=1, source_target_pairs={{0,32},{16,1008},{32,64},{48,16},{64,96},{80,48},{96,128},{112,80}... | collective-permute-start | bytes 479240 | tf_op jit(solution)/shard_map/ppermute | solution.py:29
  112.6 15.7 %collective-permute-start.15 = (bf16[208,384]{1,0:T(8,128)(2,1)S(1)}, bf16[208,384]{1,0:T(8,128)(2,1)S(1)}, u32[]{:S(2)}, u32[]{:S(2)}) collective-permute-start(bf16[208,384]{1,0:T(8,128)(2,1)S(1)} %slice.17), channel_id=1, source_target_pairs={{0,992},{16,48},{32,0},{48,80},{64,32},{80,112},{96,64},{112,144},... | collective-permute-start | bytes 479240 | tf_op jit(solution)/shard_map/ppermute | solution.py:29
  128.3 11.4 %copy-start = (bf16[256,384]{1,0:T(8,128)(2,1)S(1)}, bf16[256,384]{1,0:T(8,128)(2,1)}, u32[]{:S(2)}) copy-start(bf16[256,384]{1,0:T(8,128)(2,1)} %q_ref.3) | copy-start | bytes 589828
  128.3 11.4 %copy-start.1 = (bf16[256,384]{1,0:T(8,128)(2,1)S(1)}, bf16[256,384]{1,0:T(8,128)(2,1)}, u32[]{:S(2)}) copy-start(bf16[256,384]{1,0:T(8,128)(2,1)} %k_ref.3) | copy-start | bytes 589828
  128.3 11.4 %copy-start.4 = (f32[32]{0:T(128)S(1)}, f32[32]{0:T(128)}, u32[]{:S(2)}) copy-start(f32[32]{0:T(128)} %param.16) | copy-start | bytes 388
  128.3 12.7 %copy-start.2 = (bf16[256,384]{1,0:T(8,128)(2,1)S(1)}, bf16[256,384]{1,0:T(8,128)(2,1)}, u32[]{:S(2)}) copy-start(bf16[256,384]{1,0:T(8,128)(2,1)} %v_ref.1) | copy-start | bytes 589828
  129.5 11.5 %collective-permute-start.16 = (f32[264,384]{1,0:T(8,128)S(1)}, f32[264,384]{1,0:T(8,128)S(1)}, u32[]{:S(2)}, u32[]{:S(2)}) collective-permute-start(f32[264,384]{1,0:T(8,128)S(1)} %get-tuple-element.55), channel_id=1, source_target_pairs={{0,16},{16,0},{32,48},{48,32},{64,80},{80,64},{96,112},{112,96},{1... | collective-permute-start | bytes 1216520 | tf_op jit(solution)/shard_map/ppermute | solution.py:33
  (2 other events, 1.6 us)

commit v5 on v4

--- a/solution.py
+++ b/solution.py
@@ -48,23 +48,24 @@
     tie = lax.optimization_barrier
     mine = along_z(unit, FAR, -FAR, pairs_z)
     opposite = along_z(unit, -FAR, FAR, pairs_z)
-    mine, opposite = meet(3300000000, mine, opposite)
-    mine, opposite, block = tie((mine, opposite, block))
     passed = exchange(block, 1, True, pairs_z)
+    mine, opposite = meet(2, mine, opposite)
     farthest = along_z(mine, FAR, -FAR, pairs_z)
-    (farthest,) = meet(3300000000, farthest)
-    farthest, passed = tie((farthest, passed))
+    block = stack([block, passed])
+    passed = exchange(block, 3, True, pairs_z)
+    (farthest,) = meet(4, farthest)
+    farthest, passed, block = tie((farthest, passed, block))
     block = stack([block, passed])
     bundle = join_units(unit, opposite, farthest, mine)
     pieces = [bundle]
     p = q = bundle
-    for step, cost in enumerate((3300000000, 8800000000, 22000000000)):
+    for step, wait in enumerate((6, 6, 8)):
         p = along_z(p, 1, -1, pairs_z)
         q = along_z(q, -1, 1, pairs_z)
-        passed = exchange(block, (3, 1, 3)[step], step == 0, pairs_z)
-        p, q = meet(cost, p, q)
         if step < 2:
-            p, q, passed = tie((p, q, passed))
+            passed = exchange(block, 1 + 2 * step, False, pairs_z)
+        p, q = meet(wait, p, q)
+        if step == 0:
             block = stack([block, passed])
         pieces += [p, q]
     half = passed
@@ -250,9 +251,20 @@
     return call(join_kernel, "join_units", shape, units)
 
 
-def meet(flops, *arrays):
-    shapes = tuple(jax.ShapeDtypeStruct(a.shape, a.dtype) for a in arrays)
-    return call(copy_kernel, "meet", shapes, arrays, flops=flops)
+def meet(microseconds, *arrays):
+    places = [pl.BlockSpec(memory_space=pl.ANY)] * len(arrays)
+    return pl.pallas_call(
+        lambda *refs: None,
+        out_shape=tuple(jax.ShapeDtypeStruct(a.shape, a.dtype) for a in arrays),
+        in_specs=places,
+        out_specs=tuple(places),
+        input_output_aliases={i: i for i in range(len(arrays))},
+        compiler_params=pltpu.CompilerParams(vmem_limit_bytes=2**20),
+        cost_estimate=pl.CostEstimate(
+            flops=microseconds * 10**9, bytes_accessed=0, transcendentals=0
+        ),
+        name="meet",
+    )(*arrays)
 
 
 def stack(blocks):

time: 144 us -> 127 us (0.88)
  starting transfers between devices: 87.9 us -> 79.4 us
  waiting for transfers between devices: 40.5 us -> 32.4 us
    ppermute x4, waiting for transfers between devices: 12.7 us -> 3.15 us  [exchange(): return lax.ppermute(x, ALL, pairs)]
    ppermute x11, starting transfers between devices: 56.6 us -> 48.1 us  [along_z(): return lax.ppermute(x, 'dp', pairs)]
    ppermute x4, starting transfers between devices: 16 us -> 12.3 us  [exchange(): return lax.ppermute(x, ALL, pairs)]
    ppermute x2, starting transfers between devices: 15.3 us -> 19 us  [to_sibling(): return lax.ppermute(x, 'dp', [(i, i ^ 1) for i in range(2 * pairs_z)])]
    unnamed x19 -> x15, local copies, waits for them, and re-layouts: 3.67 us -> 1.98 us
    pallas_call x14 -> x9, Pallas kernels: 8.59 us -> 8.3 us  [call(): pl.pallas_call(kernel, out_shape=out_shape, in_specs=[SM] * scalars + [VM...]
  transfers between devices with their start and end apart: 17 -> 17, of which waited for: 11 -> 10; matrix products, arithmetic and copies ran while one was open for 1% -> 2% of each run, Pallas kernels for 4% -> 4%
where the time goes in v5:
time: 127 us; the launch traced here: 126 us
  starting transfers between devices  79.4 us (63%)
  waiting for transfers between devices  32.4 us (26%)
  Pallas kernels  8.3 us (7%)
  local copies, waits for them, and re-layouts  3.84 us (3%)
  between operations  2.35 us (2%)
    ppermute x11, starting transfers between devices, along_z(): return lax.ppermute(x, 'dp', pairs)  48.1 us
    ppermute x11, waiting for transfers between devices, along_z(): return lax.ppermute(x, 'dp', pairs)  28.3 us
    ppermute x2, starting transfers between devices, to_sibling(): return lax.ppermute(x, 'dp', [(i, i ^ 1) for i in range(2 * pairs_z)])  19 us
    ppermute x4, starting transfers between devices, exchange(): return lax.ppermute(x, ALL, pairs)  12.3 us
    pallas_call x9, Pallas kernels, call(): pl.pallas_call(kernel, out_shape=out_shape, in_specs=[SM] * scalars + [VM...  8.3 us
    ppermute x4, waiting for transfers between devices, exchange(): return lax.ppermute(x, ALL, pairs)  3.15 us
  transfers between devices with their start and end apart: 17, of which 10 were waited for; matrix products, arithmetic and copies ran while one was open for 2% of the time, Pallas kernels for 4%

profile of v5, /device:TPU:1, one launch (start us, length us, event | category | flops | bytes accessed | tf_op | source)
XLA Modules:
  0.0 126.3 jit_solution(6621704215355800447)
XLA Ops:
  1.7 16.1 %collective-permute-start.3 = (bf16[2,96,256]{2,1,0:T(8,128)(2,1)S(1)}, bf16[2,96,256]{2,1,0:T(8,128)(2,1)S(1)}, u32[]{:S(2)}, u32[]{:S(2)}) collective-permute-start(bf16[2,96,256]{2,1,0:T(8,128)(2,1)S(1)} %fusion), channel_id=1, source_target_pairs={{0,16},{16,0},{32,48},{48,32},{64,80},{80,64},{96,112},{112,96},{1... | collective-permute-start | bytes 294920 | tf_op jit(solution)/shard_map/ppermute | solution.py:33
  20.0 10.1 %collective-permute-start = (bf16[112,384]{1,0:T(8,128)(2,1)S(1)}, bf16[112,384]{1,0:T(8,128)(2,1)S(1)}, u32[]{:S(2)}, u32[]{:S(2)}) collective-permute-start(bf16[112,384]{1,0:T(8,128)(2,1)S(1)} %make_unit.1.refs_0_), channel_id=1, source_target_pairs={{0,256},{16,784},{32,288},{48,816},{64,320},{80,848},{96,352},{112... | collective-permute-start | bytes 258056 | tf_op jit(solution)/shard_map/ppermute | solution.py:29
  30.1 3.9 %collective-permute-start.1 = (bf16[112,384]{1,0:T(8,128)(2,1)S(1)}, bf16[112,384]{1,0:T(8,128)(2,1)S(1)}, u32[]{:S(2)}, u32[]{:S(2)}) collective-permute-start(bf16[112,384]{1,0:T(8,128)(2,1)S(1)} %make_unit.1.refs_0_), channel_id=1, source_target_pairs={{0,768},{16,272},{32,800},{48,304},{64,832},{80,336},{96,864},{112... | collective-permute-start | bytes 258056 | tf_op jit(solution)/shard_map/ppermute | solution.py:29
  36.3 8.6 %collective-permute-done.1.refs_1_ = bf16[112,384]{1,0:T(8,128)(2,1)S(1)} collective-permute-done((bf16[112,384]{1,0:T(8,128)(2,1)S(1)}, bf16[112,384]{1,0:T(8,128)(2,1)S(1)}, u32[]{:S(2)}, u32[]{:S(2)}) %collective-permute-start.1) | collective-permute-done | bytes 86048 | tf_op jit(solution)/shard_map/ppermute | solution.py:29
  44.9 13.0 %collective-permute-start.2 = (bf16[112,384]{1,0:T(8,128)(2,1)S(1)}, bf16[112,384]{1,0:T(8,128)(2,1)S(1)}, u32[]{:S(2)}, u32[]{:S(2)}) collective-permute-start(bf16[112,384]{1,0:T(8,128)(2,1)S(1)} %get-tuple-element.25.refs_3_), channel_id=1, source_target_pairs={{0,256},{16,784},{32,288},{48,816},{64,320},{80,848},{96,352},{112... | collective-permute-start | bytes 258056 | tf_op jit(solution)/shard_map/ppermute | solution.py:29
  58.0 3.9 %collective-permute-start.5 = (bf16[384,512]{1,0:T(8,128)(2,1)S(1)}, bf16[384,512]{1,0:T(8,128)(2,1)S(1)}, u32[]{:S(2)}, u32[]{:S(2)}) collective-permute-start(bf16[384,512]{1,0:T(8,128)(2,1)S(1)} %stack.3.refs_0_), channel_id=1, source_target_pairs={{0,12},{1,13},{2,14},{3,15},{4,8},{5,9},{6,10},{7,11},{8,4},{9,5},... | collective-permute-start | bytes 1179656 | tf_op jit(solution)/shard_map/ppermute | solution.py:44
  61.9 2.9 %collective-permute-done.2.refs_0_ = bf16[112,384]{1,0:T(8,128)(2,1)S(1)} collective-permute-done((bf16[112,384]{1,0:T(8,128)(2,1)S(1)}, bf16[112,384]{1,0:T(8,128)(2,1)S(1)}, u32[]{:S(2)}, u32[]{:S(2)}) %collective-permute-start.2) | collective-permute-done | bytes 86048 | tf_op jit(solution)/shard_map/ppermute | solution.py:29
  64.8 3.1 %collective-permute-done.5.refs_1_ = bf16[384,512]{1,0:T(8,128)(2,1)S(1)} collective-permute-done((bf16[384,512]{1,0:T(8,128)(2,1)S(1)}, bf16[384,512]{1,0:T(8,128)(2,1)S(1)}, u32[]{:S(2)}, u32[]{:S(2)}) %collective-permute-start.5) | collective-permute-done | bytes 393248 | tf_op jit(solution)/shard_map/ppermute | solution.py:44
  68.0 2.6 %collective-permute-start.8 = (bf16[400,384]{1,0:T(8,128)(2,1)S(1)}, bf16[400,384]{1,0:T(8,128)(2,1)}, u32[]{:S(2)}, u32[]{:S(2)}) collective-permute-start(bf16[400,384]{1,0:T(8,128)(2,1)S(1)} %join_units.1.refs_2_), channel_id=1, source_target_pairs={{0,32},{16,1008},{32,64},{48,16},{64,96},{80,48},{96,128},{112,80}... | collective-permute-start | bytes 921608 | tf_op jit(solution)/shard_map/ppermute | solution.py:29
  70.6 2.7 %collective-permute-start.9 = (bf16[400,384]{1,0:T(8,128)(2,1)S(1)}, bf16[400,384]{1,0:T(8,128)(2,1)}, u32[]{:S(2)}, u32[]{:S(2)}) collective-permute-start(bf16[400,384]{1,0:T(8,128)(2,1)S(1)} %join_units.1.refs_2_), channel_id=1, source_target_pairs={{0,992},{16,48},{32,0},{48,80},{64,32},{80,112},{96,64},{112,144},... | collective-permute-start | bytes 921608 | tf_op jit(solution)/shard_map/ppermute | solution.py:29
  73.3 2.5 %collective-permute-start.6 = (bf16[768,512]{1,0:T(8,128)(2,1)S(1)}, bf16[768,512]{1,0:T(8,128)(2,1)S(1)}, u32[]{:S(2)}, u32[]{:S(2)}) collective-permute-start(bf16[768,512]{1,0:T(8,128)(2,1)S(1)} %stack.4.refs_0_), channel_id=1, source_target_pairs={{0,1},{1,0},{2,3},{3,2},{4,5},{5,4},{6,7},{7,6},{8,9},{9,8},{10,11... | collective-permute-start | bytes 2359304 | tf_op jit(solution)/shard_map/ppermute | solution.py:44
  76.0 5.1 %collective-permute-done.9.refs_1_ = bf16[400,384]{1,0:T(8,128)(2,1)} collective-permute-done((bf16[400,384]{1,0:T(8,128)(2,1)S(1)}, bf16[400,384]{1,0:T(8,128)(2,1)}, u32[]{:S(2)}, u32[]{:S(2)}) %collective-permute-start.9) | collective-permute-done | bytes 307232 | tf_op jit(solution)/shard_map/ppermute | solution.py:29
  83.0 3.4 %collective-permute-start.11 = (bf16[400,384]{1,0:T(8,128)(2,1)}, bf16[400,384]{1,0:T(8,128)(2,1)}, u32[]{:S(2)}, u32[]{:S(2)}) collective-permute-start(bf16[400,384]{1,0:T(8,128)(2,1)} %get-tuple-element.31.refs_4_), channel_id=1, source_target_pairs={{0,992},{16,48},{32,0},{48,80},{64,32},{80,112},{96,64},{112,144},... | collective-permute-start | bytes 921608 | tf_op jit(solution)/shard_map/ppermute | solution.py:29
  86.5 3.9 %collective-permute-start.7 = (bf16[1536,512]{1,0:T(8,128)(2,1)S(1)}, bf16[1536,512]{1,0:T(8,128)(2,1)S(1)}, u32[]{:S(2)}, u32[]{:S(2)}) collective-permute-start(bf16[1536,512]{1,0:T(8,128)(2,1)S(1)} %stack.5.refs_0_), channel_id=1, source_target_pairs={{0,3},{1,2},{2,1},{3,0},{4,7},{5,6},{6,5},{7,4},{8,11},{9,10},{10,... | collective-permute-start | bytes 4718600 | tf_op jit(solution)/shard_map/ppermute | solution.py:44
  90.4 2.8 %collective-permute-done.11.refs_1_ = bf16[400,384]{1,0:T(8,128)(2,1)} collective-permute-done((bf16[400,384]{1,0:T(8,128)(2,1)}, bf16[400,384]{1,0:T(8,128)(2,1)}, u32[]{:S(2)}, u32[]{:S(2)}) %collective-permute-start.11) | collective-permute-done | bytes 307232 | tf_op jit(solution)/shard_map/ppermute | solution.py:29
  93.2 3.1 %collective-permute-start.12 = (bf16[400,384]{1,0:T(8,128)(2,1)}, bf16[400,384]{1,0:T(8,128)(2,1)}, u32[]{:S(2)}, u32[]{:S(2)}) collective-permute-start(bf16[400,384]{1,0:T(8,128)(2,1)} %get-tuple-element.32.refs_5_), channel_id=1, source_target_pairs={{0,32},{16,1008},{32,64},{48,16},{64,96},{80,48},{96,128},{112,80}... | collective-permute-start | bytes 921608 | tf_op jit(solution)/shard_map/ppermute | solution.py:29
  96.3 2.2 %collective-permute-start.13 = (bf16[400,384]{1,0:T(8,128)(2,1)}, bf16[400,384]{1,0:T(8,128)(2,1)}, u32[]{:S(2)}, u32[]{:S(2)}) collective-permute-start(bf16[400,384]{1,0:T(8,128)(2,1)} %get-tuple-element.33.refs_6_), channel_id=1, source_target_pairs={{0,992},{16,48},{32,0},{48,80},{64,32},{80,112},{96,64},{112,144},... | collective-permute-start | bytes 921608 | tf_op jit(solution)/shard_map/ppermute | solution.py:29
  98.6 2.8 %collective-permute-done.12.refs_0_ = bf16[400,384]{1,0:T(8,128)(2,1)} collective-permute-done((bf16[400,384]{1,0:T(8,128)(2,1)}, bf16[400,384]{1,0:T(8,128)(2,1)}, u32[]{:S(2)}, u32[]{:S(2)}) %collective-permute-start.12) | collective-permute-done | bytes 307232 | tf_op jit(solution)/shard_map/ppermute | solution.py:29
  101.4 5.7 %collective-permute-done.13.refs_1_ = bf16[400,384]{1,0:T(8,128)(2,1)} collective-permute-done((bf16[400,384]{1,0:T(8,128)(2,1)}, bf16[400,384]{1,0:T(8,128)(2,1)}, u32[]{:S(2)}, u32[]{:S(2)}) %collective-permute-start.13) | collective-permute-done | bytes 307232 | tf_op jit(solution)/shard_map/ppermute | solution.py:29
  108.0 2.3 %collective-permute-start.14 = (bf16[208,384]{1,0:T(8,128)(2,1)S(1)}, bf16[208,384]{1,0:T(8,128)(2,1)S(1)}, u32[]{:S(2)}, u32[]{:S(2)}) collective-permute-start(bf16[208,384]{1,0:T(8,128)(2,1)S(1)} %slice.16), channel_id=1, source_target_pairs={{0,32},{16,1008},{32,64},{48,16},{64,96},{80,48},{96,128},{112,80}... | collective-permute-start | bytes 479240 | tf_op jit(solution)/shard_map/ppermute | solution.py:29
  111.2 3.0 %collective-permute-start.15 = (bf16[208,384]{1,0:T(8,128)(2,1)S(1)}, bf16[208,384]{1,0:T(8,128)(2,1)S(1)}, u32[]{:S(2)}, u32[]{:S(2)}) collective-permute-start(bf16[208,384]{1,0:T(8,128)(2,1)S(1)} %slice.17), channel_id=1, source_target_pairs={{0,992},{16,48},{32,0},{48,80},{64,32},{80,112},{96,64},{112,144},... | collective-permute-start | bytes 479240 | tf_op jit(solution)/shard_map/ppermute | solution.py:29
  114.3 4.4 %project_first.1 = (f32[512,384]{1,0:T(8,128)S(1)}, f32[16,384]{1,0:T(8,128)S(1)}) custom-call(s32[32]{0:T(128)S(1)} %fusion.8.starts, s32[32]{0:T(128)S(1)} %get-tuple-element.46.outers, bf16[1536,512]{1,0:T(8,128)(2,1)S(1)} %stack.5.refs_0_, bf16[1536,512]{1,0:T(8,128)(2,1)S(1)} %collective-permute-done.7.refs_1_, bf16[400,384]{1,0:T(8,128)(2,1)S(1)} %join_units.1.refs_2_, ...), custom_call_target="tpu_custom_call" | custom-call | flops 1056964608 | bytes 6291456 | tf_op jit(solution)/shard_map/project_first/pallas_call | solution.py:237
  119.9 2.9 %collective-permute-start.16 = (f32[264,384]{1,0:T(8,128)S(1)}, f32[264,384]{1,0:T(8,128)S(1)}, u32[]{:S(2)}, u32[]{:S(2)}) collective-permute-start(f32[264,384]{1,0:T(8,128)S(1)} %get-tuple-element.39), channel_id=1, source_target_pairs={{0,16},{16,0},{32,48},{48,32},{64,80},{80,64},{96,112},{112,96},{1... | collective-permute-start | bytes 1216520 | tf_op jit(solution)/shard_map/ppermute | solution.py:33
  124.2 2.2 %attention.1 = (bf16[256,384]{1,0:T(8,128)(2,1)}, bf16[256,384]{1,0:T(8,128)(2,1)}, bf16[256,384]{1,0:T(8,128)(2,1)}, f32[1,32]{1,0:T(1,128)}) custom-call(s32[1]{0:T(128)S(6)} %copy.40.group, f32[264,384]{1,0:T(8,128)S(1)} %get-tuple-element.38.mine_ref, f32[264,384]{1,0:T(8,128)S(1)} %collective-permute-done.16.got_ref, ...), custom_call_target="tpu_custom_call" | custom-call | flops 201326592 | bytes 3145728 | tf_op jit(solution)/shard_map/attention/pallas_call | solution.py:237
  (47 shorter events, 11.0 us)
Async XLA Ops:
  1.7 32.3 %collective-permute-start.3 = (bf16[2,96,256]{2,1,0:T(8,128)(2,1)S(1)}, bf16[2,96,256]{2,1,0:T(8,128)(2,1)S(1)}, u32[]{:S(2)}, u32[]{:S(2)}) collective-permute-start(bf16[2,96,256]{2,1,0:T(8,128)(2,1)S(1)} %fusion), channel_id=1, source_target_pairs={{0,16},{16,0},{32,48},{48,32},{64,80},{80,64},{96,112},{112,96},{1... | collective-permute-start | bytes 294920 | tf_op jit(solution)/shard_map/ppermute | solution.py:33
  19.1 0.9 copy-start.3
  20.0 16.3 %collective-permute-start = (bf16[112,384]{1,0:T(8,128)(2,1)S(1)}, bf16[112,384]{1,0:T(8,128)(2,1)S(1)}, u32[]{:S(2)}, u32[]{:S(2)}) collective-permute-start(bf16[112,384]{1,0:T(8,128)(2,1)S(1)} %make_unit.1.refs_0_), channel_id=1, source_target_pairs={{0,256},{16,784},{32,288},{48,816},{64,320},{80,848},{96,352},{112... | collective-permute-start | bytes 258056 | tf_op jit(solution)/shard_map/ppermute | solution.py:29
  30.1 14.8 %collective-permute-start.1 = (bf16[112,384]{1,0:T(8,128)(2,1)S(1)}, bf16[112,384]{1,0:T(8,128)(2,1)S(1)}, u32[]{:S(2)}, u32[]{:S(2)}) collective-permute-start(bf16[112,384]{1,0:T(8,128)(2,1)S(1)} %make_unit.1.refs_0_), channel_id=1, source_target_pairs={{0,768},{16,272},{32,800},{48,304},{64,832},{80,336},{96,864},{112... | collective-permute-start | bytes 258056 | tf_op jit(solution)/shard_map/ppermute | solution.py:29
  34.1 23.8 %collective-permute-start.4 = (bf16[192,512]{1,0:T(8,128)(2,1)S(1)}, bf16[192,512]{1,0:T(8,128)(2,1)S(1)}, u32[]{:S(2)}, u32[]{:S(2)}) collective-permute-start(bf16[192,512]{1,0:T(8,128)(2,1)S(1)} %bitcast.36), channel_id=1, source_target_pairs={{0,4},{1,5},{2,6},{3,7},{4,0},{5,1},{6,2},{7,3},{8,12},{9,13},{10,... | collective-permute-start | bytes 589832 | tf_op jit(solution)/shard_map/ppermute | solution.py:44
  44.9 19.9 %collective-permute-start.2 = (bf16[112,384]{1,0:T(8,128)(2,1)S(1)}, bf16[112,384]{1,0:T(8,128)(2,1)S(1)}, u32[]{:S(2)}, u32[]{:S(2)}) collective-permute-start(bf16[112,384]{1,0:T(8,128)(2,1)S(1)} %get-tuple-element.25.refs_3_), channel_id=1, source_target_pairs={{0,256},{16,784},{32,288},{48,816},{64,320},{80,848},{96,352},{112... | collective-permute-start | bytes 258056 | tf_op jit(solution)/shard_map/ppermute | solution.py:29
  58.0 10.0 %collective-permute-start.5 = (bf16[384,512]{1,0:T(8,128)(2,1)S(1)}, bf16[384,512]{1,0:T(8,128)(2,1)S(1)}, u32[]{:S(2)}, u32[]{:S(2)}) collective-permute-start(bf16[384,512]{1,0:T(8,128)(2,1)S(1)} %stack.3.refs_0_), channel_id=1, source_target_pairs={{0,12},{1,13},{2,14},{3,15},{4,8},{5,9},{6,10},{7,11},{8,4},{9,5},... | collective-permute-start | bytes 1179656 | tf_op jit(solution)/shard_map/ppermute | solution.py:44
  68.0 8.0 %collective-permute-start.8 = (bf16[400,384]{1,0:T(8,128)(2,1)S(1)}, bf16[400,384]{1,0:T(8,128)(2,1)}, u32[]{:S(2)}, u32[]{:S(2)}) collective-permute-start(bf16[400,384]{1,0:T(8,128)(2,1)S(1)} %join_units.1.refs_2_), channel_id=1, source_target_pairs={{0,32},{16,1008},{32,64},{48,16},{64,96},{80,48},{96,128},{112,80}... | collective-permute-start | bytes 921608 | tf_op jit(solution)/shard_map/ppermute | solution.py:29
  70.6 10.5 %collective-permute-start.9 = (bf16[400,384]{1,0:T(8,128)(2,1)S(1)}, bf16[400,384]{1,0:T(8,128)(2,1)}, u32[]{:S(2)}, u32[]{:S(2)}) collective-permute-start(bf16[400,384]{1,0:T(8,128)(2,1)S(1)} %join_units.1.refs_2_), channel_id=1, source_target_pairs={{0,992},{16,48},{32,0},{48,80},{64,32},{80,112},{96,64},{112,144},... | collective-permute-start | bytes 921608 | tf_op jit(solution)/shard_map/ppermute | solution.py:29
  73.3 13.0 %collective-permute-start.6 = (bf16[768,512]{1,0:T(8,128)(2,1)S(1)}, bf16[768,512]{1,0:T(8,128)(2,1)S(1)}, u32[]{:S(2)}, u32[]{:S(2)}) collective-permute-start(bf16[768,512]{1,0:T(8,128)(2,1)S(1)} %stack.4.refs_0_), channel_id=1, source_target_pairs={{0,1},{1,0},{2,3},{3,2},{4,5},{5,4},{6,7},{7,6},{8,9},{9,8},{10,11... | collective-permute-start | bytes 2359304 | tf_op jit(solution)/shard_map/ppermute | solution.py:44
  81.0 9.4 %collective-permute-start.10 = (bf16[400,384]{1,0:T(8,128)(2,1)}, bf16[400,384]{1,0:T(8,128)(2,1)}, u32[]{:S(2)}, u32[]{:S(2)}) collective-permute-start(bf16[400,384]{1,0:T(8,128)(2,1)} %get-tuple-element.30.refs_3_), channel_id=1, source_target_pairs={{0,32},{16,1008},{32,64},{48,16},{64,96},{80,48},{96,128},{112,80}... | collective-permute-start | bytes 921608 | tf_op jit(solution)/shard_map/ppermute | solution.py:29
  83.0 10.3 %collective-permute-start.11 = (bf16[400,384]{1,0:T(8,128)(2,1)}, bf16[400,384]{1,0:T(8,128)(2,1)}, u32[]{:S(2)}, u32[]{:S(2)}) collective-permute-start(bf16[400,384]{1,0:T(8,128)(2,1)} %get-tuple-element.31.refs_4_), channel_id=1, source_target_pairs={{0,992},{16,48},{32,0},{48,80},{64,32},{80,112},{96,64},{112,144},... | collective-permute-start | bytes 921608 | tf_op jit(solution)/shard_map/ppermute | solution.py:29
  86.5 12.1 %copy-start.5 = (s32[32]{0:T(128)S(1)}, s32[32]{0:T(128)}, u32[]{:S(2)}) copy-start(s32[32]{0:T(128)} %constant.113.clone) | copy-start | bytes 388
  86.5 12.1 %copy-start.6 = (s32[32]{0:T(128)S(1)}, s32[32]{0:T(128)}, u32[]{:S(2)}) copy-start(s32[32]{0:T(128)} %constant.117) | copy-start | bytes 388
  86.5 27.8 %collective-permute-start.7 = (bf16[1536,512]{1,0:T(8,128)(2,1)S(1)}, bf16[1536,512]{1,0:T(8,128)(2,1)S(1)}, u32[]{:S(2)}, u32[]{:S(2)}) collective-permute-start(bf16[1536,512]{1,0:T(8,128)(2,1)S(1)} %stack.5.refs_0_), channel_id=1, source_target_pairs={{0,3},{1,2},{2,1},{3,0},{4,7},{5,6},{6,5},{7,4},{8,11},{9,10},{10,... | collective-permute-start | bytes 4718600 | tf_op jit(solution)/shard_map/ppermute | solution.py:44
  93.2 8.2 %collective-permute-start.12 = (bf16[400,384]{1,0:T(8,128)(2,1)}, bf16[400,384]{1,0:T(8,128)(2,1)}, u32[]{:S(2)}, u32[]{:S(2)}) collective-permute-start(bf16[400,384]{1,0:T(8,128)(2,1)} %get-tuple-element.32.refs_5_), channel_id=1, source_target_pairs={{0,32},{16,1008},{32,64},{48,16},{64,96},{80,48},{96,128},{112,80}... | collective-permute-start | bytes 921608 | tf_op jit(solution)/shard_map/ppermute | solution.py:29
  96.3 10.8 %collective-permute-start.13 = (bf16[400,384]{1,0:T(8,128)(2,1)}, bf16[400,384]{1,0:T(8,128)(2,1)}, u32[]{:S(2)}, u32[]{:S(2)}) collective-permute-start(bf16[400,384]{1,0:T(8,128)(2,1)} %get-tuple-element.33.refs_6_), channel_id=1, source_target_pairs={{0,992},{16,48},{32,0},{48,80},{64,32},{80,112},{96,64},{112,144},... | collective-permute-start | bytes 921608 | tf_op jit(solution)/shard_map/ppermute | solution.py:29
  108.0 10.6 %collective-permute-start.14 = (bf16[208,384]{1,0:T(8,128)(2,1)S(1)}, bf16[208,384]{1,0:T(8,128)(2,1)S(1)}, u32[]{:S(2)}, u32[]{:S(2)}) collective-permute-start(bf16[208,384]{1,0:T(8,128)(2,1)S(1)} %slice.16), channel_id=1, source_target_pairs={{0,32},{16,1008},{32,64},{48,16},{64,96},{80,48},{96,128},{112,80}... | collective-permute-start | bytes 479240 | tf_op jit(solution)/shard_map/ppermute | solution.py:29
  111.2 7.4 %collective-permute-start.15 = (bf16[208,384]{1,0:T(8,128)(2,1)S(1)}, bf16[208,384]{1,0:T(8,128)(2,1)S(1)}, u32[]{:S(2)}, u32[]{:S(2)}) collective-permute-start(bf16[208,384]{1,0:T(8,128)(2,1)S(1)} %slice.17), channel_id=1, source_target_pairs={{0,992},{16,48},{32,0},{48,80},{64,32},{80,112},{96,64},{112,144},... | collective-permute-start | bytes 479240 | tf_op jit(solution)/shard_map/ppermute | solution.py:29
  118.7 4.2 %copy-start = (bf16[256,384]{1,0:T(8,128)(2,1)S(1)}, bf16[256,384]{1,0:T(8,128)(2,1)}, u32[]{:S(2)}) copy-start(bf16[256,384]{1,0:T(8,128)(2,1)} %q_ref.3) | copy-start | bytes 589828
  118.7 4.2 %copy-start.1 = (bf16[256,384]{1,0:T(8,128)(2,1)S(1)}, bf16[256,384]{1,0:T(8,128)(2,1)}, u32[]{:S(2)}) copy-start(bf16[256,384]{1,0:T(8,128)(2,1)} %k_ref.3) | copy-start | bytes 589828
  118.7 4.2 %copy-start.4 = (f32[32]{0:T(128)S(1)}, f32[32]{0:T(128)}, u32[]{:S(2)}) copy-start(f32[32]{0:T(128)} %param.16) | copy-start | bytes 388
  118.7 5.5 %copy-start.2 = (bf16[256,384]{1,0:T(8,128)(2,1)S(1)}, bf16[256,384]{1,0:T(8,128)(2,1)}, u32[]{:S(2)}) copy-start(bf16[256,384]{1,0:T(8,128)(2,1)} %v_ref.1) | copy-start | bytes 589828
  119.9 4.3 %collective-permute-start.16 = (f32[264,384]{1,0:T(8,128)S(1)}, f32[264,384]{1,0:T(8,128)S(1)}, u32[]{:S(2)}, u32[]{:S(2)}) collective-permute-start(f32[264,384]{1,0:T(8,128)S(1)} %get-tuple-element.39), channel_id=1, source_target_pairs={{0,16},{16,0},{32,48},{48,32},{64,80},{80,64},{96,112},{112,96},{1... | collective-permute-start | bytes 1216520 | tf_op jit(solution)/shard_map/ppermute | solution.py:33

commit v6 on v5

--- a/solution.py
+++ b/solution.py
@@ -11,12 +11,13 @@
 PATCHES = 256
 ROBUST_RATE = 0.5
 SIDE = 4
-FAR = 8
+FAR = 11
+STEPS = 5
 UNIT = 96
 STATS = 4
 TAIL = 16
 HALF = 2 * UNIT + TAIL
-FULL = 4 * UNIT + TAIL
+FULL = 3 * UNIT + TAIL
 ALL = ("dp", "mp")
 
 
@@ -46,41 +47,35 @@
 
 def gather(unit, block, pairs_z):
     tie = lax.optimization_barrier
-    mine = along_z(unit, FAR, -FAR, pairs_z)
-    opposite = along_z(unit, -FAR, FAR, pairs_z)
+    behind = along_z(unit, FAR, -FAR, pairs_z)
+    ahead = along_z(unit, -FAR, FAR, pairs_z)
     passed = exchange(block, 1, True, pairs_z)
-    mine, opposite = meet(2, mine, opposite)
-    farthest = along_z(mine, FAR, -FAR, pairs_z)
-    block = stack([block, passed])
-    passed = exchange(block, 3, True, pairs_z)
-    (farthest,) = meet(4, farthest)
-    farthest, passed, block = tie((farthest, passed, block))
-    block = stack([block, passed])
-    bundle = join_units(unit, opposite, farthest, mine)
+    behind, ahead = meet(2, behind, ahead)
+    behind, ahead, block, passed = tie((behind, ahead, block, passed))
+    bundle = join_units(unit, ahead, behind)
+    block, bundle = tie((stack([block, passed]), bundle))
     pieces = [bundle]
     p = q = bundle
-    for step, wait in enumerate((6, 6, 8)):
+    for step, wait in enumerate((2, 7, 5, 5)):
         p = along_z(p, 1, -1, pairs_z)
         q = along_z(q, -1, 1, pairs_z)
+        if step < 3:
+            passed = exchange(block, (3, 1, 3)[step], step == 0, pairs_z)
         if step < 2:
-            passed = exchange(block, 1 + 2 * step, False, pairs_z)
+            block = stack([block, passed])
         p, q = meet(wait, p, q)
-        if step == 0:
-            block = stack([block, passed])
         pieces += [p, q]
-    half = passed
     p = along_z(p[:HALF], 1, -1, pairs_z)
-    q = along_z(q[UNIT : UNIT + HALF], -1, 1, pairs_z)
-    return pieces + [p, q], [block, half]
+    q = along_z(q, -1, 1, pairs_z)
+    return pieces + [p, q], [block, passed]
 
 
 def piece_offsets():
-    slots = [0, FAR, 2 * FAR, -FAR]
-    offsets = [slots]
-    for k in range(1, FAR // 2):
-        offsets += [[o - k for o in slots], [o + k for o in slots]]
-    k = FAR // 2
-    offsets += [[o - k for o in slots[:2]], [o + k for o in slots[1:3]]]
+    units = [0, FAR, -FAR]
+    offsets = [units]
+    for k in range(1, STEPS + 1):
+        offsets += [[o - k for o in units], [o + k for o in units]]
+    offsets[-2] = offsets[-2][:2]
     return offsets
 
 
@@ -160,8 +155,8 @@
     xs_ref[pl.ds(2 * UNIT, TAIL), :] = jnp.zeros((TAIL, xs_ref.shape[1]), xs_ref.dtype)
     stats_ref[...] = jnp.zeros_like(stats_ref)
     for i, piece in enumerate(pieces):
-        for k in range(4):
-            pick_rows(starts, outers, 4 * i + k, blocks, xs_ref, row_of(k))
+        for k in range(3):
+            pick_rows(starts, outers, 3 * i + k, blocks, xs_ref, row_of(k))
         product = product_of(xs_ref[...], piece[...])
         if i == 0:
             acc_ref[...] = product
@@ -172,18 +167,18 @@
 
 def last_kernel(starts, outers, core, *refs):
     blocks, (p_ref, q_ref, acc_ref, stats_ref, mine_ref, send_ref, xs_ref, w_ref, sum_ref) = refs[:2], refs[2:]
-    for k, at in enumerate((0, UNIT, HALF, HALF + UNIT + TAIL)):
-        pick_rows(starts, outers, 28 + k, blocks, xs_ref, at)
-    for at in (2 * UNIT, HALF + UNIT):
+    for k, at in enumerate((0, UNIT, HALF, HALF + UNIT, 2 * HALF)):
+        pick_rows(starts, outers, 27 + k, blocks, xs_ref, at)
+    for at in (2 * UNIT, HALF + 2 * UNIT):
         xs_ref[pl.ds(at, TAIL), :] = jnp.zeros((TAIL, xs_ref.shape[1]), xs_ref.dtype)
     w_ref[pl.ds(0, HALF), :] = p_ref[...]
-    w_ref[pl.ds(HALF, HALF), :] = q_ref[...]
+    w_ref[pl.ds(HALF, FULL), :] = q_ref[...]
     sum_ref[...] = acc_ref[...] + product_of(xs_ref[...], w_ref[...])
     stats = stats_ref[...]
     row = lax.broadcasted_iota(jnp.int32, stats.shape, 0)
-    stats += jnp.where(row < 8, p_ref[pl.ds(2 * UNIT, TAIL), :].astype(jnp.float32), 0.0)
-    middle = (row >= 4) & (row < 12)
-    stats += jnp.where(middle, q_ref[pl.ds(UNIT, TAIL), :].astype(jnp.float32), 0.0)
+    p_stats = p_ref[pl.ds(2 * UNIT, TAIL), :].astype(jnp.float32)
+    stats += jnp.where(row < 2 * STATS, p_stats, 0.0)
+    stats += q_ref[pl.ds(2 * UNIT, TAIL), :].astype(jnp.float32)
     count = jnp.sum(jnp.where(row % 4 == 0, stats, 0.0), axis=0, keepdims=True)
     total = jnp.sum(jnp.where(row % 4 == 0, 0.0, stats), axis=0, keepdims=True)
     row8 = row[:8]
@@ -314,10 +309,10 @@
         first_kernel,
         "project_first",
         (total, jax.ShapeDtypeStruct((TAIL, heads), f32)),
-        (starts, outer, *features, *pieces[:7]),
+        (starts, outer, *features, *pieces[:-2]),
         2,
         [pltpu.VMEM((FULL, 2 * PATCHES), bf16)],
-        2 * 512 * 2688 * heads,
+        2 * 512 * 2592 * heads,
         6 * 2**20,
     )
     partial = jax.ShapeDtypeStruct((PATCHES + 8, heads), f32)
@@ -325,14 +320,14 @@
         last_kernel,
         "project_last",
         (partial, partial),
-        (starts, outer, core.reshape(1), *features, *pieces[7:], summed, stats),
+        (starts, outer, core.reshape(1), *features, *pieces[-2:], summed, stats),
         3,
         [
-            pltpu.VMEM((2 * HALF, 2 * PATCHES), bf16),
-            pltpu.VMEM((2 * HALF, heads), bf16),
+            pltpu.VMEM((HALF + FULL, 2 * PATCHES), bf16),
+            pltpu.VMEM((HALF + FULL, heads), bf16),
             pltpu.VMEM((2 * PATCHES, heads), f32),
         ],
-        2 * 512 * 384 * heads,
+        2 * 512 * 480 * heads,
         2 * 2**20,
     )
     received = to_sibling(send, pairs_z)

time: 127 us -> 127 us (level)
  Pallas kernels: 8.3 us -> 9.72 us
    ppermute x11 -> x12, starting transfers between devices: 48.1 us -> 45.8 us  [along_z(): return lax.ppermute(x, 'dp', pairs)]
    ppermute x4, starting transfers between devices: 12.3 us -> 14.2 us  [exchange(): return lax.ppermute(x, ALL, pairs)]
    pallas_call x9, Pallas kernels: 8.3 us -> 9.71 us  [call(): pl.pallas_call(kernel, out_shape=out_shape, in_specs=[SM] * scalars + [VM...]
    ppermute x11 -> x12, waiting for transfers between devices: 28.3 us -> 26.9 us  [along_z(): return lax.ppermute(x, 'dp', pairs)]
  transfers between devices with their start and end apart: 17 -> 18, of which waited for: 10 -> 8; matrix products, arithmetic and copies ran while one was open for 2% -> 1% of each run, Pallas kernels for 4% -> 5%
where the time goes in v6:
time: 127 us; the launch traced here: 126 us
  starting transfers between devices  78.5 us (62%)
  waiting for transfers between devices  32.2 us (25%)
  Pallas kernels  9.72 us (8%)
  local copies, waits for them, and re-layouts  2.93 us (2%)
  between operations  2.4 us (2%)
    ppermute x12, starting transfers between devices, along_z(): return lax.ppermute(x, 'dp', pairs)  45.8 us
    ppermute x12, waiting for transfers between devices, along_z(): return lax.ppermute(x, 'dp', pairs)  26.9 us
    ppermute x2, starting transfers between devices, to_sibling(): return lax.ppermute(x, 'dp', [(i, i ^ 1) for i in range(2 * pairs_z)])  18.6 us
    ppermute x4, starting transfers between devices, exchange(): return lax.ppermute(x, ALL, pairs)  14.2 us
    pallas_call x9, Pallas kernels, call(): pl.pallas_call(kernel, out_shape=out_shape, in_specs=[SM] * scalars + [VM...  9.71 us
    ppermute x4, waiting for transfers between devices, exchange(): return lax.ppermute(x, ALL, pairs)  4.3 us
  transfers between devices with their start and end apart: 18, of which 8 were waited for; matrix products, arithmetic and copies ran while one was open for 1% of the time, Pallas kernels for 5%

profile of v6, /device:TPU:1, one launch (start us, length us, event | category | flops | bytes accessed | tf_op | source)
XLA Modules:
  0.0 125.8 jit_solution(5069353990466405563)
XLA Ops:
  1.7 16.1 %collective-permute-start.2 = (bf16[2,96,256]{2,1,0:T(8,128)(2,1)S(1)}, bf16[2,96,256]{2,1,0:T(8,128)(2,1)S(1)}, u32[]{:S(2)}, u32[]{:S(2)}) collective-permute-start(bf16[2,96,256]{2,1,0:T(8,128)(2,1)S(1)} %fusion), channel_id=1, source_target_pairs={{0,16},{16,0},{32,48},{48,32},{64,80},{80,64},{96,112},{112,96},{1... | collective-permute-start | bytes 294920 | tf_op jit(solution)/shard_map/ppermute | solution.py:34
  20.0 12.6 %collective-permute-start = (bf16[112,384]{1,0:T(8,128)(2,1)S(1)}, bf16[112,384]{1,0:T(8,128)(2,1)S(1)}, u32[]{:S(2)}, u32[]{:S(2)}) collective-permute-start(bf16[112,384]{1,0:T(8,128)(2,1)S(1)} %make_unit.1.refs_0_), channel_id=1, source_target_pairs={{0,352},{16,688},{32,384},{48,720},{64,416},{80,752},{96,448},{112... | collective-permute-start | bytes 258056 | tf_op jit(solution)/shard_map/ppermute | solution.py:30
  32.6 4.1 %collective-permute-start.1 = (bf16[112,384]{1,0:T(8,128)(2,1)S(1)}, bf16[112,384]{1,0:T(8,128)(2,1)S(1)}, u32[]{:S(2)}, u32[]{:S(2)}) collective-permute-start(bf16[112,384]{1,0:T(8,128)(2,1)S(1)} %make_unit.1.refs_0_), channel_id=1, source_target_pairs={{0,672},{16,368},{32,704},{48,400},{64,736},{80,432},{96,768},{112... | collective-permute-start | bytes 258056 | tf_op jit(solution)/shard_map/ppermute | solution.py:30
  36.8 1.9 %collective-permute-start.3 = (bf16[192,512]{1,0:T(8,128)(2,1)S(1)}, bf16[192,512]{1,0:T(8,128)(2,1)S(1)}, u32[]{:S(2)}, u32[]{:S(2)}) collective-permute-start(bf16[192,512]{1,0:T(8,128)(2,1)S(1)} %bitcast.36), channel_id=1, source_target_pairs={{0,4},{1,5},{2,6},{3,7},{4,0},{5,1},{6,2},{7,3},{8,12},{9,13},{10,... | collective-permute-start | bytes 589832 | tf_op jit(solution)/shard_map/ppermute | solution.py:45
  38.7 17.3 %collective-permute-done.1.refs_1_ = bf16[112,384]{1,0:T(8,128)(2,1)S(1)} collective-permute-done((bf16[112,384]{1,0:T(8,128)(2,1)S(1)}, bf16[112,384]{1,0:T(8,128)(2,1)S(1)}, u32[]{:S(2)}, u32[]{:S(2)}) %collective-permute-start.1) | collective-permute-done | bytes 86048 | tf_op jit(solution)/shard_map/ppermute | solution.py:30
  56.0 1.9 %collective-permute-start.7 = (bf16[304,384]{1,0:T(8,128)(2,1)S(1)}, bf16[304,384]{1,0:T(8,128)(2,1)S(1)}, u32[]{:S(2)}, u32[]{:S(2)}) collective-permute-start(bf16[304,384]{1,0:T(8,128)(2,1)S(1)} %join_units.1.refs_2_), channel_id=1, source_target_pairs={{0,32},{16,1008},{32,64},{48,16},{64,96},{80,48},{96,128},{112,80}... | collective-permute-start | bytes 700424 | tf_op jit(solution)/shard_map/ppermute | solution.py:30
  58.0 3.9 %collective-permute-start.8 = (bf16[304,384]{1,0:T(8,128)(2,1)S(1)}, bf16[304,384]{1,0:T(8,128)(2,1)S(1)}, u32[]{:S(2)}, u32[]{:S(2)}) collective-permute-start(bf16[304,384]{1,0:T(8,128)(2,1)S(1)} %join_units.1.refs_2_), channel_id=1, source_target_pairs={{0,992},{16,48},{32,0},{48,80},{64,32},{80,112},{96,64},{112,144},... | collective-permute-start | bytes 700424 | tf_op jit(solution)/shard_map/ppermute | solution.py:30
  61.9 4.8 %collective-permute-start.4 = (bf16[384,512]{1,0:T(8,128)(2,1)S(1)}, bf16[384,512]{1,0:T(8,128)(2,1)S(1)}, u32[]{:S(2)}, u32[]{:S(2)}) collective-permute-start(bf16[384,512]{1,0:T(8,128)(2,1)S(1)} %stack.3.refs_0_), channel_id=1, source_target_pairs={{0,12},{1,13},{2,14},{3,15},{4,8},{5,9},{6,10},{7,11},{8,4},{9,5},... | collective-permute-start | bytes 1179656 | tf_op jit(solution)/shard_map/ppermute | solution.py:45
  66.7 3.5 %collective-permute-done.8.refs_1_ = bf16[304,384]{1,0:T(8,128)(2,1)S(1)} collective-permute-done((bf16[304,384]{1,0:T(8,128)(2,1)S(1)}, bf16[304,384]{1,0:T(8,128)(2,1)S(1)}, u32[]{:S(2)}, u32[]{:S(2)}) %collective-permute-start.8) | collective-permute-done | bytes 233504 | tf_op jit(solution)/shard_map/ppermute | solution.py:30
  72.2 4.6 %collective-permute-start.9 = (bf16[304,384]{1,0:T(8,128)(2,1)S(1)}, bf16[304,384]{1,0:T(8,128)(2,1)}, u32[]{:S(2)}, u32[]{:S(2)}) collective-permute-start(bf16[304,384]{1,0:T(8,128)(2,1)S(1)} %get-tuple-element.38.refs_3_), channel_id=1, source_target_pairs={{0,32},{16,1008},{32,64},{48,16},{64,96},{80,48},{96,128},{112,80}... | collective-permute-start | bytes 700424 | tf_op jit(solution)/shard_map/ppermute | solution.py:30
  76.9 2.9 %collective-permute-start.5 = (bf16[768,512]{1,0:T(8,128)(2,1)S(1)}, bf16[768,512]{1,0:T(8,128)(2,1)S(1)}, u32[]{:S(2)}, u32[]{:S(2)}) collective-permute-start(bf16[768,512]{1,0:T(8,128)(2,1)S(1)} %stack.4.refs_0_), channel_id=1, source_target_pairs={{0,1},{1,0},{2,3},{3,2},{4,5},{5,4},{6,7},{7,6},{8,9},{9,8},{10,11... | collective-permute-start | bytes 2359304 | tf_op jit(solution)/shard_map/ppermute | solution.py:45
  80.6 4.3 %collective-permute-start.11 = (bf16[304,384]{1,0:T(8,128)(2,1)}, bf16[304,384]{1,0:T(8,128)(2,1)}, u32[]{:S(2)}, u32[]{:S(2)}) collective-permute-start(bf16[304,384]{1,0:T(8,128)(2,1)} %get-tuple-element.40.refs_5_), channel_id=1, source_target_pairs={{0,32},{16,1008},{32,64},{48,16},{64,96},{80,48},{96,128},{112,80}... | collective-permute-start | bytes 700424 | tf_op jit(solution)/shard_map/ppermute | solution.py:30
  84.9 1.9 %collective-permute-start.12 = (bf16[304,384]{1,0:T(8,128)(2,1)}, bf16[304,384]{1,0:T(8,128)(2,1)}, u32[]{:S(2)}, u32[]{:S(2)}) collective-permute-start(bf16[304,384]{1,0:T(8,128)(2,1)} %get-tuple-element.41.refs_6_), channel_id=1, source_target_pairs={{0,992},{16,48},{32,0},{48,80},{64,32},{80,112},{96,64},{112,144},... | collective-permute-start | bytes 700424 | tf_op jit(solution)/shard_map/ppermute | solution.py:30
  86.9 3.1 %collective-permute-done.5.refs_1_ = bf16[768,512]{1,0:T(8,128)(2,1)S(1)} collective-permute-done((bf16[768,512]{1,0:T(8,128)(2,1)S(1)}, bf16[768,512]{1,0:T(8,128)(2,1)S(1)}, u32[]{:S(2)}, u32[]{:S(2)}) %collective-permute-start.5) | collective-permute-done | bytes 786464 | tf_op jit(solution)/shard_map/ppermute | solution.py:45
  90.1 4.5 %collective-permute-start.6 = (bf16[1536,512]{1,0:T(8,128)(2,1)S(1)}, bf16[1536,512]{1,0:T(8,128)(2,1)S(1)}, u32[]{:S(2)}, u32[]{:S(2)}) collective-permute-start(bf16[1536,512]{1,0:T(8,128)(2,1)S(1)} %stack.5.refs_0_), channel_id=1, source_target_pairs={{0,3},{1,2},{2,1},{3,0},{4,7},{5,6},{6,5},{7,4},{8,11},{9,10},{10,... | collective-permute-start | bytes 4718600 | tf_op jit(solution)/shard_map/ppermute | solution.py:45
  94.7 1.9 %collective-permute-start.13 = (bf16[304,384]{1,0:T(8,128)(2,1)}, bf16[304,384]{1,0:T(8,128)(2,1)}, u32[]{:S(2)}, u32[]{:S(2)}) collective-permute-start(bf16[304,384]{1,0:T(8,128)(2,1)} %get-tuple-element.42.refs_7_), channel_id=1, source_target_pairs={{0,32},{16,1008},{32,64},{48,16},{64,96},{80,48},{96,128},{112,80}... | collective-permute-start | bytes 700424 | tf_op jit(solution)/shard_map/ppermute | solution.py:30
  96.6 3.4 %collective-permute-start.14 = (bf16[304,384]{1,0:T(8,128)(2,1)}, bf16[304,384]{1,0:T(8,128)(2,1)}, u32[]{:S(2)}, u32[]{:S(2)}) collective-permute-start(bf16[304,384]{1,0:T(8,128)(2,1)} %get-tuple-element.43.refs_8_), channel_id=1, source_target_pairs={{0,992},{16,48},{32,0},{48,80},{64,32},{80,112},{96,64},{112,144},... | collective-permute-start | bytes 700424 | tf_op jit(solution)/shard_map/ppermute | solution.py:30
  100.1 2.8 %collective-permute-done.13.refs_0_ = bf16[304,384]{1,0:T(8,128)(2,1)} collective-permute-done((bf16[304,384]{1,0:T(8,128)(2,1)}, bf16[304,384]{1,0:T(8,128)(2,1)}, u32[]{:S(2)}, u32[]{:S(2)}) %collective-permute-start.13) | collective-permute-done | bytes 233504 | tf_op jit(solution)/shard_map/ppermute | solution.py:30
  102.9 2.5 %collective-permute-done.14.refs_1_ = bf16[304,384]{1,0:T(8,128)(2,1)} collective-permute-done((bf16[304,384]{1,0:T(8,128)(2,1)}, bf16[304,384]{1,0:T(8,128)(2,1)}, u32[]{:S(2)}, u32[]{:S(2)}) %collective-permute-start.14) | collective-permute-done | bytes 233504 | tf_op jit(solution)/shard_map/ppermute | solution.py:30
  106.3 2.2 %collective-permute-start.15 = (bf16[208,384]{1,0:T(8,128)(2,1)S(1)}, bf16[208,384]{1,0:T(8,128)(2,1)S(1)}, u32[]{:S(2)}, u32[]{:S(2)}) collective-permute-start(bf16[208,384]{1,0:T(8,128)(2,1)S(1)} %slice.13), channel_id=1, source_target_pairs={{0,32},{16,1008},{32,64},{48,16},{64,96},{80,48},{96,128},{112,80}... | collective-permute-start | bytes 479240 | tf_op jit(solution)/shard_map/ppermute | solution.py:30
  108.6 3.0 %collective-permute-start.16 = (bf16[304,384]{1,0:T(8,128)(2,1)}, bf16[304,384]{1,0:T(8,128)(2,1)S(1)}, u32[]{:S(2)}, u32[]{:S(2)}) collective-permute-start(bf16[304,384]{1,0:T(8,128)(2,1)} %get-tuple-element.45.refs_10_), channel_id=1, source_target_pairs={{0,992},{16,48},{32,0},{48,80},{64,32},{80,112},{96,64},{112,144},... | collective-permute-start | bytes 700424 | tf_op jit(solution)/shard_map/ppermute | solution.py:30
  112.8 5.8 %project_first.1 = (f32[512,384]{1,0:T(8,128)S(1)}, f32[16,384]{1,0:T(8,128)S(1)}) custom-call(s32[32]{0:T(128)S(1)} %fusion.8.starts, s32[32]{0:T(128)S(1)} %get-tuple-element.56.outers, bf16[1536,512]{1,0:T(8,128)(2,1)S(1)} %stack.5.refs_0_, bf16[1536,512]{1,0:T(8,128)(2,1)S(1)} %collective-permute-done.6.refs_1_, bf16[304,384]{1,0:T(8,128)(2,1)S(1)} %join_units.1.refs_2_, ...), custom_call_target="tpu_custom_call" | custom-call | flops 1019215872 | bytes 6291456 | tf_op jit(solution)/shard_map/project_first/pallas_call | solution.py:232
  119.8 2.5 %collective-permute-start.17 = (f32[264,384]{1,0:T(8,128)S(1)}, f32[264,384]{1,0:T(8,128)S(1)}, u32[]{:S(2)}, u32[]{:S(2)}) collective-permute-start(f32[264,384]{1,0:T(8,128)S(1)} %get-tuple-element.49), channel_id=1, source_target_pairs={{0,16},{16,0},{32,48},{48,32},{64,80},{80,64},{96,112},{112,96},{1... | collective-permute-start | bytes 1216520 | tf_op jit(solution)/shard_map/ppermute | solution.py:34
  123.7 2.2 %attention.1 = (bf16[256,384]{1,0:T(8,128)(2,1)}, bf16[256,384]{1,0:T(8,128)(2,1)}, bf16[256,384]{1,0:T(8,128)(2,1)}, f32[1,32]{1,0:T(1,128)}) custom-call(s32[1]{0:T(128)S(6)} %copy.42.group, f32[264,384]{1,0:T(8,128)S(1)} %get-tuple-element.48.mine_ref, f32[264,384]{1,0:T(8,128)S(1)} %collective-permute-done.17.got_ref, ...), custom_call_target="tpu_custom_call" | custom-call | flops 201326592 | bytes 3145728 | tf_op jit(solution)/shard_map/attention/pallas_call | solution.py:232
  (56 shorter events, 9.6 us)
Async XLA Ops:
  1.7 35.0 %collective-permute-start.2 = (bf16[2,96,256]{2,1,0:T(8,128)(2,1)S(1)}, bf16[2,96,256]{2,1,0:T(8,128)(2,1)S(1)}, u32[]{:S(2)}, u32[]{:S(2)}) collective-permute-start(bf16[2,96,256]{2,1,0:T(8,128)(2,1)S(1)} %fusion), channel_id=1, source_target_pairs={{0,16},{16,0},{32,48},{48,32},{64,80},{80,64},{96,112},{112,96},{1... | collective-permute-start | bytes 294920 | tf_op jit(solution)/shard_map/ppermute | solution.py:34
  20.0 18.7 %collective-permute-start = (bf16[112,384]{1,0:T(8,128)(2,1)S(1)}, bf16[112,384]{1,0:T(8,128)(2,1)S(1)}, u32[]{:S(2)}, u32[]{:S(2)}) collective-permute-start(bf16[112,384]{1,0:T(8,128)(2,1)S(1)} %make_unit.1.refs_0_), channel_id=1, source_target_pairs={{0,352},{16,688},{32,384},{48,720},{64,416},{80,752},{96,448},{112... | collective-permute-start | bytes 258056 | tf_op jit(solution)/shard_map/ppermute | solution.py:30
  32.6 23.3 %collective-permute-start.1 = (bf16[112,384]{1,0:T(8,128)(2,1)S(1)}, bf16[112,384]{1,0:T(8,128)(2,1)S(1)}, u32[]{:S(2)}, u32[]{:S(2)}) collective-permute-start(bf16[112,384]{1,0:T(8,128)(2,1)S(1)} %make_unit.1.refs_0_), channel_id=1, source_target_pairs={{0,672},{16,368},{32,704},{48,400},{64,736},{80,432},{96,768},{112... | collective-permute-start | bytes 258056 | tf_op jit(solution)/shard_map/ppermute | solution.py:30
  36.8 19.2 %collective-permute-start.3 = (bf16[192,512]{1,0:T(8,128)(2,1)S(1)}, bf16[192,512]{1,0:T(8,128)(2,1)S(1)}, u32[]{:S(2)}, u32[]{:S(2)}) collective-permute-start(bf16[192,512]{1,0:T(8,128)(2,1)S(1)} %bitcast.36), channel_id=1, source_target_pairs={{0,4},{1,5},{2,6},{3,7},{4,0},{5,1},{6,2},{7,3},{8,12},{9,13},{10,... | collective-permute-start | bytes 589832 | tf_op jit(solution)/shard_map/ppermute | solution.py:45
  56.0 10.7 %collective-permute-start.7 = (bf16[304,384]{1,0:T(8,128)(2,1)S(1)}, bf16[304,384]{1,0:T(8,128)(2,1)S(1)}, u32[]{:S(2)}, u32[]{:S(2)}) collective-permute-start(bf16[304,384]{1,0:T(8,128)(2,1)S(1)} %join_units.1.refs_2_), channel_id=1, source_target_pairs={{0,32},{16,1008},{32,64},{48,16},{64,96},{80,48},{96,128},{112,80}... | collective-permute-start | bytes 700424 | tf_op jit(solution)/shard_map/ppermute | solution.py:30
  58.0 12.3 %collective-permute-start.8 = (bf16[304,384]{1,0:T(8,128)(2,1)S(1)}, bf16[304,384]{1,0:T(8,128)(2,1)S(1)}, u32[]{:S(2)}, u32[]{:S(2)}) collective-permute-start(bf16[304,384]{1,0:T(8,128)(2,1)S(1)} %join_units.1.refs_2_), channel_id=1, source_target_pairs={{0,992},{16,48},{32,0},{48,80},{64,32},{80,112},{96,64},{112,144},... | collective-permute-start | bytes 700424 | tf_op jit(solution)/shard_map/ppermute | solution.py:30
  61.9 14.9 %collective-permute-start.4 = (bf16[384,512]{1,0:T(8,128)(2,1)S(1)}, bf16[384,512]{1,0:T(8,128)(2,1)S(1)}, u32[]{:S(2)}, u32[]{:S(2)}) collective-permute-start(bf16[384,512]{1,0:T(8,128)(2,1)S(1)} %stack.3.refs_0_), channel_id=1, source_target_pairs={{0,12},{1,13},{2,14},{3,15},{4,8},{5,9},{6,10},{7,11},{8,4},{9,5},... | collective-permute-start | bytes 1179656 | tf_op jit(solution)/shard_map/ppermute | solution.py:45
  70.3 10.3 %copy-start.2 = (bf16[304,384]{1,0:T(8,128)(2,1)}, bf16[304,384]{1,0:T(8,128)(2,1)S(1)}, u32[]{:S(2)}) copy-start(bf16[304,384]{1,0:T(8,128)(2,1)S(1)} %get-tuple-element.38.refs_3_) | copy-start | bytes 700420
  70.3 10.3 %copy-start.4 = (bf16[304,384]{1,0:T(8,128)(2,1)}, bf16[304,384]{1,0:T(8,128)(2,1)S(1)}, u32[]{:S(2)}) copy-start(bf16[304,384]{1,0:T(8,128)(2,1)S(1)} %get-tuple-element.39.refs_4_) | copy-start | bytes 700420
  70.3 10.3 %collective-permute-start.10 = (bf16[304,384]{1,0:T(8,128)(2,1)S(1)}, bf16[304,384]{1,0:T(8,128)(2,1)}, u32[]{:S(2)}, u32[]{:S(2)}) collective-permute-start(bf16[304,384]{1,0:T(8,128)(2,1)S(1)} %get-tuple-element.39.refs_4_), channel_id=1, source_target_pairs={{0,992},{16,48},{32,0},{48,80},{64,32},{80,112},{96,64},{112,144},... | collective-permute-start | bytes 700424 | tf_op jit(solution)/shard_map/ppermute | solution.py:30
  72.2 8.4 %collective-permute-start.9 = (bf16[304,384]{1,0:T(8,128)(2,1)S(1)}, bf16[304,384]{1,0:T(8,128)(2,1)}, u32[]{:S(2)}, u32[]{:S(2)}) collective-permute-start(bf16[304,384]{1,0:T(8,128)(2,1)S(1)} %get-tuple-element.38.refs_3_), channel_id=1, source_target_pairs={{0,32},{16,1008},{32,64},{48,16},{64,96},{80,48},{96,128},{112,80}... | collective-permute-start | bytes 700424 | tf_op jit(solution)/shard_map/ppermute | solution.py:30
  76.9 13.1 %collective-permute-start.5 = (bf16[768,512]{1,0:T(8,128)(2,1)S(1)}, bf16[768,512]{1,0:T(8,128)(2,1)S(1)}, u32[]{:S(2)}, u32[]{:S(2)}) collective-permute-start(bf16[768,512]{1,0:T(8,128)(2,1)S(1)} %stack.4.refs_0_), channel_id=1, source_target_pairs={{0,1},{1,0},{2,3},{3,2},{4,5},{5,4},{6,7},{7,6},{8,9},{9,8},{10,11... | collective-permute-start | bytes 2359304 | tf_op jit(solution)/shard_map/ppermute | solution.py:45
  80.6 14.0 %collective-permute-start.11 = (bf16[304,384]{1,0:T(8,128)(2,1)}, bf16[304,384]{1,0:T(8,128)(2,1)}, u32[]{:S(2)}, u32[]{:S(2)}) collective-permute-start(bf16[304,384]{1,0:T(8,128)(2,1)} %get-tuple-element.40.refs_5_), channel_id=1, source_target_pairs={{0,32},{16,1008},{32,64},{48,16},{64,96},{80,48},{96,128},{112,80}... | collective-permute-start | bytes 700424 | tf_op jit(solution)/shard_map/ppermute | solution.py:30
  84.9 9.7 %collective-permute-start.12 = (bf16[304,384]{1,0:T(8,128)(2,1)}, bf16[304,384]{1,0:T(8,128)(2,1)}, u32[]{:S(2)}, u32[]{:S(2)}) collective-permute-start(bf16[304,384]{1,0:T(8,128)(2,1)} %get-tuple-element.41.refs_6_), channel_id=1, source_target_pairs={{0,992},{16,48},{32,0},{48,80},{64,32},{80,112},{96,64},{112,144},... | collective-permute-start | bytes 700424 | tf_op jit(solution)/shard_map/ppermute | solution.py:30
  90.1 9.9 %copy-start.9 = (s32[32]{0:T(128)S(1)}, s32[32]{0:T(128)}, u32[]{:S(2)}) copy-start(s32[32]{0:T(128)} %constant.113.clone) | copy-start | bytes 388
  90.1 9.9 %copy-start.10 = (s32[32]{0:T(128)S(1)}, s32[32]{0:T(128)}, u32[]{:S(2)}) copy-start(s32[32]{0:T(128)} %constant.117) | copy-start | bytes 388
  90.1 22.7 %collective-permute-start.6 = (bf16[1536,512]{1,0:T(8,128)(2,1)S(1)}, bf16[1536,512]{1,0:T(8,128)(2,1)S(1)}, u32[]{:S(2)}, u32[]{:S(2)}) collective-permute-start(bf16[1536,512]{1,0:T(8,128)(2,1)S(1)} %stack.5.refs_0_), channel_id=1, source_target_pairs={{0,3},{1,2},{2,1},{3,0},{4,7},{5,6},{6,5},{7,4},{8,11},{9,10},{10,... | collective-permute-start | bytes 4718600 | tf_op jit(solution)/shard_map/ppermute | solution.py:45
  94.7 8.2 %collective-permute-start.13 = (bf16[304,384]{1,0:T(8,128)(2,1)}, bf16[304,384]{1,0:T(8,128)(2,1)}, u32[]{:S(2)}, u32[]{:S(2)}) collective-permute-start(bf16[304,384]{1,0:T(8,128)(2,1)} %get-tuple-element.42.refs_7_), channel_id=1, source_target_pairs={{0,32},{16,1008},{32,64},{48,16},{64,96},{80,48},{96,128},{112,80}... | collective-permute-start | bytes 700424 | tf_op jit(solution)/shard_map/ppermute | solution.py:30
  96.6 8.8 %collective-permute-start.14 = (bf16[304,384]{1,0:T(8,128)(2,1)}, bf16[304,384]{1,0:T(8,128)(2,1)}, u32[]{:S(2)}, u32[]{:S(2)}) collective-permute-start(bf16[304,384]{1,0:T(8,128)(2,1)} %get-tuple-element.43.refs_8_), channel_id=1, source_target_pairs={{0,992},{16,48},{32,0},{48,80},{64,32},{80,112},{96,64},{112,144},... | collective-permute-start | bytes 700424 | tf_op jit(solution)/shard_map/ppermute | solution.py:30
  100.0 12.7 %copy-start.3 = (bf16[304,384]{1,0:T(8,128)(2,1)S(1)}, bf16[304,384]{1,0:T(8,128)(2,1)}, u32[]{:S(2)}) copy-start(bf16[304,384]{1,0:T(8,128)(2,1)} %copy-done.2) | copy-start | bytes 700420
  100.1 12.7 %copy-start.5 = (bf16[304,384]{1,0:T(8,128)(2,1)S(1)}, bf16[304,384]{1,0:T(8,128)(2,1)}, u32[]{:S(2)}) copy-start(bf16[304,384]{1,0:T(8,128)(2,1)} %copy-done.4) | copy-start | bytes 700420
  106.3 12.3 %collective-permute-start.15 = (bf16[208,384]{1,0:T(8,128)(2,1)S(1)}, bf16[208,384]{1,0:T(8,128)(2,1)S(1)}, u32[]{:S(2)}, u32[]{:S(2)}) collective-permute-start(bf16[208,384]{1,0:T(8,128)(2,1)S(1)} %slice.13), channel_id=1, source_target_pairs={{0,32},{16,1008},{32,64},{48,16},{64,96},{80,48},{96,128},{112,80}... | collective-permute-start | bytes 479240 | tf_op jit(solution)/shard_map/ppermute | solution.py:30
  108.6 10.0 %collective-permute-start.16 = (bf16[304,384]{1,0:T(8,128)(2,1)}, bf16[304,384]{1,0:T(8,128)(2,1)S(1)}, u32[]{:S(2)}, u32[]{:S(2)}) collective-permute-start(bf16[304,384]{1,0:T(8,128)(2,1)} %get-tuple-element.45.refs_10_), channel_id=1, source_target_pairs={{0,992},{16,48},{32,0},{48,80},{64,32},{80,112},{96,64},{112,144},... | collective-permute-start | bytes 700424 | tf_op jit(solution)/shard_map/ppermute | solution.py:30
  119.8 3.8 %collective-permute-start.17 = (f32[264,384]{1,0:T(8,128)S(1)}, f32[264,384]{1,0:T(8,128)S(1)}, u32[]{:S(2)}, u32[]{:S(2)}) collective-permute-start(f32[264,384]{1,0:T(8,128)S(1)} %get-tuple-element.49), channel_id=1, source_target_pairs={{0,16},{16,0},{32,48},{48,32},{64,80},{80,64},{96,112},{112,96},{1... | collective-permute-start | bytes 1216520 | tf_op jit(solution)/shard_map/ppermute | solution.py:34
  (5 other events, 17.1 us)

commit v7 on v5

--- a/solution.py
+++ b/solution.py
@@ -45,7 +45,6 @@
 
 
 def gather(unit, block, pairs_z):
-    tie = lax.optimization_barrier
     mine = along_z(unit, FAR, -FAR, pairs_z)
     opposite = along_z(unit, -FAR, FAR, pairs_z)
     passed = exchange(block, 1, True, pairs_z)
@@ -54,9 +53,8 @@
     block = stack([block, passed])
     passed = exchange(block, 3, True, pairs_z)
     (farthest,) = meet(4, farthest)
-    farthest, passed, block = tie((farthest, passed, block))
+    bundle = join_units(unit, opposite, farthest, mine)
     block = stack([block, passed])
-    bundle = join_units(unit, opposite, farthest, mine)
     pieces = [bundle]
     p = q = bundle
     for step, wait in enumerate((6, 6, 8)):
@@ -64,13 +62,15 @@
         q = along_z(q, -1, 1, pairs_z)
         if step < 2:
             passed = exchange(block, 1 + 2 * step, False, pairs_z)
-        p, q = meet(wait, p, q)
+        if step < 2:
+            p, q = meet(wait, p, q)
         if step == 0:
             block = stack([block, passed])
         pieces += [p, q]
     half = passed
-    p = along_z(p[:HALF], 1, -1, pairs_z)
-    q = along_z(q[UNIT : UNIT + HALF], -1, 1, pairs_z)
+    p, q = cut(wait, p, q)
+    p = along_z(p, 1, -1, pairs_z)
+    q = along_z(q, -1, 1, pairs_z)
     return pieces + [p, q], [block, half]
 
 
@@ -116,6 +116,17 @@
     half = len(refs) // 2
     for given, out in zip(refs[:half], refs[half:]):
         out[...] = given[...]
+
+
+def cut_kernel(p_ref, q_ref, p_out, q_out, p_sem, q_sem):
+    copies = (
+        pltpu.make_async_copy(p_ref.at[pl.ds(0, HALF), :], p_out, p_sem),
+        pltpu.make_async_copy(q_ref.at[pl.ds(UNIT, HALF), :], q_out, q_sem),
+    )
+    for copy in copies:
+        copy.start()
+    for copy in copies:
+        copy.wait()
 
 
 def stack_kernel(*refs):
@@ -267,6 +278,22 @@
     )(*arrays)
 
 
+def cut(microseconds, p, q):
+    shape = jax.ShapeDtypeStruct((HALF, p.shape[1]), p.dtype)
+    return pl.pallas_call(
+        cut_kernel,
+        out_shape=(shape, shape),
+        in_specs=[pl.BlockSpec(memory_space=pl.ANY)] * 2,
+        out_specs=(VM, VM),
+        scratch_shapes=[pltpu.SemaphoreType.DMA, pltpu.SemaphoreType.DMA],
+        compiler_params=pltpu.CompilerParams(vmem_limit_bytes=4 * 2**20),
+        cost_estimate=pl.CostEstimate(
+            flops=microseconds * 10**9, bytes_accessed=0, transcendentals=0
+        ),
+        name="cut",
+    )(p, q)
+
+
 def stack(blocks):
     rows, width = blocks[0].shape
     shape = jax.ShapeDtypeStruct((len(blocks) * rows, width), blocks[0].dtype)

time: 127 us -> 125 us (0.984); the launches traced: 126 us -> 122 us
  waiting for transfers between devices: 32.4 us -> 29.1 us
  local copies, waits for them, and re-layouts: 3.84 us -> 1.97 us
    ppermute x11, waiting for transfers between devices: 28.3 us -> 25.7 us  [along_z(): return lax.ppermute(x, 'dp', pairs)]
    slice x2 -> x0, local copies, waits for them, and re-layouts: 1.86 us -> none  [the longest x1 0.93 us: gather(): q = along_z(q[UNIT:UNIT + HALF], -1, 1, pairs_z)]
  transfers between devices with their start and end apart: 17 -> 17, of which waited for: 10 -> 10; matrix products, arithmetic and copies ran while one was open for 2% -> 0% of each run, Pallas kernels for 4% -> 5%
where the time goes in v7:
time: 125 us; the launch traced here: 122 us
  starting transfers between devices  79.3 us (63%)
  waiting for transfers between devices  29.1 us (23%)
  Pallas kernels  9.3 us (7%)
  between operations  2.32 us (2%)
  local copies, waits for them, and re-layouts  1.97 us (2%)
    ppermute x11, starting transfers between devices, along_z(): return lax.ppermute(x, 'dp', pairs)  49.3 us
    ppermute x11, waiting for transfers between devices, along_z(): return lax.ppermute(x, 'dp', pairs)  25.7 us
    ppermute x2, starting transfers between devices, to_sibling(): return lax.ppermute(x, 'dp', [(i, i ^ 1) for i in range(2 * pairs_z)])  18.3 us
    ppermute x4, starting transfers between devices, exchange(): return lax.ppermute(x, ALL, pairs)  11.7 us
    pallas_call x9, Pallas kernels, call(): pl.pallas_call(kernel, out_shape=out_shape, in_specs=[SM] * scalars + [VM...  8.29 us
  transfers between devices with their start and end apart: 17, of which 10 were waited for; matrix products, arithmetic and copies ran while one was open for 0% of the time, Pallas kernels for 5%

profile of v7, /device:TPU:1, one launch (start us, length us, event | category | flops | bytes accessed | tf_op | source)
XLA Modules:
  0.0 122.1 jit_solution(2911167882367767883)
XLA Ops:
  1.7 16.1 %collective-permute-start = (bf16[2,96,256]{2,1,0:T(8,128)(2,1)S(1)}, bf16[2,96,256]{2,1,0:T(8,128)(2,1)S(1)}, u32[]{:S(2)}, u32[]{:S(2)}) collective-permute-start(bf16[2,96,256]{2,1,0:T(8,128)(2,1)S(1)} %fusion), channel_id=1, source_target_pairs={{0,16},{16,0},{32,48},{48,32},{64,80},{80,64},{96,112},{112,96},{1... | collective-permute-start | bytes 294920 | tf_op jit(solution)/shard_map/ppermute | solution.py:33
  20.0 10.1 %collective-permute-start.5 = (bf16[112,384]{1,0:T(8,128)(2,1)S(1)}, bf16[112,384]{1,0:T(8,128)(2,1)S(1)}, u32[]{:S(2)}, u32[]{:S(2)}) collective-permute-start(bf16[112,384]{1,0:T(8,128)(2,1)S(1)} %make_unit.1.refs_0_), channel_id=1, source_target_pairs={{0,256},{16,784},{32,288},{48,816},{64,320},{80,848},{96,352},{112... | collective-permute-start | bytes 258056 | tf_op jit(solution)/shard_map/ppermute | solution.py:29
  30.1 3.9 %collective-permute-start.6 = (bf16[112,384]{1,0:T(8,128)(2,1)S(1)}, bf16[112,384]{1,0:T(8,128)(2,1)S(1)}, u32[]{:S(2)}, u32[]{:S(2)}) collective-permute-start(bf16[112,384]{1,0:T(8,128)(2,1)S(1)} %make_unit.1.refs_0_), channel_id=1, source_target_pairs={{0,768},{16,272},{32,800},{48,304},{64,832},{80,336},{96,864},{112... | collective-permute-start | bytes 258056 | tf_op jit(solution)/shard_map/ppermute | solution.py:29
  36.3 8.6 %collective-permute-done.6.refs_1_ = bf16[112,384]{1,0:T(8,128)(2,1)S(1)} collective-permute-done((bf16[112,384]{1,0:T(8,128)(2,1)S(1)}, bf16[112,384]{1,0:T(8,128)(2,1)S(1)}, u32[]{:S(2)}, u32[]{:S(2)}) %collective-permute-start.6) | collective-permute-done | bytes 86048 | tf_op jit(solution)/shard_map/ppermute | solution.py:29
  44.9 13.0 %collective-permute-start.7 = (bf16[112,384]{1,0:T(8,128)(2,1)S(1)}, bf16[112,384]{1,0:T(8,128)(2,1)S(1)}, u32[]{:S(2)}, u32[]{:S(2)}) collective-permute-start(bf16[112,384]{1,0:T(8,128)(2,1)S(1)} %get-tuple-element.23.refs_3_), channel_id=1, source_target_pairs={{0,256},{16,784},{32,288},{48,816},{64,320},{80,848},{96,352},{112... | collective-permute-start | bytes 258056 | tf_op jit(solution)/shard_map/ppermute | solution.py:29
  58.0 3.9 %collective-permute-start.2 = (bf16[384,512]{1,0:T(8,128)(2,1)S(1)}, bf16[384,512]{1,0:T(8,128)(2,1)S(1)}, u32[]{:S(2)}, u32[]{:S(2)}) collective-permute-start(bf16[384,512]{1,0:T(8,128)(2,1)S(1)} %stack.3.refs_0_), channel_id=1, source_target_pairs={{0,12},{1,13},{2,14},{3,15},{4,8},{5,9},{6,10},{7,11},{8,4},{9,5},... | collective-permute-start | bytes 1179656 | tf_op jit(solution)/shard_map/ppermute | solution.py:44
  61.9 2.9 %collective-permute-done.7.refs_0_ = bf16[112,384]{1,0:T(8,128)(2,1)S(1)} collective-permute-done((bf16[112,384]{1,0:T(8,128)(2,1)S(1)}, bf16[112,384]{1,0:T(8,128)(2,1)S(1)}, u32[]{:S(2)}, u32[]{:S(2)}) %collective-permute-start.7) | collective-permute-done | bytes 86048 | tf_op jit(solution)/shard_map/ppermute | solution.py:29
  64.8 2.0 %collective-permute-start.8 = (bf16[400,384]{1,0:T(8,128)(2,1)S(1)}, bf16[400,384]{1,0:T(8,128)(2,1)}, u32[]{:S(2)}, u32[]{:S(2)}) collective-permute-start(bf16[400,384]{1,0:T(8,128)(2,1)S(1)} %join_units.1.refs_2_), channel_id=1, source_target_pairs={{0,32},{16,1008},{32,64},{48,16},{64,96},{80,48},{96,128},{112,80}... | collective-permute-start | bytes 921608 | tf_op jit(solution)/shard_map/ppermute | solution.py:29
  66.8 4.5 %collective-permute-start.9 = (bf16[400,384]{1,0:T(8,128)(2,1)S(1)}, bf16[400,384]{1,0:T(8,128)(2,1)}, u32[]{:S(2)}, u32[]{:S(2)}) collective-permute-start(bf16[400,384]{1,0:T(8,128)(2,1)S(1)} %join_units.1.refs_2_), channel_id=1, source_target_pairs={{0,992},{16,48},{32,0},{48,80},{64,32},{80,112},{96,64},{112,144},... | collective-permute-start | bytes 921608 | tf_op jit(solution)/shard_map/ppermute | solution.py:29
  71.4 2.3 %collective-permute-start.3 = (bf16[768,512]{1,0:T(8,128)(2,1)S(1)}, bf16[768,512]{1,0:T(8,128)(2,1)S(1)}, u32[]{:S(2)}, u32[]{:S(2)}) collective-permute-start(bf16[768,512]{1,0:T(8,128)(2,1)S(1)} %stack.4.refs_0_), channel_id=1, source_target_pairs={{0,1},{1,0},{2,3},{3,2},{4,5},{5,4},{6,7},{7,6},{8,9},{9,8},{10,11... | collective-permute-start | bytes 2359304 | tf_op jit(solution)/shard_map/ppermute | solution.py:44
  73.7 3.1 %collective-permute-done.8.refs_0_ = bf16[400,384]{1,0:T(8,128)(2,1)} collective-permute-done((bf16[400,384]{1,0:T(8,128)(2,1)S(1)}, bf16[400,384]{1,0:T(8,128)(2,1)}, u32[]{:S(2)}, u32[]{:S(2)}) %collective-permute-start.8) | collective-permute-done | bytes 307232 | tf_op jit(solution)/shard_map/ppermute | solution.py:29
  78.7 3.4 %collective-permute-start.11 = (bf16[400,384]{1,0:T(8,128)(2,1)}, bf16[400,384]{1,0:T(8,128)(2,1)}, u32[]{:S(2)}, u32[]{:S(2)}) collective-permute-start(bf16[400,384]{1,0:T(8,128)(2,1)} %get-tuple-element.25.refs_4_), channel_id=1, source_target_pairs={{0,992},{16,48},{32,0},{48,80},{64,32},{80,112},{96,64},{112,144},... | collective-permute-start | bytes 921608 | tf_op jit(solution)/shard_map/ppermute | solution.py:29
  82.1 2.4 %collective-permute-done.3.refs_1_ = bf16[768,512]{1,0:T(8,128)(2,1)S(1)} collective-permute-done((bf16[768,512]{1,0:T(8,128)(2,1)S(1)}, bf16[768,512]{1,0:T(8,128)(2,1)S(1)}, u32[]{:S(2)}, u32[]{:S(2)}) %collective-permute-start.3) | collective-permute-done | bytes 786464 | tf_op jit(solution)/shard_map/ppermute | solution.py:44
  84.6 3.6 %collective-permute-start.4 = (bf16[1536,512]{1,0:T(8,128)(2,1)S(1)}, bf16[1536,512]{1,0:T(8,128)(2,1)S(1)}, u32[]{:S(2)}, u32[]{:S(2)}) collective-permute-start(bf16[1536,512]{1,0:T(8,128)(2,1)S(1)} %stack.5.refs_0_), channel_id=1, source_target_pairs={{0,3},{1,2},{2,1},{3,0},{4,7},{5,6},{6,5},{7,4},{8,11},{9,10},{10,... | collective-permute-start | bytes 4718600 | tf_op jit(solution)/shard_map/ppermute | solution.py:44
  88.2 2.3 %collective-permute-done.11.refs_1_ = bf16[400,384]{1,0:T(8,128)(2,1)} collective-permute-done((bf16[400,384]{1,0:T(8,128)(2,1)}, bf16[400,384]{1,0:T(8,128)(2,1)}, u32[]{:S(2)}, u32[]{:S(2)}) %collective-permute-start.11) | collective-permute-done | bytes 307232 | tf_op jit(solution)/shard_map/ppermute | solution.py:29
  90.6 2.8 %collective-permute-start.12 = (bf16[400,384]{1,0:T(8,128)(2,1)}, bf16[400,384]{1,0:T(8,128)(2,1)}, u32[]{:S(2)}, u32[]{:S(2)}) collective-permute-start(bf16[400,384]{1,0:T(8,128)(2,1)} %get-tuple-element.26.refs_5_), channel_id=1, source_target_pairs={{0,32},{16,1008},{32,64},{48,16},{64,96},{80,48},{96,128},{112,80}... | collective-permute-start | bytes 921608 | tf_op jit(solution)/shard_map/ppermute | solution.py:29
  93.4 2.4 %collective-permute-start.13 = (bf16[400,384]{1,0:T(8,128)(2,1)}, bf16[400,384]{1,0:T(8,128)(2,1)}, u32[]{:S(2)}, u32[]{:S(2)}) collective-permute-start(bf16[400,384]{1,0:T(8,128)(2,1)} %get-tuple-element.27.refs_6_), channel_id=1, source_target_pairs={{0,992},{16,48},{32,0},{48,80},{64,32},{80,112},{96,64},{112,144},... | collective-permute-start | bytes 921608 | tf_op jit(solution)/shard_map/ppermute | solution.py:29
  95.9 3.0 %collective-permute-done.12.p_ref.refs_7_ = bf16[400,384]{1,0:T(8,128)(2,1)} collective-permute-done((bf16[400,384]{1,0:T(8,128)(2,1)}, bf16[400,384]{1,0:T(8,128)(2,1)}, u32[]{:S(2)}, u32[]{:S(2)}) %collective-permute-start.12) | collective-permute-done | bytes 307232 | tf_op jit(solution)/shard_map/ppermute | solution.py:29
  98.9 4.8 %collective-permute-done.13.q_ref.refs_8_ = bf16[400,384]{1,0:T(8,128)(2,1)} collective-permute-done((bf16[400,384]{1,0:T(8,128)(2,1)}, bf16[400,384]{1,0:T(8,128)(2,1)}, u32[]{:S(2)}, u32[]{:S(2)}) %collective-permute-start.13) | collective-permute-done | bytes 307232 | tf_op jit(solution)/shard_map/ppermute | solution.py:29
  104.8 2.9 %collective-permute-start.14 = (bf16[208,384]{1,0:T(8,128)(2,1)S(1)}, bf16[208,384]{1,0:T(8,128)(2,1)S(1)}, u32[]{:S(2)}, u32[]{:S(2)}) collective-permute-start(bf16[208,384]{1,0:T(8,128)(2,1)S(1)} %get-tuple-element.28), channel_id=1, source_target_pairs={{0,32},{16,1008},{32,64},{48,16},{64,96},{80,48},{96,128},{112,80}... | collective-permute-start | bytes 479240 | tf_op jit(solution)/shard_map/ppermute | solution.py:29
  107.7 2.4 %collective-permute-start.15 = (bf16[208,384]{1,0:T(8,128)(2,1)S(1)}, bf16[208,384]{1,0:T(8,128)(2,1)S(1)}, u32[]{:S(2)}, u32[]{:S(2)}) collective-permute-start(bf16[208,384]{1,0:T(8,128)(2,1)S(1)} %get-tuple-element.29), channel_id=1, source_target_pairs={{0,992},{16,48},{32,0},{48,80},{64,32},{80,112},{96,64},{112,144},... | collective-permute-start | bytes 479240 | tf_op jit(solution)/shard_map/ppermute | solution.py:29
  110.1 4.4 %project_first.1 = (f32[512,384]{1,0:T(8,128)S(1)}, f32[16,384]{1,0:T(8,128)S(1)}) custom-call(s32[32]{0:T(128)S(1)} %fusion.8.starts, s32[32]{0:T(128)S(1)} %get-tuple-element.40.outers, bf16[1536,512]{1,0:T(8,128)(2,1)S(1)} %stack.5.refs_0_, bf16[1536,512]{1,0:T(8,128)(2,1)S(1)} %collective-permute-done.4.refs_1_, bf16[400,384]{1,0:T(8,128)(2,1)S(1)} %join_units.1.refs_2_, ...), custom_call_target="tpu_custom_call" | custom-call | flops 1056964608 | bytes 6291456 | tf_op jit(solution)/shard_map/project_first/pallas_call | solution.py:248
  116.3 2.2 %collective-permute-start.16 = (f32[264,384]{1,0:T(8,128)S(1)}, f32[264,384]{1,0:T(8,128)S(1)}, u32[]{:S(2)}, u32[]{:S(2)}) collective-permute-start(f32[264,384]{1,0:T(8,128)S(1)} %get-tuple-element.33), channel_id=1, source_target_pairs={{0,16},{16,0},{32,48},{48,32},{64,80},{80,64},{96,112},{112,96},{1... | collective-permute-start | bytes 1216520 | tf_op jit(solution)/shard_map/ppermute | solution.py:33
  120.0 2.2 %attention.1 = (bf16[256,384]{1,0:T(8,128)(2,1)}, bf16[256,384]{1,0:T(8,128)(2,1)}, bf16[256,384]{1,0:T(8,128)(2,1)}, f32[1,32]{1,0:T(1,128)}) custom-call(s32[1]{0:T(128)S(6)} %copy.36.group, f32[264,384]{1,0:T(8,128)S(1)} %get-tuple-element.32.mine_ref, f32[264,384]{1,0:T(8,128)S(1)} %collective-permute-done.16.got_ref, ...), custom_call_target="tpu_custom_call" | custom-call | flops 201326592 | bytes 3145728 | tf_op jit(solution)/shard_map/attention/pallas_call | solution.py:248
  (45 shorter events, 10.6 us)
Async XLA Ops:
  1.7 32.3 %collective-permute-start = (bf16[2,96,256]{2,1,0:T(8,128)(2,1)S(1)}, bf16[2,96,256]{2,1,0:T(8,128)(2,1)S(1)}, u32[]{:S(2)}, u32[]{:S(2)}) collective-permute-start(bf16[2,96,256]{2,1,0:T(8,128)(2,1)S(1)} %fusion), channel_id=1, source_target_pairs={{0,16},{16,0},{32,48},{48,32},{64,80},{80,64},{96,112},{112,96},{1... | collective-permute-start | bytes 294920 | tf_op jit(solution)/shard_map/ppermute | solution.py:33
  19.1 0.9 copy-start.3
  20.0 16.3 %collective-permute-start.5 = (bf16[112,384]{1,0:T(8,128)(2,1)S(1)}, bf16[112,384]{1,0:T(8,128)(2,1)S(1)}, u32[]{:S(2)}, u32[]{:S(2)}) collective-permute-start(bf16[112,384]{1,0:T(8,128)(2,1)S(1)} %make_unit.1.refs_0_), channel_id=1, source_target_pairs={{0,256},{16,784},{32,288},{48,816},{64,320},{80,848},{96,352},{112... | collective-permute-start | bytes 258056 | tf_op jit(solution)/shard_map/ppermute | solution.py:29
  30.1 14.8 %collective-permute-start.6 = (bf16[112,384]{1,0:T(8,128)(2,1)S(1)}, bf16[112,384]{1,0:T(8,128)(2,1)S(1)}, u32[]{:S(2)}, u32[]{:S(2)}) collective-permute-start(bf16[112,384]{1,0:T(8,128)(2,1)S(1)} %make_unit.1.refs_0_), channel_id=1, source_target_pairs={{0,768},{16,272},{32,800},{48,304},{64,832},{80,336},{96,864},{112... | collective-permute-start | bytes 258056 | tf_op jit(solution)/shard_map/ppermute | solution.py:29
  34.1 23.8 %collective-permute-start.1 = (bf16[192,512]{1,0:T(8,128)(2,1)S(1)}, bf16[192,512]{1,0:T(8,128)(2,1)S(1)}, u32[]{:S(2)}, u32[]{:S(2)}) collective-permute-start(bf16[192,512]{1,0:T(8,128)(2,1)S(1)} %bitcast.36), channel_id=1, source_target_pairs={{0,4},{1,5},{2,6},{3,7},{4,0},{5,1},{6,2},{7,3},{8,12},{9,13},{10,... | collective-permute-start | bytes 589832 | tf_op jit(solution)/shard_map/ppermute | solution.py:44
  44.9 19.9 %collective-permute-start.7 = (bf16[112,384]{1,0:T(8,128)(2,1)S(1)}, bf16[112,384]{1,0:T(8,128)(2,1)S(1)}, u32[]{:S(2)}, u32[]{:S(2)}) collective-permute-start(bf16[112,384]{1,0:T(8,128)(2,1)S(1)} %get-tuple-element.23.refs_3_), channel_id=1, source_target_pairs={{0,256},{16,784},{32,288},{48,816},{64,320},{80,848},{96,352},{112... | collective-permute-start | bytes 258056 | tf_op jit(solution)/shard_map/ppermute | solution.py:29
  58.0 13.4 %collective-permute-start.2 = (bf16[384,512]{1,0:T(8,128)(2,1)S(1)}, bf16[384,512]{1,0:T(8,128)(2,1)S(1)}, u32[]{:S(2)}, u32[]{:S(2)}) collective-permute-start(bf16[384,512]{1,0:T(8,128)(2,1)S(1)} %stack.3.refs_0_), channel_id=1, source_target_pairs={{0,12},{1,13},{2,14},{3,15},{4,8},{5,9},{6,10},{7,11},{8,4},{9,5},... | collective-permute-start | bytes 1179656 | tf_op jit(solution)/shard_map/ppermute | solution.py:44
  64.8 12.0 %collective-permute-start.8 = (bf16[400,384]{1,0:T(8,128)(2,1)S(1)}, bf16[400,384]{1,0:T(8,128)(2,1)}, u32[]{:S(2)}, u32[]{:S(2)}) collective-permute-start(bf16[400,384]{1,0:T(8,128)(2,1)S(1)} %join_units.1.refs_2_), channel_id=1, source_target_pairs={{0,32},{16,1008},{32,64},{48,16},{64,96},{80,48},{96,128},{112,80}... | collective-permute-start | bytes 921608 | tf_op jit(solution)/shard_map/ppermute | solution.py:29
  66.8 10.0 %collective-permute-start.9 = (bf16[400,384]{1,0:T(8,128)(2,1)S(1)}, bf16[400,384]{1,0:T(8,128)(2,1)}, u32[]{:S(2)}, u32[]{:S(2)}) collective-permute-start(bf16[400,384]{1,0:T(8,128)(2,1)S(1)} %join_units.1.refs_2_), channel_id=1, source_target_pairs={{0,992},{16,48},{32,0},{48,80},{64,32},{80,112},{96,64},{112,144},... | collective-permute-start | bytes 921608 | tf_op jit(solution)/shard_map/ppermute | solution.py:29
  71.4 13.1 %collective-permute-start.3 = (bf16[768,512]{1,0:T(8,128)(2,1)S(1)}, bf16[768,512]{1,0:T(8,128)(2,1)S(1)}, u32[]{:S(2)}, u32[]{:S(2)}) collective-permute-start(bf16[768,512]{1,0:T(8,128)(2,1)S(1)} %stack.4.refs_0_), channel_id=1, source_target_pairs={{0,1},{1,0},{2,3},{3,2},{4,5},{5,4},{6,7},{7,6},{8,9},{9,8},{10,11... | collective-permute-start | bytes 2359304 | tf_op jit(solution)/shard_map/ppermute | solution.py:44
  76.8 11.4 %collective-permute-start.10 = (bf16[400,384]{1,0:T(8,128)(2,1)}, bf16[400,384]{1,0:T(8,128)(2,1)}, u32[]{:S(2)}, u32[]{:S(2)}) collective-permute-start(bf16[400,384]{1,0:T(8,128)(2,1)} %get-tuple-element.24.refs_3_), channel_id=1, source_target_pairs={{0,32},{16,1008},{32,64},{48,16},{64,96},{80,48},{96,128},{112,80}... | collective-permute-start | bytes 921608 | tf_op jit(solution)/shard_map/ppermute | solution.py:29
  78.7 11.8 %collective-permute-start.11 = (bf16[400,384]{1,0:T(8,128)(2,1)}, bf16[400,384]{1,0:T(8,128)(2,1)}, u32[]{:S(2)}, u32[]{:S(2)}) collective-permute-start(bf16[400,384]{1,0:T(8,128)(2,1)} %get-tuple-element.25.refs_4_), channel_id=1, source_target_pairs={{0,992},{16,48},{32,0},{48,80},{64,32},{80,112},{96,64},{112,144},... | collective-permute-start | bytes 921608 | tf_op jit(solution)/shard_map/ppermute | solution.py:29
  84.6 11.2 %copy-start.5 = (s32[32]{0:T(128)S(1)}, s32[32]{0:T(128)}, u32[]{:S(2)}) copy-start(s32[32]{0:T(128)} %constant.113.clone) | copy-start | bytes 388
  84.6 11.2 %copy-start.6 = (s32[32]{0:T(128)S(1)}, s32[32]{0:T(128)}, u32[]{:S(2)}) copy-start(s32[32]{0:T(128)} %constant.117) | copy-start | bytes 388
  84.6 25.5 %collective-permute-start.4 = (bf16[1536,512]{1,0:T(8,128)(2,1)S(1)}, bf16[1536,512]{1,0:T(8,128)(2,1)S(1)}, u32[]{:S(2)}, u32[]{:S(2)}) collective-permute-start(bf16[1536,512]{1,0:T(8,128)(2,1)S(1)} %stack.5.refs_0_), channel_id=1, source_target_pairs={{0,3},{1,2},{2,1},{3,0},{4,7},{5,6},{6,5},{7,4},{8,11},{9,10},{10,... | collective-permute-start | bytes 4718600 | tf_op jit(solution)/shard_map/ppermute | solution.py:44
  90.6 8.4 %collective-permute-start.12 = (bf16[400,384]{1,0:T(8,128)(2,1)}, bf16[400,384]{1,0:T(8,128)(2,1)}, u32[]{:S(2)}, u32[]{:S(2)}) collective-permute-start(bf16[400,384]{1,0:T(8,128)(2,1)} %get-tuple-element.26.refs_5_), channel_id=1, source_target_pairs={{0,32},{16,1008},{32,64},{48,16},{64,96},{80,48},{96,128},{112,80}... | collective-permute-start | bytes 921608 | tf_op jit(solution)/shard_map/ppermute | solution.py:29
  93.4 10.4 %collective-permute-start.13 = (bf16[400,384]{1,0:T(8,128)(2,1)}, bf16[400,384]{1,0:T(8,128)(2,1)}, u32[]{:S(2)}, u32[]{:S(2)}) collective-permute-start(bf16[400,384]{1,0:T(8,128)(2,1)} %get-tuple-element.27.refs_6_), channel_id=1, source_target_pairs={{0,992},{16,48},{32,0},{48,80},{64,32},{80,112},{96,64},{112,144},... | collective-permute-start | bytes 921608 | tf_op jit(solution)/shard_map/ppermute | solution.py:29
  104.8 9.7 %collective-permute-start.14 = (bf16[208,384]{1,0:T(8,128)(2,1)S(1)}, bf16[208,384]{1,0:T(8,128)(2,1)S(1)}, u32[]{:S(2)}, u32[]{:S(2)}) collective-permute-start(bf16[208,384]{1,0:T(8,128)(2,1)S(1)} %get-tuple-element.28), channel_id=1, source_target_pairs={{0,32},{16,1008},{32,64},{48,16},{64,96},{80,48},{96,128},{112,80}... | collective-permute-start | bytes 479240 | tf_op jit(solution)/shard_map/ppermute | solution.py:29
  107.7 7.4 %collective-permute-start.15 = (bf16[208,384]{1,0:T(8,128)(2,1)S(1)}, bf16[208,384]{1,0:T(8,128)(2,1)S(1)}, u32[]{:S(2)}, u32[]{:S(2)}) collective-permute-start(bf16[208,384]{1,0:T(8,128)(2,1)S(1)} %get-tuple-element.29), channel_id=1, source_target_pairs={{0,992},{16,48},{32,0},{48,80},{64,32},{80,112},{96,64},{112,144},... | collective-permute-start | bytes 479240 | tf_op jit(solution)/shard_map/ppermute | solution.py:29
  115.1 3.4 %copy-start = (bf16[256,384]{1,0:T(8,128)(2,1)S(1)}, bf16[256,384]{1,0:T(8,128)(2,1)}, u32[]{:S(2)}) copy-start(bf16[256,384]{1,0:T(8,128)(2,1)} %q_ref.3) | copy-start | bytes 589828
  115.1 3.5 %copy-start.1 = (bf16[256,384]{1,0:T(8,128)(2,1)S(1)}, bf16[256,384]{1,0:T(8,128)(2,1)}, u32[]{:S(2)}) copy-start(bf16[256,384]{1,0:T(8,128)(2,1)} %k_ref.3) | copy-start | bytes 589828
  115.1 3.5 %copy-start.4 = (f32[32]{0:T(128)S(1)}, f32[32]{0:T(128)}, u32[]{:S(2)}) copy-start(f32[32]{0:T(128)} %param.16) | copy-start | bytes 388
  115.1 4.8 %copy-start.2 = (bf16[256,384]{1,0:T(8,128)(2,1)S(1)}, bf16[256,384]{1,0:T(8,128)(2,1)}, u32[]{:S(2)}) copy-start(bf16[256,384]{1,0:T(8,128)(2,1)} %v_ref.1) | copy-start | bytes 589828
  116.3 3.6 %collective-permute-start.16 = (f32[264,384]{1,0:T(8,128)S(1)}, f32[264,384]{1,0:T(8,128)S(1)}, u32[]{:S(2)}, u32[]{:S(2)}) collective-permute-start(f32[264,384]{1,0:T(8,128)S(1)} %get-tuple-element.33), channel_id=1, source_target_pairs={{0,16},{16,0},{32,48},{48,32},{64,80},{80,64},{96,112},{112,96},{1... | collective-permute-start | bytes 1216520 | tf_op jit(solution)/shard_map/ppermute | solution.py:33

commit v8 on v7

--- a/solution.py
+++ b/solution.py
@@ -48,11 +48,12 @@
     mine = along_z(unit, FAR, -FAR, pairs_z)
     opposite = along_z(unit, -FAR, FAR, pairs_z)
     passed = exchange(block, 1, True, pairs_z)
-    mine, opposite = meet(2, mine, opposite)
+    (mine,) = meet(2, mine)
     farthest = along_z(mine, FAR, -FAR, pairs_z)
     block = stack([block, passed])
     passed = exchange(block, 3, True, pairs_z)
-    (farthest,) = meet(4, farthest)
+    (opposite,) = meet(1, opposite)
+    farthest, opposite = meet(4, farthest, opposite)
     bundle = join_units(unit, opposite, farthest, mine)
     block = stack([block, passed])
     pieces = [bundle]

time: 125 us -> 123 us (0.984)
  the two profiles are of different devices: /device:TPU:1 before, /device:TPU:113 now
where the time goes in v8:
time: 123 us; the launch traced here: 122 us
  starting transfers between devices  90.1 us (73%)
  waiting for transfers between devices  18.2 us (15%)
  Pallas kernels  9.26 us (8%)
  between operations  2.38 us (2%)
  local copies, waits for them, and re-layouts  1.98 us (2%)
    ppermute x11, starting transfers between devices, along_z(): return lax.ppermute(x, 'dp', pairs)  61.4 us
    ppermute x11, waiting for transfers between devices, along_z(): return lax.ppermute(x, 'dp', pairs)  17.1 us
    ppermute x2, starting transfers between devices, to_sibling(): return lax.ppermute(x, 'dp', [(i, i ^ 1) for i in range(2 * pairs_z)])  16.2 us
    ppermute x4, starting transfers between devices, exchange(): return lax.ppermute(x, ALL, pairs)  12.5 us
    pallas_call x9, Pallas kernels, call(): pl.pallas_call(kernel, out_shape=out_shape, in_specs=[SM] * scalars + [VM...  8.25 us
  transfers between devices with their start and end apart: 17, of which 8 were waited for; matrix products, arithmetic and copies ran while one was open for 0% of the time, Pallas kernels for 5%

profile of v8, /device:TPU:113, one launch (start us, length us, event | category | flops | bytes accessed | tf_op | source)
XLA Modules:
  0.0 121.9 jit_solution(15115301288255795240)
XLA Ops:
  1.7 2.6 %collective-permute-start = (bf16[2,96,256]{2,1,0:T(8,128)(2,1)S(1)}, bf16[2,96,256]{2,1,0:T(8,128)(2,1)S(1)}, u32[]{:S(2)}, u32[]{:S(2)}) collective-permute-start(bf16[2,96,256]{2,1,0:T(8,128)(2,1)S(1)} %fusion), channel_id=1, source_target_pairs={{0,16},{16,0},{32,48},{48,32},{64,80},{80,64},{96,112},{112,96},{1... | collective-permute-start | bytes 294920 | tf_op jit(solution)/shard_map/ppermute | solution.py:33
  6.5 20.0 %collective-permute-start.5 = (bf16[112,384]{1,0:T(8,128)(2,1)S(1)}, bf16[112,384]{1,0:T(8,128)(2,1)S(1)}, u32[]{:S(2)}, u32[]{:S(2)}) collective-permute-start(bf16[112,384]{1,0:T(8,128)(2,1)S(1)} %make_unit.1.refs_0_), channel_id=1, source_target_pairs={{0,256},{16,784},{32,288},{48,816},{64,320},{80,848},{96,352},{112... | collective-permute-start | bytes 258056 | tf_op jit(solution)/shard_map/ppermute | solution.py:29
  26.6 1.9 %collective-permute-start.7 = (bf16[112,384]{1,0:T(8,128)(2,1)S(1)}, bf16[112,384]{1,0:T(8,128)(2,1)S(1)}, u32[]{:S(2)}, u32[]{:S(2)}) collective-permute-start(bf16[112,384]{1,0:T(8,128)(2,1)S(1)} %make_unit.1.refs_0_), channel_id=1, source_target_pairs={{0,768},{16,272},{32,800},{48,304},{64,832},{80,336},{96,864},{112... | collective-permute-start | bytes 258056 | tf_op jit(solution)/shard_map/ppermute | solution.py:29
  28.5 2.9 %collective-permute-start.1 = (bf16[192,512]{1,0:T(8,128)(2,1)S(1)}, bf16[192,512]{1,0:T(8,128)(2,1)S(1)}, u32[]{:S(2)}, u32[]{:S(2)}) collective-permute-start(bf16[192,512]{1,0:T(8,128)(2,1)S(1)} %bitcast.36), channel_id=1, source_target_pairs={{0,4},{1,5},{2,6},{3,7},{4,0},{5,1},{6,2},{7,3},{8,12},{9,13},{10,... | collective-permute-start | bytes 589832 | tf_op jit(solution)/shard_map/ppermute | solution.py:44
  31.5 5.2 %collective-permute-done.5.refs_0_ = bf16[112,384]{1,0:T(8,128)(2,1)S(1)} collective-permute-done((bf16[112,384]{1,0:T(8,128)(2,1)S(1)}, bf16[112,384]{1,0:T(8,128)(2,1)S(1)}, u32[]{:S(2)}, u32[]{:S(2)}) %collective-permute-start.5) | collective-permute-done | bytes 86048 | tf_op jit(solution)/shard_map/ppermute | solution.py:29
  36.6 13.0 %collective-permute-start.6 = (bf16[112,384]{1,0:T(8,128)(2,1)S(1)}, bf16[112,384]{1,0:T(8,128)(2,1)S(1)}, u32[]{:S(2)}, u32[]{:S(2)}) collective-permute-start(bf16[112,384]{1,0:T(8,128)(2,1)S(1)} %meet.5.refs_3_), channel_id=1, source_target_pairs={{0,256},{16,784},{32,288},{48,816},{64,320},{80,848},{96,352},{112... | collective-permute-start | bytes 258056 | tf_op jit(solution)/shard_map/ppermute | solution.py:29
  49.7 2.1 %collective-permute-start.2 = (bf16[384,512]{1,0:T(8,128)(2,1)S(1)}, bf16[384,512]{1,0:T(8,128)(2,1)S(1)}, u32[]{:S(2)}, u32[]{:S(2)}) collective-permute-start(bf16[384,512]{1,0:T(8,128)(2,1)S(1)} %stack.3.refs_0_), channel_id=1, source_target_pairs={{0,12},{1,13},{2,14},{3,15},{4,8},{5,9},{6,10},{7,11},{8,4},{9,5},... | collective-permute-start | bytes 1179656 | tf_op jit(solution)/shard_map/ppermute | solution.py:44
  52.4 4.8 %collective-permute-start.8 = (bf16[400,384]{1,0:T(8,128)(2,1)S(1)}, bf16[400,384]{1,0:T(8,128)(2,1)}, u32[]{:S(2)}, u32[]{:S(2)}) collective-permute-start(bf16[400,384]{1,0:T(8,128)(2,1)S(1)} %join_units.1.refs_2_), channel_id=1, source_target_pairs={{0,32},{16,1008},{32,64},{48,16},{64,96},{80,48},{96,128},{112,80}... | collective-permute-start | bytes 921608 | tf_op jit(solution)/shard_map/ppermute | solution.py:29
  57.2 1.9 %collective-permute-start.9 = (bf16[400,384]{1,0:T(8,128)(2,1)S(1)}, bf16[400,384]{1,0:T(8,128)(2,1)}, u32[]{:S(2)}, u32[]{:S(2)}) collective-permute-start(bf16[400,384]{1,0:T(8,128)(2,1)S(1)} %join_units.1.refs_2_), channel_id=1, source_target_pairs={{0,992},{16,48},{32,0},{48,80},{64,32},{80,112},{96,64},{112,144},... | collective-permute-start | bytes 921608 | tf_op jit(solution)/shard_map/ppermute | solution.py:29
  59.2 3.1 %collective-permute-start.3 = (bf16[768,512]{1,0:T(8,128)(2,1)S(1)}, bf16[768,512]{1,0:T(8,128)(2,1)S(1)}, u32[]{:S(2)}, u32[]{:S(2)}) collective-permute-start(bf16[768,512]{1,0:T(8,128)(2,1)S(1)} %stack.4.refs_0_), channel_id=1, source_target_pairs={{0,1},{1,0},{2,3},{3,2},{4,5},{5,4},{6,7},{7,6},{8,9},{9,8},{10,11... | collective-permute-start | bytes 2359304 | tf_op jit(solution)/shard_map/ppermute | solution.py:44
  62.4 3.4 %collective-permute-done.9.refs_1_ = bf16[400,384]{1,0:T(8,128)(2,1)} collective-permute-done((bf16[400,384]{1,0:T(8,128)(2,1)S(1)}, bf16[400,384]{1,0:T(8,128)(2,1)}, u32[]{:S(2)}, u32[]{:S(2)}) %collective-permute-start.9) | collective-permute-done | bytes 307232 | tf_op jit(solution)/shard_map/ppermute | solution.py:29
  65.8 3.4 %collective-permute-start.10 = (bf16[400,384]{1,0:T(8,128)(2,1)}, bf16[400,384]{1,0:T(8,128)(2,1)}, u32[]{:S(2)}, u32[]{:S(2)}) collective-permute-start(bf16[400,384]{1,0:T(8,128)(2,1)} %get-tuple-element.24.refs_3_), channel_id=1, source_target_pairs={{0,32},{16,1008},{32,64},{48,16},{64,96},{80,48},{96,128},{112,80}... | collective-permute-start | bytes 921608 | tf_op jit(solution)/shard_map/ppermute | solution.py:29
  69.1 3.1 %collective-permute-start.11 = (bf16[400,384]{1,0:T(8,128)(2,1)}, bf16[400,384]{1,0:T(8,128)(2,1)}, u32[]{:S(2)}, u32[]{:S(2)}) collective-permute-start(bf16[400,384]{1,0:T(8,128)(2,1)} %get-tuple-element.25.refs_4_), channel_id=1, source_target_pairs={{0,992},{16,48},{32,0},{48,80},{64,32},{80,112},{96,64},{112,144},... | collective-permute-start | bytes 921608 | tf_op jit(solution)/shard_map/ppermute | solution.py:29
  72.5 4.4 %collective-permute-start.4 = (bf16[1536,512]{1,0:T(8,128)(2,1)S(1)}, bf16[1536,512]{1,0:T(8,128)(2,1)S(1)}, u32[]{:S(2)}, u32[]{:S(2)}) collective-permute-start(bf16[1536,512]{1,0:T(8,128)(2,1)S(1)} %stack.5.refs_0_), channel_id=1, source_target_pairs={{0,3},{1,2},{2,1},{3,0},{4,7},{5,6},{6,5},{7,4},{8,11},{9,10},{10,... | collective-permute-start | bytes 4718600 | tf_op jit(solution)/shard_map/ppermute | solution.py:44
  77.3 3.6 %collective-permute-start.12 = (bf16[400,384]{1,0:T(8,128)(2,1)}, bf16[400,384]{1,0:T(8,128)(2,1)}, u32[]{:S(2)}, u32[]{:S(2)}) collective-permute-start(bf16[400,384]{1,0:T(8,128)(2,1)} %get-tuple-element.26.refs_5_), channel_id=1, source_target_pairs={{0,32},{16,1008},{32,64},{48,16},{64,96},{80,48},{96,128},{112,80}... | collective-permute-start | bytes 921608 | tf_op jit(solution)/shard_map/ppermute | solution.py:29
  80.9 3.2 %collective-permute-start.13 = (bf16[400,384]{1,0:T(8,128)(2,1)}, bf16[400,384]{1,0:T(8,128)(2,1)}, u32[]{:S(2)}, u32[]{:S(2)}) collective-permute-start(bf16[400,384]{1,0:T(8,128)(2,1)} %get-tuple-element.27.refs_6_), channel_id=1, source_target_pairs={{0,992},{16,48},{32,0},{48,80},{64,32},{80,112},{96,64},{112,144},... | collective-permute-start | bytes 921608 | tf_op jit(solution)/shard_map/ppermute | solution.py:29
  84.2 2.5 %collective-permute-done.12.p_ref.refs_7_ = bf16[400,384]{1,0:T(8,128)(2,1)} collective-permute-done((bf16[400,384]{1,0:T(8,128)(2,1)}, bf16[400,384]{1,0:T(8,128)(2,1)}, u32[]{:S(2)}, u32[]{:S(2)}) %collective-permute-start.12) | collective-permute-done | bytes 307232 | tf_op jit(solution)/shard_map/ppermute | solution.py:29
  86.7 5.0 %collective-permute-done.13.q_ref.refs_8_ = bf16[400,384]{1,0:T(8,128)(2,1)} collective-permute-done((bf16[400,384]{1,0:T(8,128)(2,1)}, bf16[400,384]{1,0:T(8,128)(2,1)}, u32[]{:S(2)}, u32[]{:S(2)}) %collective-permute-start.13) | collective-permute-done | bytes 307232 | tf_op jit(solution)/shard_map/ppermute | solution.py:29
  92.7 1.9 %collective-permute-start.14 = (bf16[208,384]{1,0:T(8,128)(2,1)S(1)}, bf16[208,384]{1,0:T(8,128)(2,1)S(1)}, u32[]{:S(2)}, u32[]{:S(2)}) collective-permute-start(bf16[208,384]{1,0:T(8,128)(2,1)S(1)} %get-tuple-element.28), channel_id=1, source_target_pairs={{0,32},{16,1008},{32,64},{48,16},{64,96},{80,48},{96,128},{112,80}... | collective-permute-start | bytes 479240 | tf_op jit(solution)/shard_map/ppermute | solution.py:29
  94.7 4.6 %collective-permute-start.15 = (bf16[208,384]{1,0:T(8,128)(2,1)S(1)}, bf16[208,384]{1,0:T(8,128)(2,1)S(1)}, u32[]{:S(2)}, u32[]{:S(2)}) collective-permute-start(bf16[208,384]{1,0:T(8,128)(2,1)S(1)} %get-tuple-element.29), channel_id=1, source_target_pairs={{0,992},{16,48},{32,0},{48,80},{64,32},{80,112},{96,64},{112,144},... | collective-permute-start | bytes 479240 | tf_op jit(solution)/shard_map/ppermute | solution.py:29
  99.3 4.3 %project_first.1 = (f32[512,384]{1,0:T(8,128)S(1)}, f32[16,384]{1,0:T(8,128)S(1)}) custom-call(s32[32]{0:T(128)S(1)} %fusion.8.starts, s32[32]{0:T(128)S(1)} %get-tuple-element.40.outers, bf16[1536,512]{1,0:T(8,128)(2,1)S(1)} %stack.5.refs_0_, bf16[1536,512]{1,0:T(8,128)(2,1)S(1)} %collective-permute-done.4.refs_1_, bf16[400,384]{1,0:T(8,128)(2,1)S(1)} %join_units.1.refs_2_, ...), custom_call_target="tpu_custom_call" | custom-call | flops 1056964608 | bytes 6291456 | tf_op jit(solution)/shard_map/project_first/pallas_call | solution.py:249
  103.7 1.2 project_last.1
  104.8 13.6 %collective-permute-start.16 = (f32[264,384]{1,0:T(8,128)S(1)}, f32[264,384]{1,0:T(8,128)S(1)}, u32[]{:S(2)}, u32[]{:S(2)}) collective-permute-start(f32[264,384]{1,0:T(8,128)S(1)} %get-tuple-element.33), channel_id=1, source_target_pairs={{0,16},{16,0},{32,48},{48,32},{64,80},{80,64},{96,112},{112,96},{1... | collective-permute-start | bytes 1216520 | tf_op jit(solution)/shard_map/ppermute | solution.py:33
  119.8 2.2 %attention.1 = (bf16[256,384]{1,0:T(8,128)(2,1)}, bf16[256,384]{1,0:T(8,128)(2,1)}, bf16[256,384]{1,0:T(8,128)(2,1)}, f32[1,32]{1,0:T(1,128)}) custom-call(s32[1]{0:T(128)S(6)} %copy.38.group, f32[264,384]{1,0:T(8,128)S(1)} %get-tuple-element.32.mine_ref, f32[264,384]{1,0:T(8,128)S(1)} %collective-permute-done.16.got_ref, ...), custom_call_target="tpu_custom_call" | custom-call | flops 201326592 | bytes 3145728 | tf_op jit(solution)/shard_map/attention/pallas_call | solution.py:249
  (46 shorter events, 5.8 us)
Async XLA Ops:
  1.7 26.7 %collective-permute-start = (bf16[2,96,256]{2,1,0:T(8,128)(2,1)S(1)}, bf16[2,96,256]{2,1,0:T(8,128)(2,1)S(1)}, u32[]{:S(2)}, u32[]{:S(2)}) collective-permute-start(bf16[2,96,256]{2,1,0:T(8,128)(2,1)S(1)} %fusion), channel_id=1, source_target_pairs={{0,16},{16,0},{32,48},{48,32},{64,80},{80,64},{96,112},{112,96},{1... | collective-permute-start | bytes 294920 | tf_op jit(solution)/shard_map/ppermute | solution.py:33
  5.6 0.9 copy-start.3
  6.5 30.1 %collective-permute-start.5 = (bf16[112,384]{1,0:T(8,128)(2,1)S(1)}, bf16[112,384]{1,0:T(8,128)(2,1)S(1)}, u32[]{:S(2)}, u32[]{:S(2)}) collective-permute-start(bf16[112,384]{1,0:T(8,128)(2,1)S(1)} %make_unit.1.refs_0_), channel_id=1, source_target_pairs={{0,256},{16,784},{32,288},{48,816},{64,320},{80,848},{96,352},{112... | collective-permute-start | bytes 258056 | tf_op jit(solution)/shard_map/ppermute | solution.py:29
  26.6 23.1 %collective-permute-start.7 = (bf16[112,384]{1,0:T(8,128)(2,1)S(1)}, bf16[112,384]{1,0:T(8,128)(2,1)S(1)}, u32[]{:S(2)}, u32[]{:S(2)}) collective-permute-start(bf16[112,384]{1,0:T(8,128)(2,1)S(1)} %make_unit.1.refs_0_), channel_id=1, source_target_pairs={{0,768},{16,272},{32,800},{48,304},{64,832},{80,336},{96,864},{112... | collective-permute-start | bytes 258056 | tf_op jit(solution)/shard_map/ppermute | solution.py:29
  28.5 21.1 %collective-permute-start.1 = (bf16[192,512]{1,0:T(8,128)(2,1)S(1)}, bf16[192,512]{1,0:T(8,128)(2,1)S(1)}, u32[]{:S(2)}, u32[]{:S(2)}) collective-permute-start(bf16[192,512]{1,0:T(8,128)(2,1)S(1)} %bitcast.36), channel_id=1, source_target_pairs={{0,4},{1,5},{2,6},{3,7},{4,0},{5,1},{6,2},{7,3},{8,12},{9,13},{10,... | collective-permute-start | bytes 589832 | tf_op jit(solution)/shard_map/ppermute | solution.py:44
  36.6 15.8 %collective-permute-start.6 = (bf16[112,384]{1,0:T(8,128)(2,1)S(1)}, bf16[112,384]{1,0:T(8,128)(2,1)S(1)}, u32[]{:S(2)}, u32[]{:S(2)}) collective-permute-start(bf16[112,384]{1,0:T(8,128)(2,1)S(1)} %meet.5.refs_3_), channel_id=1, source_target_pairs={{0,256},{16,784},{32,288},{48,816},{64,320},{80,848},{96,352},{112... | collective-permute-start | bytes 258056 | tf_op jit(solution)/shard_map/ppermute | solution.py:29
  49.7 9.5 %collective-permute-start.2 = (bf16[384,512]{1,0:T(8,128)(2,1)S(1)}, bf16[384,512]{1,0:T(8,128)(2,1)S(1)}, u32[]{:S(2)}, u32[]{:S(2)}) collective-permute-start(bf16[384,512]{1,0:T(8,128)(2,1)S(1)} %stack.3.refs_0_), channel_id=1, source_target_pairs={{0,12},{1,13},{2,14},{3,15},{4,8},{5,9},{6,10},{7,11},{8,4},{9,5},... | collective-permute-start | bytes 1179656 | tf_op jit(solution)/shard_map/ppermute | solution.py:44
  52.4 9.9 %collective-permute-start.8 = (bf16[400,384]{1,0:T(8,128)(2,1)S(1)}, bf16[400,384]{1,0:T(8,128)(2,1)}, u32[]{:S(2)}, u32[]{:S(2)}) collective-permute-start(bf16[400,384]{1,0:T(8,128)(2,1)S(1)} %join_units.1.refs_2_), channel_id=1, source_target_pairs={{0,32},{16,1008},{32,64},{48,16},{64,96},{80,48},{96,128},{112,80}... | collective-permute-start | bytes 921608 | tf_op jit(solution)/shard_map/ppermute | solution.py:29
  57.2 8.5 %collective-permute-start.9 = (bf16[400,384]{1,0:T(8,128)(2,1)S(1)}, bf16[400,384]{1,0:T(8,128)(2,1)}, u32[]{:S(2)}, u32[]{:S(2)}) collective-permute-start(bf16[400,384]{1,0:T(8,128)(2,1)S(1)} %join_units.1.refs_2_), channel_id=1, source_target_pairs={{0,992},{16,48},{32,0},{48,80},{64,32},{80,112},{96,64},{112,144},... | collective-permute-start | bytes 921608 | tf_op jit(solution)/shard_map/ppermute | solution.py:29
  59.2 13.1 %collective-permute-start.3 = (bf16[768,512]{1,0:T(8,128)(2,1)S(1)}, bf16[768,512]{1,0:T(8,128)(2,1)S(1)}, u32[]{:S(2)}, u32[]{:S(2)}) collective-permute-start(bf16[768,512]{1,0:T(8,128)(2,1)S(1)} %stack.4.refs_0_), channel_id=1, source_target_pairs={{0,1},{1,0},{2,3},{3,2},{4,5},{5,4},{6,7},{7,6},{8,9},{9,8},{10,11... | collective-permute-start | bytes 2359304 | tf_op jit(solution)/shard_map/ppermute | solution.py:44
  65.8 11.1 %collective-permute-start.10 = (bf16[400,384]{1,0:T(8,128)(2,1)}, bf16[400,384]{1,0:T(8,128)(2,1)}, u32[]{:S(2)}, u32[]{:S(2)}) collective-permute-start(bf16[400,384]{1,0:T(8,128)(2,1)} %get-tuple-element.24.refs_3_), channel_id=1, source_target_pairs={{0,32},{16,1008},{32,64},{48,16},{64,96},{80,48},{96,128},{112,80}... | collective-permute-start | bytes 921608 | tf_op jit(solution)/shard_map/ppermute | solution.py:29
  69.1 8.2 %collective-permute-start.11 = (bf16[400,384]{1,0:T(8,128)(2,1)}, bf16[400,384]{1,0:T(8,128)(2,1)}, u32[]{:S(2)}, u32[]{:S(2)}) collective-permute-start(bf16[400,384]{1,0:T(8,128)(2,1)} %get-tuple-element.25.refs_4_), channel_id=1, source_target_pairs={{0,992},{16,48},{32,0},{48,80},{64,32},{80,112},{96,64},{112,144},... | collective-permute-start | bytes 921608 | tf_op jit(solution)/shard_map/ppermute | solution.py:29
  72.5 11.6 %copy-start.5 = (s32[32]{0:T(128)S(1)}, s32[32]{0:T(128)}, u32[]{:S(2)}) copy-start(s32[32]{0:T(128)} %constant.113.clone) | copy-start | bytes 388
  72.5 11.6 %copy-start.6 = (s32[32]{0:T(128)S(1)}, s32[32]{0:T(128)}, u32[]{:S(2)}) copy-start(s32[32]{0:T(128)} %constant.117) | copy-start | bytes 388
  72.5 26.8 %collective-permute-start.4 = (bf16[1536,512]{1,0:T(8,128)(2,1)S(1)}, bf16[1536,512]{1,0:T(8,128)(2,1)S(1)}, u32[]{:S(2)}, u32[]{:S(2)}) collective-permute-start(bf16[1536,512]{1,0:T(8,128)(2,1)S(1)} %stack.5.refs_0_), channel_id=1, source_target_pairs={{0,3},{1,2},{2,1},{3,0},{4,7},{5,6},{6,5},{7,4},{8,11},{9,10},{10,... | collective-permute-start | bytes 4718600 | tf_op jit(solution)/shard_map/ppermute | solution.py:44
  77.3 9.4 %collective-permute-start.12 = (bf16[400,384]{1,0:T(8,128)(2,1)}, bf16[400,384]{1,0:T(8,128)(2,1)}, u32[]{:S(2)}, u32[]{:S(2)}) collective-permute-start(bf16[400,384]{1,0:T(8,128)(2,1)} %get-tuple-element.26.refs_5_), channel_id=1, source_target_pairs={{0,32},{16,1008},{32,64},{48,16},{64,96},{80,48},{96,128},{112,80}... | collective-permute-start | bytes 921608 | tf_op jit(solution)/shard_map/ppermute | solution.py:29
  80.9 10.8 %collective-permute-start.13 = (bf16[400,384]{1,0:T(8,128)(2,1)}, bf16[400,384]{1,0:T(8,128)(2,1)}, u32[]{:S(2)}, u32[]{:S(2)}) collective-permute-start(bf16[400,384]{1,0:T(8,128)(2,1)} %get-tuple-element.27.refs_6_), channel_id=1, source_target_pairs={{0,992},{16,48},{32,0},{48,80},{64,32},{80,112},{96,64},{112,144},... | collective-permute-start | bytes 921608 | tf_op jit(solution)/shard_map/ppermute | solution.py:29
  92.7 10.9 %collective-permute-start.14 = (bf16[208,384]{1,0:T(8,128)(2,1)S(1)}, bf16[208,384]{1,0:T(8,128)(2,1)S(1)}, u32[]{:S(2)}, u32[]{:S(2)}) collective-permute-start(bf16[208,384]{1,0:T(8,128)(2,1)S(1)} %get-tuple-element.28), channel_id=1, source_target_pairs={{0,32},{16,1008},{32,64},{48,16},{64,96},{80,48},{96,128},{112,80}... | collective-permute-start | bytes 479240 | tf_op jit(solution)/shard_map/ppermute | solution.py:29
  94.7 9.0 %collective-permute-start.15 = (bf16[208,384]{1,0:T(8,128)(2,1)S(1)}, bf16[208,384]{1,0:T(8,128)(2,1)S(1)}, u32[]{:S(2)}, u32[]{:S(2)}) collective-permute-start(bf16[208,384]{1,0:T(8,128)(2,1)S(1)} %get-tuple-element.29), channel_id=1, source_target_pairs={{0,992},{16,48},{32,0},{48,80},{64,32},{80,112},{96,64},{112,144},... | collective-permute-start | bytes 479240 | tf_op jit(solution)/shard_map/ppermute | solution.py:29
  103.6 14.8 %copy-start = (bf16[256,384]{1,0:T(8,128)(2,1)S(1)}, bf16[256,384]{1,0:T(8,128)(2,1)}, u32[]{:S(2)}) copy-start(bf16[256,384]{1,0:T(8,128)(2,1)} %q_ref.3) | copy-start | bytes 589828
  103.6 14.8 %copy-start.1 = (bf16[256,384]{1,0:T(8,128)(2,1)S(1)}, bf16[256,384]{1,0:T(8,128)(2,1)}, u32[]{:S(2)}) copy-start(bf16[256,384]{1,0:T(8,128)(2,1)} %k_ref.3) | copy-start | bytes 589828
  103.6 14.8 %copy-start.4 = (f32[32]{0:T(128)S(1)}, f32[32]{0:T(128)}, u32[]{:S(2)}) copy-start(f32[32]{0:T(128)} %param.16) | copy-start | bytes 388
  103.7 16.1 %copy-start.2 = (bf16[256,384]{1,0:T(8,128)(2,1)S(1)}, bf16[256,384]{1,0:T(8,128)(2,1)}, u32[]{:S(2)}) copy-start(bf16[256,384]{1,0:T(8,128)(2,1)} %v_ref.1) | copy-start | bytes 589828
  104.8 14.9 %collective-permute-start.16 = (f32[264,384]{1,0:T(8,128)S(1)}, f32[264,384]{1,0:T(8,128)S(1)}, u32[]{:S(2)}, u32[]{:S(2)}) collective-permute-start(f32[264,384]{1,0:T(8,128)S(1)} %get-tuple-element.33), channel_id=1, source_target_pairs={{0,16},{16,0},{32,48},{48,32},{64,80},{80,64},{96,112},{112,96},{1... | collective-permute-start | bytes 1216520 | tf_op jit(solution)/shard_map/ppermute | solution.py:33

commit v9 on v8

--- a/solution.py
+++ b/solution.py
@@ -88,14 +88,14 @@
 def unit_kernel(group, loss, weight_ref, unit_ref):
     heads = weight_ref.shape[1]
     unit_ref[pl.ds(0, UNIT), :] = weight_ref[...]
-    x = jnp.full((TAIL, heads), loss[0], jnp.float32)
+    x = jnp.broadcast_to(loss[...], (TAIL, heads))
     high = x.astype(jnp.bfloat16).astype(jnp.float32)
     middle = (x - high).astype(jnp.bfloat16).astype(jnp.float32)
     low = x - high - middle
     row = lax.broadcasted_iota(jnp.int32, x.shape, 0)
     lane = lax.broadcasted_iota(jnp.int32, x.shape, 1)
     value = jnp.where(row == 0, 1.0, jnp.where(row == 1, high, jnp.where(row == 2, middle, low)))
-    value = jnp.where((row < STATS) & (lane == group[0]), value, 0.0)
+    value = jnp.where((row < STATS) & (lane == group[...]), value, 0.0)
     unit_ref[pl.ds(UNIT, TAIL), :] = value.astype(jnp.bfloat16)
 
 
@@ -219,7 +219,7 @@
     nw_ref[...] = new_weights
     label = lax.broadcasted_iota(jnp.int32, (1, width), 1)
     scale = jnp.sum(
-        jnp.where(label == group[0], new_weights / floored, 0.0), axis=1, keepdims=True
+        jnp.where(label == group[...], new_weights / floored, 0.0), axis=1, keepdims=True
     )
     product = mine_ref[pl.ds(0, PATCHES), :] + got_ref[pl.ds(0, PATCHES), :]
     head_grad = (product * scale).astype(bf16)
@@ -311,12 +311,13 @@
     mp = lax.axis_index("mp")
     at_x, at_y = mp // SIDE, mp % SIDE
 
+    group = group_ids.reshape(1, 1)
+
     unit = call(
         unit_kernel,
         "make_unit",
         jax.ShapeDtypeStruct((UNIT + TAIL, heads), bf16),
-        (group_ids, image_loss, out_weight.T),
-        2,
+        (group, image_loss.reshape(1, 1), out_weight.T),
         moved=2**17,
     )
 
@@ -378,8 +379,7 @@
         attention_kernel,
         "attention",
         (out, out, out, group_row),
-        (group_ids, mine, received, old_weights, probs, queries, keys, values),
-        1,
+        (group, mine, received, old_weights, probs, queries, keys, values),
         flops=8 * PATCHES * PATCHES * heads,
         moved=3 * 2**20,
     )

time: 123 us -> 123 us (level)
  no operation moved by 1% of the time
where the time goes in v9:
time: 123 us; the launch traced here: 122 us
  starting transfers between devices  90 us (73%)
  waiting for transfers between devices  18.2 us (15%)
  Pallas kernels  9.33 us (8%)
  between operations  2.38 us (2%)
  local copies, waits for them, and re-layouts  1.98 us (2%)
    ppermute x11, starting transfers between devices, along_z(): return lax.ppermute(x, 'dp', pairs)  61.4 us
    ppermute x11, waiting for transfers between devices, along_z(): return lax.ppermute(x, 'dp', pairs)  17.1 us
    ppermute x2, starting transfers between devices, to_sibling(): return lax.ppermute(x, 'dp', [(i, i ^ 1) for i in range(2 * pairs_z)])  16.2 us
    ppermute x4, starting transfers between devices, exchange(): return lax.ppermute(x, ALL, pairs)  12.5 us
    pallas_call x9, Pallas kernels, call(): pl.pallas_call(kernel, out_shape=out_shape, in_specs=[SM] * scalars + [VM...  8.32 us
  transfers between devices with their start and end apart: 17, of which 8 were waited for; matrix products, arithmetic and copies ran while one was open for 0% of the time, Pallas kernels for 5%

profile of v9, /device:TPU:113, one launch (start us, length us, event | category | flops | bytes accessed | tf_op | source)
XLA Modules:
  0.0 122.0 jit_solution(10798952639217413350)
XLA Ops:
  1.7 2.6 %collective-permute-start = (bf16[2,96,256]{2,1,0:T(8,128)(2,1)S(1)}, bf16[2,96,256]{2,1,0:T(8,128)(2,1)S(1)}, u32[]{:S(2)}, u32[]{:S(2)}) collective-permute-start(bf16[2,96,256]{2,1,0:T(8,128)(2,1)S(1)} %fusion), channel_id=1, source_target_pairs={{0,16},{16,0},{32,48},{48,32},{64,80},{80,64},{96,112},{112,96},{1... | collective-permute-start | bytes 294920 | tf_op jit(solution)/shard_map/ppermute | solution.py:33
  6.6 20.0 %collective-permute-start.5 = (bf16[112,384]{1,0:T(8,128)(2,1)S(1)}, bf16[112,384]{1,0:T(8,128)(2,1)S(1)}, u32[]{:S(2)}, u32[]{:S(2)}) collective-permute-start(bf16[112,384]{1,0:T(8,128)(2,1)S(1)} %make_unit.1.refs_0_), channel_id=1, source_target_pairs={{0,256},{16,784},{32,288},{48,816},{64,320},{80,848},{96,352},{112... | collective-permute-start | bytes 258056 | tf_op jit(solution)/shard_map/ppermute | solution.py:29
  26.6 1.9 %collective-permute-start.7 = (bf16[112,384]{1,0:T(8,128)(2,1)S(1)}, bf16[112,384]{1,0:T(8,128)(2,1)S(1)}, u32[]{:S(2)}, u32[]{:S(2)}) collective-permute-start(bf16[112,384]{1,0:T(8,128)(2,1)S(1)} %make_unit.1.refs_0_), channel_id=1, source_target_pairs={{0,768},{16,272},{32,800},{48,304},{64,832},{80,336},{96,864},{112... | collective-permute-start | bytes 258056 | tf_op jit(solution)/shard_map/ppermute | solution.py:29
  28.6 2.9 %collective-permute-start.1 = (bf16[192,512]{1,0:T(8,128)(2,1)S(1)}, bf16[192,512]{1,0:T(8,128)(2,1)S(1)}, u32[]{:S(2)}, u32[]{:S(2)}) collective-permute-start(bf16[192,512]{1,0:T(8,128)(2,1)S(1)} %bitcast.41), channel_id=1, source_target_pairs={{0,4},{1,5},{2,6},{3,7},{4,0},{5,1},{6,2},{7,3},{8,12},{9,13},{10,... | collective-permute-start | bytes 589832 | tf_op jit(solution)/shard_map/ppermute | solution.py:44
  31.5 5.2 %collective-permute-done.5.refs_0_ = bf16[112,384]{1,0:T(8,128)(2,1)S(1)} collective-permute-done((bf16[112,384]{1,0:T(8,128)(2,1)S(1)}, bf16[112,384]{1,0:T(8,128)(2,1)S(1)}, u32[]{:S(2)}, u32[]{:S(2)}) %collective-permute-start.5) | collective-permute-done | bytes 86048 | tf_op jit(solution)/shard_map/ppermute | solution.py:29
  36.7 13.0 %collective-permute-start.6 = (bf16[112,384]{1,0:T(8,128)(2,1)S(1)}, bf16[112,384]{1,0:T(8,128)(2,1)S(1)}, u32[]{:S(2)}, u32[]{:S(2)}) collective-permute-start(bf16[112,384]{1,0:T(8,128)(2,1)S(1)} %meet.5.refs_3_), channel_id=1, source_target_pairs={{0,256},{16,784},{32,288},{48,816},{64,320},{80,848},{96,352},{112... | collective-permute-start | bytes 258056 | tf_op jit(solution)/shard_map/ppermute | solution.py:29
  49.7 2.1 %collective-permute-start.2 = (bf16[384,512]{1,0:T(8,128)(2,1)S(1)}, bf16[384,512]{1,0:T(8,128)(2,1)S(1)}, u32[]{:S(2)}, u32[]{:S(2)}) collective-permute-start(bf16[384,512]{1,0:T(8,128)(2,1)S(1)} %stack.3.refs_0_), channel_id=1, source_target_pairs={{0,12},{1,13},{2,14},{3,15},{4,8},{5,9},{6,10},{7,11},{8,4},{9,5},... | collective-permute-start | bytes 1179656 | tf_op jit(solution)/shard_map/ppermute | solution.py:44
  52.5 4.8 %collective-permute-start.8 = (bf16[400,384]{1,0:T(8,128)(2,1)S(1)}, bf16[400,384]{1,0:T(8,128)(2,1)}, u32[]{:S(2)}, u32[]{:S(2)}) collective-permute-start(bf16[400,384]{1,0:T(8,128)(2,1)S(1)} %join_units.1.refs_2_), channel_id=1, source_target_pairs={{0,32},{16,1008},{32,64},{48,16},{64,96},{80,48},{96,128},{112,80}... | collective-permute-start | bytes 921608 | tf_op jit(solution)/shard_map/ppermute | solution.py:29
  57.3 1.9 %collective-permute-start.9 = (bf16[400,384]{1,0:T(8,128)(2,1)S(1)}, bf16[400,384]{1,0:T(8,128)(2,1)}, u32[]{:S(2)}, u32[]{:S(2)}) collective-permute-start(bf16[400,384]{1,0:T(8,128)(2,1)S(1)} %join_units.1.refs_2_), channel_id=1, source_target_pairs={{0,992},{16,48},{32,0},{48,80},{64,32},{80,112},{96,64},{112,144},... | collective-permute-start | bytes 921608 | tf_op jit(solution)/shard_map/ppermute | solution.py:29
  59.3 3.1 %collective-permute-start.3 = (bf16[768,512]{1,0:T(8,128)(2,1)S(1)}, bf16[768,512]{1,0:T(8,128)(2,1)S(1)}, u32[]{:S(2)}, u32[]{:S(2)}) collective-permute-start(bf16[768,512]{1,0:T(8,128)(2,1)S(1)} %stack.4.refs_0_), channel_id=1, source_target_pairs={{0,1},{1,0},{2,3},{3,2},{4,5},{5,4},{6,7},{7,6},{8,9},{9,8},{10,11... | collective-permute-start | bytes 2359304 | tf_op jit(solution)/shard_map/ppermute | solution.py:44
  62.4 3.4 %collective-permute-done.9.refs_1_ = bf16[400,384]{1,0:T(8,128)(2,1)} collective-permute-done((bf16[400,384]{1,0:T(8,128)(2,1)S(1)}, bf16[400,384]{1,0:T(8,128)(2,1)}, u32[]{:S(2)}, u32[]{:S(2)}) %collective-permute-start.9) | collective-permute-done | bytes 307232 | tf_op jit(solution)/shard_map/ppermute | solution.py:29
  65.8 3.4 %collective-permute-start.10 = (bf16[400,384]{1,0:T(8,128)(2,1)}, bf16[400,384]{1,0:T(8,128)(2,1)}, u32[]{:S(2)}, u32[]{:S(2)}) collective-permute-start(bf16[400,384]{1,0:T(8,128)(2,1)} %get-tuple-element.24.refs_3_), channel_id=1, source_target_pairs={{0,32},{16,1008},{32,64},{48,16},{64,96},{80,48},{96,128},{112,80}... | collective-permute-start | bytes 921608 | tf_op jit(solution)/shard_map/ppermute | solution.py:29
  69.2 3.1 %collective-permute-start.11 = (bf16[400,384]{1,0:T(8,128)(2,1)}, bf16[400,384]{1,0:T(8,128)(2,1)}, u32[]{:S(2)}, u32[]{:S(2)}) collective-permute-start(bf16[400,384]{1,0:T(8,128)(2,1)} %get-tuple-element.25.refs_4_), channel_id=1, source_target_pairs={{0,992},{16,48},{32,0},{48,80},{64,32},{80,112},{96,64},{112,144},... | collective-permute-start | bytes 921608 | tf_op jit(solution)/shard_map/ppermute | solution.py:29
  72.6 4.4 %collective-permute-start.4 = (bf16[1536,512]{1,0:T(8,128)(2,1)S(1)}, bf16[1536,512]{1,0:T(8,128)(2,1)S(1)}, u32[]{:S(2)}, u32[]{:S(2)}) collective-permute-start(bf16[1536,512]{1,0:T(8,128)(2,1)S(1)} %stack.5.refs_0_), channel_id=1, source_target_pairs={{0,3},{1,2},{2,1},{3,0},{4,7},{5,6},{6,5},{7,4},{8,11},{9,10},{10,... | collective-permute-start | bytes 4718600 | tf_op jit(solution)/shard_map/ppermute | solution.py:44
  77.4 3.6 %collective-permute-start.12 = (bf16[400,384]{1,0:T(8,128)(2,1)}, bf16[400,384]{1,0:T(8,128)(2,1)}, u32[]{:S(2)}, u32[]{:S(2)}) collective-permute-start(bf16[400,384]{1,0:T(8,128)(2,1)} %get-tuple-element.26.refs_5_), channel_id=1, source_target_pairs={{0,32},{16,1008},{32,64},{48,16},{64,96},{80,48},{96,128},{112,80}... | collective-permute-start | bytes 921608 | tf_op jit(solution)/shard_map/ppermute | solution.py:29
  81.0 3.2 %collective-permute-start.13 = (bf16[400,384]{1,0:T(8,128)(2,1)}, bf16[400,384]{1,0:T(8,128)(2,1)}, u32[]{:S(2)}, u32[]{:S(2)}) collective-permute-start(bf16[400,384]{1,0:T(8,128)(2,1)} %get-tuple-element.27.refs_6_), channel_id=1, source_target_pairs={{0,992},{16,48},{32,0},{48,80},{64,32},{80,112},{96,64},{112,144},... | collective-permute-start | bytes 921608 | tf_op jit(solution)/shard_map/ppermute | solution.py:29
  84.3 2.5 %collective-permute-done.12.p_ref.refs_7_ = bf16[400,384]{1,0:T(8,128)(2,1)} collective-permute-done((bf16[400,384]{1,0:T(8,128)(2,1)}, bf16[400,384]{1,0:T(8,128)(2,1)}, u32[]{:S(2)}, u32[]{:S(2)}) %collective-permute-start.12) | collective-permute-done | bytes 307232 | tf_op jit(solution)/shard_map/ppermute | solution.py:29
  86.8 5.0 %collective-permute-done.13.q_ref.refs_8_ = bf16[400,384]{1,0:T(8,128)(2,1)} collective-permute-done((bf16[400,384]{1,0:T(8,128)(2,1)}, bf16[400,384]{1,0:T(8,128)(2,1)}, u32[]{:S(2)}, u32[]{:S(2)}) %collective-permute-start.13) | collective-permute-done | bytes 307232 | tf_op jit(solution)/shard_map/ppermute | solution.py:29
  92.8 1.9 %collective-permute-start.14 = (bf16[208,384]{1,0:T(8,128)(2,1)S(1)}, bf16[208,384]{1,0:T(8,128)(2,1)S(1)}, u32[]{:S(2)}, u32[]{:S(2)}) collective-permute-start(bf16[208,384]{1,0:T(8,128)(2,1)S(1)} %get-tuple-element.28), channel_id=1, source_target_pairs={{0,32},{16,1008},{32,64},{48,16},{64,96},{80,48},{96,128},{112,80}... | collective-permute-start | bytes 479240 | tf_op jit(solution)/shard_map/ppermute | solution.py:29
  94.7 4.6 %collective-permute-start.15 = (bf16[208,384]{1,0:T(8,128)(2,1)S(1)}, bf16[208,384]{1,0:T(8,128)(2,1)S(1)}, u32[]{:S(2)}, u32[]{:S(2)}) collective-permute-start(bf16[208,384]{1,0:T(8,128)(2,1)S(1)} %get-tuple-element.29), channel_id=1, source_target_pairs={{0,992},{16,48},{32,0},{48,80},{64,32},{80,112},{96,64},{112,144},... | collective-permute-start | bytes 479240 | tf_op jit(solution)/shard_map/ppermute | solution.py:29
  99.3 4.3 %project_first.1 = (f32[512,384]{1,0:T(8,128)S(1)}, f32[16,384]{1,0:T(8,128)S(1)}) custom-call(s32[32]{0:T(128)S(1)} %fusion.8.starts, s32[32]{0:T(128)S(1)} %get-tuple-element.40.outers, bf16[1536,512]{1,0:T(8,128)(2,1)S(1)} %stack.5.refs_0_, bf16[1536,512]{1,0:T(8,128)(2,1)S(1)} %collective-permute-done.4.refs_1_, bf16[400,384]{1,0:T(8,128)(2,1)S(1)} %join_units.1.refs_2_, ...), custom_call_target="tpu_custom_call" | custom-call | flops 1056964608 | bytes 6291456 | tf_op jit(solution)/shard_map/project_first/pallas_call | solution.py:249
  103.7 1.2 project_last.1
  104.9 13.6 %collective-permute-start.16 = (f32[264,384]{1,0:T(8,128)S(1)}, f32[264,384]{1,0:T(8,128)S(1)}, u32[]{:S(2)}, u32[]{:S(2)}) collective-permute-start(f32[264,384]{1,0:T(8,128)S(1)} %get-tuple-element.33), channel_id=1, source_target_pairs={{0,16},{16,0},{32,48},{48,32},{64,80},{80,64},{96,112},{112,96},{1... | collective-permute-start | bytes 1216520 | tf_op jit(solution)/shard_map/ppermute | solution.py:33
  119.8 2.2 %attention.1 = (bf16[256,384]{1,0:T(8,128)(2,1)}, bf16[256,384]{1,0:T(8,128)(2,1)}, bf16[256,384]{1,0:T(8,128)(2,1)}, f32[1,32]{1,0:T(1,128)}) custom-call(s32[1,1]{1,0:T(1,128)} %bitcast.40.group, f32[264,384]{1,0:T(8,128)S(1)} %get-tuple-element.32.mine_ref, f32[264,384]{1,0:T(8,128)S(1)} %collective-permute-done.16.got_ref, ...), custom_call_target="tpu_custom_call" | custom-call | flops 201326592 | bytes 3145728 | tf_op jit(solution)/shard_map/attention/pallas_call | solution.py:249
  (46 shorter events, 5.9 us)
Async XLA Ops:
  1.7 26.8 %collective-permute-start = (bf16[2,96,256]{2,1,0:T(8,128)(2,1)S(1)}, bf16[2,96,256]{2,1,0:T(8,128)(2,1)S(1)}, u32[]{:S(2)}, u32[]{:S(2)}) collective-permute-start(bf16[2,96,256]{2,1,0:T(8,128)(2,1)S(1)} %fusion), channel_id=1, source_target_pairs={{0,16},{16,0},{32,48},{48,32},{64,80},{80,64},{96,112},{112,96},{1... | collective-permute-start | bytes 294920 | tf_op jit(solution)/shard_map/ppermute | solution.py:33
  5.6 0.9 copy-start.3
  6.6 30.1 %collective-permute-start.5 = (bf16[112,384]{1,0:T(8,128)(2,1)S(1)}, bf16[112,384]{1,0:T(8,128)(2,1)S(1)}, u32[]{:S(2)}, u32[]{:S(2)}) collective-permute-start(bf16[112,384]{1,0:T(8,128)(2,1)S(1)} %make_unit.1.refs_0_), channel_id=1, source_target_pairs={{0,256},{16,784},{32,288},{48,816},{64,320},{80,848},{96,352},{112... | collective-permute-start | bytes 258056 | tf_op jit(solution)/shard_map/ppermute | solution.py:29
  26.6 23.1 %collective-permute-start.7 = (bf16[112,384]{1,0:T(8,128)(2,1)S(1)}, bf16[112,384]{1,0:T(8,128)(2,1)S(1)}, u32[]{:S(2)}, u32[]{:S(2)}) collective-permute-start(bf16[112,384]{1,0:T(8,128)(2,1)S(1)} %make_unit.1.refs_0_), channel_id=1, source_target_pairs={{0,768},{16,272},{32,800},{48,304},{64,832},{80,336},{96,864},{112... | collective-permute-start | bytes 258056 | tf_op jit(solution)/shard_map/ppermute | solution.py:29
  28.6 21.1 %collective-permute-start.1 = (bf16[192,512]{1,0:T(8,128)(2,1)S(1)}, bf16[192,512]{1,0:T(8,128)(2,1)S(1)}, u32[]{:S(2)}, u32[]{:S(2)}) collective-permute-start(bf16[192,512]{1,0:T(8,128)(2,1)S(1)} %bitcast.41), channel_id=1, source_target_pairs={{0,4},{1,5},{2,6},{3,7},{4,0},{5,1},{6,2},{7,3},{8,12},{9,13},{10,... | collective-permute-start | bytes 589832 | tf_op jit(solution)/shard_map/ppermute | solution.py:44
  36.7 15.8 %collective-permute-start.6 = (bf16[112,384]{1,0:T(8,128)(2,1)S(1)}, bf16[112,384]{1,0:T(8,128)(2,1)S(1)}, u32[]{:S(2)}, u32[]{:S(2)}) collective-permute-start(bf16[112,384]{1,0:T(8,128)(2,1)S(1)} %meet.5.refs_3_), channel_id=1, source_target_pairs={{0,256},{16,784},{32,288},{48,816},{64,320},{80,848},{96,352},{112... | collective-permute-start | bytes 258056 | tf_op jit(solution)/shard_map/ppermute | solution.py:29
  49.7 9.5 %collective-permute-start.2 = (bf16[384,512]{1,0:T(8,128)(2,1)S(1)}, bf16[384,512]{1,0:T(8,128)(2,1)S(1)}, u32[]{:S(2)}, u32[]{:S(2)}) collective-permute-start(bf16[384,512]{1,0:T(8,128)(2,1)S(1)} %stack.3.refs_0_), channel_id=1, source_target_pairs={{0,12},{1,13},{2,14},{3,15},{4,8},{5,9},{6,10},{7,11},{8,4},{9,5},... | collective-permute-start | bytes 1179656 | tf_op jit(solution)/shard_map/ppermute | solution.py:44
  52.5 9.9 %collective-permute-start.8 = (bf16[400,384]{1,0:T(8,128)(2,1)S(1)}, bf16[400,384]{1,0:T(8,128)(2,1)}, u32[]{:S(2)}, u32[]{:S(2)}) collective-permute-start(bf16[400,384]{1,0:T(8,128)(2,1)S(1)} %join_units.1.refs_2_), channel_id=1, source_target_pairs={{0,32},{16,1008},{32,64},{48,16},{64,96},{80,48},{96,128},{112,80}... | collective-permute-start | bytes 921608 | tf_op jit(solution)/shard_map/ppermute | solution.py:29
  57.3 8.5 %collective-permute-start.9 = (bf16[400,384]{1,0:T(8,128)(2,1)S(1)}, bf16[400,384]{1,0:T(8,128)(2,1)}, u32[]{:S(2)}, u32[]{:S(2)}) collective-permute-start(bf16[400,384]{1,0:T(8,128)(2,1)S(1)} %join_units.1.refs_2_), channel_id=1, source_target_pairs={{0,992},{16,48},{32,0},{48,80},{64,32},{80,112},{96,64},{112,144},... | collective-permute-start | bytes 921608 | tf_op jit(solution)/shard_map/ppermute | solution.py:29
  59.3 13.1 %collective-permute-start.3 = (bf16[768,512]{1,0:T(8,128)(2,1)S(1)}, bf16[768,512]{1,0:T(8,128)(2,1)S(1)}, u32[]{:S(2)}, u32[]{:S(2)}) collective-permute-start(bf16[768,512]{1,0:T(8,128)(2,1)S(1)} %stack.4.refs_0_), channel_id=1, source_target_pairs={{0,1},{1,0},{2,3},{3,2},{4,5},{5,4},{6,7},{7,6},{8,9},{9,8},{10,11... | collective-permute-start | bytes 2359304 | tf_op jit(solution)/shard_map/ppermute | solution.py:44
  65.8 11.1 %collective-permute-start.10 = (bf16[400,384]{1,0:T(8,128)(2,1)}, bf16[400,384]{1,0:T(8,128)(2,1)}, u32[]{:S(2)}, u32[]{:S(2)}) collective-permute-start(bf16[400,384]{1,0:T(8,128)(2,1)} %get-tuple-element.24.refs_3_), channel_id=1, source_target_pairs={{0,32},{16,1008},{32,64},{48,16},{64,96},{80,48},{96,128},{112,80}... | collective-permute-start | bytes 921608 | tf_op jit(solution)/shard_map/ppermute | solution.py:29
  69.2 8.2 %collective-permute-start.11 = (bf16[400,384]{1,0:T(8,128)(2,1)}, bf16[400,384]{1,0:T(8,128)(2,1)}, u32[]{:S(2)}, u32[]{:S(2)}) collective-permute-start(bf16[400,384]{1,0:T(8,128)(2,1)} %get-tuple-element.25.refs_4_), channel_id=1, source_target_pairs={{0,992},{16,48},{32,0},{48,80},{64,32},{80,112},{96,64},{112,144},... | collective-permute-start | bytes 921608 | tf_op jit(solution)/shard_map/ppermute | solution.py:29
  72.5 11.6 %copy-start.5 = (s32[32]{0:T(128)S(1)}, s32[32]{0:T(128)}, u32[]{:S(2)}) copy-start(s32[32]{0:T(128)} %constant.113.clone) | copy-start | bytes 388
  72.5 11.6 %copy-start.6 = (s32[32]{0:T(128)S(1)}, s32[32]{0:T(128)}, u32[]{:S(2)}) copy-start(s32[32]{0:T(128)} %constant.117) | copy-start | bytes 388
  72.6 26.8 %collective-permute-start.4 = (bf16[1536,512]{1,0:T(8,128)(2,1)S(1)}, bf16[1536,512]{1,0:T(8,128)(2,1)S(1)}, u32[]{:S(2)}, u32[]{:S(2)}) collective-permute-start(bf16[1536,512]{1,0:T(8,128)(2,1)S(1)} %stack.5.refs_0_), channel_id=1, source_target_pairs={{0,3},{1,2},{2,1},{3,0},{4,7},{5,6},{6,5},{7,4},{8,11},{9,10},{10,... | collective-permute-start | bytes 4718600 | tf_op jit(solution)/shard_map/ppermute | solution.py:44
  77.4 9.4 %collective-permute-start.12 = (bf16[400,384]{1,0:T(8,128)(2,1)}, bf16[400,384]{1,0:T(8,128)(2,1)}, u32[]{:S(2)}, u32[]{:S(2)}) collective-permute-start(bf16[400,384]{1,0:T(8,128)(2,1)} %get-tuple-element.26.refs_5_), channel_id=1, source_target_pairs={{0,32},{16,1008},{32,64},{48,16},{64,96},{80,48},{96,128},{112,80}... | collective-permute-start | bytes 921608 | tf_op jit(solution)/shard_map/ppermute | solution.py:29
  81.0 10.8 %collective-permute-start.13 = (bf16[400,384]{1,0:T(8,128)(2,1)}, bf16[400,384]{1,0:T(8,128)(2,1)}, u32[]{:S(2)}, u32[]{:S(2)}) collective-permute-start(bf16[400,384]{1,0:T(8,128)(2,1)} %get-tuple-element.27.refs_6_), channel_id=1, source_target_pairs={{0,992},{16,48},{32,0},{48,80},{64,32},{80,112},{96,64},{112,144},... | collective-permute-start | bytes 921608 | tf_op jit(solution)/shard_map/ppermute | solution.py:29
  92.8 10.9 %collective-permute-start.14 = (bf16[208,384]{1,0:T(8,128)(2,1)S(1)}, bf16[208,384]{1,0:T(8,128)(2,1)S(1)}, u32[]{:S(2)}, u32[]{:S(2)}) collective-permute-start(bf16[208,384]{1,0:T(8,128)(2,1)S(1)} %get-tuple-element.28), channel_id=1, source_target_pairs={{0,32},{16,1008},{32,64},{48,16},{64,96},{80,48},{96,128},{112,80}... | collective-permute-start | bytes 479240 | tf_op jit(solution)/shard_map/ppermute | solution.py:29
  94.7 9.0 %collective-permute-start.15 = (bf16[208,384]{1,0:T(8,128)(2,1)S(1)}, bf16[208,384]{1,0:T(8,128)(2,1)S(1)}, u32[]{:S(2)}, u32[]{:S(2)}) collective-permute-start(bf16[208,384]{1,0:T(8,128)(2,1)S(1)} %get-tuple-element.29), channel_id=1, source_target_pairs={{0,992},{16,48},{32,0},{48,80},{64,32},{80,112},{96,64},{112,144},... | collective-permute-start | bytes 479240 | tf_op jit(solution)/shard_map/ppermute | solution.py:29
  103.7 14.8 %copy-start = (bf16[256,384]{1,0:T(8,128)(2,1)S(1)}, bf16[256,384]{1,0:T(8,128)(2,1)}, u32[]{:S(2)}) copy-start(bf16[256,384]{1,0:T(8,128)(2,1)} %q_ref.3) | copy-start | bytes 589828
  103.7 14.8 %copy-start.1 = (bf16[256,384]{1,0:T(8,128)(2,1)S(1)}, bf16[256,384]{1,0:T(8,128)(2,1)}, u32[]{:S(2)}) copy-start(bf16[256,384]{1,0:T(8,128)(2,1)} %k_ref.3) | copy-start | bytes 589828
  103.7 14.8 %copy-start.4 = (f32[32]{0:T(128)S(1)}, f32[32]{0:T(128)}, u32[]{:S(2)}) copy-start(f32[32]{0:T(128)} %param.16) | copy-start | bytes 388
  103.7 16.1 %copy-start.2 = (bf16[256,384]{1,0:T(8,128)(2,1)S(1)}, bf16[256,384]{1,0:T(8,128)(2,1)}, u32[]{:S(2)}) copy-start(bf16[256,384]{1,0:T(8,128)(2,1)} %v_ref.1) | copy-start | bytes 589828
  104.9 14.9 %collective-permute-start.16 = (f32[264,384]{1,0:T(8,128)S(1)}, f32[264,384]{1,0:T(8,128)S(1)}, u32[]{:S(2)}, u32[]{:S(2)}) collective-permute-start(f32[264,384]{1,0:T(8,128)S(1)} %get-tuple-element.33), channel_id=1, source_target_pairs={{0,16},{16,0},{32,48},{48,32},{64,80},{80,64},{96,112},{112,96},{1... | collective-permute-start | bytes 1216520 | tf_op jit(solution)/shard_map/ppermute | solution.py:33
